TPU v7x, 128 devices: a whole 4x4x4 slice. The times are simulated.
128 devices in a mesh: section: 2 (over x_lo), dp: 4 (over x_hi, core), ctx: 16 (over y, z).
Axes of the slice: x: 4 (x_hi: 2, x_lo: 2; x = x_hi * 2 + x_lo), y: 4, z: 4, core: 2. Of those that a mesh axis runs over, the one named last changes fastest.
Arguments:
- inputs: bfloat16 [8, 1024, 1536], P('dp', 'ctx'), may hold values from -6 to 6
- cotangent: bfloat16 [8, 1024, 1536], P('dp', 'ctx'), may hold values from -6 to 6
- positions: int32 [8, 1024], P('dp'), may hold values from 0 to 1023, each once within a row
- granularity: int32 [8], P('dp'), may hold values from 0 to 3, as said below
- attention_gain: bfloat16 [2, 1536], P('section', ('dp', 'ctx')), may hold values from 0.25 to 1.75
- attention_in: bfloat16 [2, 1536, 4608], P('section', ('dp', 'ctx')), may hold values from -0.15625 to 0.15625
- attention_out: bfloat16 [2, 1536, 1536], P('section', ('dp', 'ctx')), may hold values from -2.5 to 2.5
- feed_gain: bfloat16 [2, 1536], P('section', ('dp', 'ctx')), may hold values from 0.25 to 1.75
- feed_up: bfloat16 [2, 1536, 6144], P('section', ('dp', 'ctx')), may hold values from -0.15625 to 0.15625
- feed_down: bfloat16 [2, 6144, 1536], P('section', ('dp', 'ctx')), may hold values from -0.15625 to 0.15625
Outputs:
- hidden: bfloat16 [2, 8, 1024, 1536], P('section', 'dp', 'ctx')
- input_grads: bfloat16 [2, 8, 1024, 1536], P('section', 'dp', 'ctx')
- grad_attention_gain: float32 [2, 1536], P('section', ('dp', 'ctx'))
- grad_attention_in: float32 [2, 1536, 4608], P('section', ('dp', 'ctx'))
- grad_attention_out: float32 [2, 1536, 1536], P('section', ('dp', 'ctx'))
- grad_feed_gain: float32 [2, 1536], P('section', ('dp', 'ctx'))
- grad_feed_up: float32 [2, 1536, 6144], P('section', ('dp', 'ctx'))
- grad_feed_down: float32 [2, 6144, 1536], P('section', ('dp', 'ctx'))
Inputs may be any that keep to these rules, and one draw needn't show every extreme that they name: Each row of positions holds every position of its sequence once. The feed-forward of a micro-batch uses 6144 // 8 * 2 ** granularity hidden units.
All inputs are finite; a program needn't handle non-finite values.
Results may differ from a plain program's by a relative error of at most 0.022.
Values may be sent and summed in bfloat16 or wider, within the bound.
No kernel may reach another device: no remote copies, remote signals or barrier semaphores. Data moves between devices by JAX's collectives and lax.ppermute only.
A program may use at most 512 MiB of HBM per device.

v0:
```python
import math

import jax
import jax.numpy as jnp
from jax import lax
from jax.sharding import PartitionSpec as P

HEAD = 128


EPS = 1e-05
THETA = 10000.0
MASKED = -1e30


def side_by_side(arrays, axis, dim, along):
    ends, at = ([], 0)
    for a in arrays[:-1]:
        at += a.shape[along]
        ends.append(at)
    both = jnp.concatenate(arrays, axis=along)
    return tuple(jnp.split(lax.all_gather(both, axis, axis=dim, tiled=True), ends, axis=along))


def sent_together(arrays, axis, dim, along):
    widths = [math.prod(a.shape[along:]) for a in arrays]
    both = jnp.concatenate(
        [a.reshape(*a.shape[:along], w) for a, w in zip(arrays, widths)], axis=along
    )
    out = lax.all_gather(both, axis, axis=dim, tiled=True)
    tiles = jnp.split(out, [sum(widths[:k]) for k in range(1, len(widths))], axis=along)
    return tuple((b.reshape(*out.shape[:along], *a.shape[along:]) for a, b in zip(arrays, tiles)))


def from_behind(block, axis, distance):
    devices = range(lax.axis_size(axis))
    route = [(i - distance, i) for i in devices if i - distance in devices]
    return lax.ppermute(block, axis, route)


def rotary_angles(pos_rows, half_size):
    freqs = jnp.exp(-math.log(THETA) * jnp.arange(half_size, dtype=jnp.float32) / half_size)
    angles = pos_rows.astype(jnp.float32)[..., None] * freqs
    return (jnp.cos(angles)[..., None, :], jnp.sin(angles)[..., None, :])


def rotate(vectors, cosines, sine_table):
    half_size = vectors.shape[-1] // 2
    first_half, second_half = (vectors[..., :half_size], vectors[..., half_size:])
    return jnp.concatenate(
        [
            first_half * cosines - second_half * sine_table,
            second_half * cosines + first_half * sine_table,
        ],
        -1,
    )


def unrotate(grads_in, cosines, sine_table):
    half_size = grads_in.shape[-1] // 2
    first_half, second_half = (grads_in[..., :half_size], grads_in[..., half_size:])
    return jnp.concatenate(
        [
            first_half * cosines + second_half * sine_table,
            second_half * cosines - first_half * sine_table,
        ],
        -1,
    )


def project(rows_in, weight):
    return jnp.dot(rows_in, weight, preferred_element_type=jnp.float32)


def norm_scale(stream):
    return lax.rsqrt(jnp.mean(stream * stream, -1, keepdims=True) + EPS)


def store(buffer, slot_index, update, is_valid):
    current = lax.dynamic_index_in_dim(buffer, slot_index, 0, keepdims=False)
    return lax.dynamic_update_index_in_dim(
        buffer, jnp.where(is_valid, update, current), slot_index, 0
    )


def unit_mask_of(gran_level, ff_full):
    width_units = (
        jnp.where(gran_level == 0, ff_full // 8, 0)
        + jnp.where(gran_level == 1, ff_full // 4, 0)
        + jnp.where(gran_level == 2, ff_full // 2, 0)
        + jnp.where(gran_level == 3, ff_full, 0)
    )
    return (jnp.arange(ff_full) < width_units).astype(jnp.float32)


def attention_inputs(layer_in, pos_here, weights):
    attention_gain, attention_in = (weights[0], weights[1])
    model_width = layer_in.shape[-1]
    leading = layer_in.shape[:2]
    head_shape = leading + (model_width // HEAD, HEAD)
    scale_first = norm_scale(layer_in)
    normed = (layer_in * scale_first * attention_gain).astype(jnp.bfloat16)
    projected = project(normed, attention_in)
    cosines, sine_table = rotary_angles(pos_here, HEAD // 2)
    queries = rotate(projected[..., :model_width].reshape(head_shape), cosines, sine_table).astype(
        jnp.bfloat16
    )
    keys_here = rotate(
        projected[..., model_width : 2 * model_width].reshape(head_shape), cosines, sine_table
    )
    keys_here = keys_here.astype(jnp.bfloat16).reshape(leading + (model_width,))
    values_here = projected[..., 2 * model_width :].astype(jnp.bfloat16)
    return (scale_first, normed, queries, keys_here, values_here, cosines, sine_table)


def attention_core(queries, keys_whole, values_whole, pos_here, pos_whole):
    seq_count, seq_length, model_width = keys_whole.shape
    head_count = model_width // HEAD
    keys_four = keys_whole.reshape(seq_count, seq_length, head_count, HEAD)
    values_four = values_whole.reshape(seq_count, seq_length, head_count, HEAD)
    scores = jnp.einsum("sqhd,skhd->shqk", queries, keys_four, preferred_element_type=jnp.float32)
    scores = scores * (1.0 / math.sqrt(HEAD))
    visible = pos_whole[:, None, None, :] <= pos_here[:, None, :, None]
    scores = jnp.where(visible, scores, MASKED)
    row_max = jnp.max(scores, -1, keepdims=True)
    exponent = jnp.exp(scores - row_max)
    row_total = jnp.sum(exponent, -1, keepdims=True)
    attn_probs = exponent / row_total
    probs_low = attn_probs.astype(jnp.bfloat16)
    combined = jnp.einsum(
        "shqk,skhd->sqhd", probs_low, values_four, preferred_element_type=jnp.float32
    )
    mixed_low = combined.reshape(queries.shape[:2] + (model_width,)).astype(jnp.bfloat16)
    return (attn_probs, probs_low, mixed_low, keys_four, values_four, row_max, row_total)


def block_rest(layer_in, mixed_low, gran_level, weights):
    attention_out, feed_gain, feed_up, feed_down = (weights[2], weights[3], weights[4], weights[5])
    middle = layer_in + project(mixed_low, attention_out)
    normed_two = (middle * norm_scale(middle) * feed_gain).astype(jnp.bfloat16)
    unit_mask = unit_mask_of(gran_level, feed_up.shape[1])
    up_proj = project(normed_two, feed_up)
    hidden = (jax.nn.gelu(up_proj, approximate=False) * unit_mask).astype(jnp.bfloat16)
    return middle + project(hidden, feed_down)


def feed_backward(normed_two, grad_out, feed_up, feed_down, acc_up, acc_down, unit_mask):
    up_proj = project(normed_two, feed_up)
    activated, gelu_back = jax.vjp(
        lambda value: jax.nn.gelu(value, approximate=False) * unit_mask, up_proj
    )
    hidden = activated.astype(jnp.bfloat16)
    branch_out = grad_out.astype(jnp.bfloat16)
    acc_down = acc_down + jnp.einsum(
        "sqf,sqd->fd", hidden, branch_out, preferred_element_type=jnp.float32
    )
    grad_hidden = jnp.einsum(
        "sqd,fd->sqf", branch_out, feed_down, preferred_element_type=jnp.float32
    )
    grad_up = gelu_back(grad_hidden)[0].astype(jnp.bfloat16)
    acc_up = acc_up + jnp.einsum(
        "sqd,sqf->df", normed_two, grad_up, preferred_element_type=jnp.float32
    )
    grad_normed = jnp.einsum("sqf,df->sqd", grad_up, feed_up, preferred_element_type=jnp.float32)
    return (grad_normed, acc_up, acc_down)


def layer_backward(
    layer_in,
    grad_out,
    parts,
    keys_whole,
    values_whole,
    pos_here,
    pos_whole,
    gran_level,
    weights,
    grads_acc,
):
    attention_gain, attention_in, attention_out, feed_gain, feed_up, feed_down = weights
    acc_gain_one, acc_in, acc_out, acc_gain_two, acc_up, acc_down = grads_acc
    scale_first, normed, queries, keys_here, values_here, cosines, sine_table = parts
    attn_probs, probs_low, mixed_low, keys_four, values_four, row_max, row_total = attention_core(
        queries, keys_whole, values_whole, pos_here, pos_whole
    )
    model_width = layer_in.shape[-1]
    score_scale = 1.0 / math.sqrt(HEAD)
    middle = layer_in + project(mixed_low, attention_out)
    scale_second = norm_scale(middle)
    normed_middle = middle * scale_second
    normed_two = (normed_middle * feed_gain).astype(jnp.bfloat16)
    unit_mask = unit_mask_of(gran_level, feed_up.shape[1])
    grad_normed_two, acc_up, acc_down = feed_backward(
        normed_two, grad_out, feed_up, feed_down, acc_up, acc_down, unit_mask
    )
    scaled_two = grad_normed_two * feed_gain
    acc_gain_two = acc_gain_two + jnp.sum(grad_normed_two * normed_middle, (0, 1))
    grad_middle = grad_out + scale_second * (
        scaled_two - normed_middle * jnp.mean(scaled_two * normed_middle, -1, keepdims=True)
    )
    branch_attn = grad_middle.astype(jnp.bfloat16)
    acc_out = acc_out + jnp.einsum(
        "sqd,sqe->de", mixed_low, branch_attn, preferred_element_type=jnp.float32
    )
    grad_mixed = jnp.einsum(
        "sqe,de->sqd", branch_attn, attention_out, preferred_element_type=jnp.float32
    )
    grad_mixed = grad_mixed.astype(jnp.bfloat16).reshape(queries.shape)
    grad_probs = jnp.einsum(
        "sqhd,skhd->shqk", grad_mixed, values_four, preferred_element_type=jnp.float32
    )
    weighted_sum = jnp.sum(attn_probs * grad_probs, -1, keepdims=True)
    grad_scores = attn_probs * (grad_probs - weighted_sum)
    scores_low = grad_scores.astype(jnp.bfloat16)
    grad_queries = (
        jnp.einsum("shqk,skhd->sqhd", scores_low, keys_four, preferred_element_type=jnp.float32)
        * score_scale
    )
    head_shape = queries.shape
    queries_all, grad_mixed_all = (
        lax.all_gather(queries, "ctx", axis=1, tiled=True),
        lax.all_gather(grad_mixed, "ctx", axis=1, tiled=True),
    )
    max_all, total_all, weighted_all = side_by_side((row_max, row_total, weighted_sum), "ctx", 2, 0)
    keys_local = keys_here.reshape(head_shape)
    values_local = values_here.reshape(head_shape)
    local_scores = (
        jnp.einsum("sqhd,skhd->shqk", queries_all, keys_local, preferred_element_type=jnp.float32)
        * score_scale
    )
    seen = pos_here[:, None, None, :] <= pos_whole[:, None, :, None]
    local_scores = jnp.where(seen, local_scores, MASKED)
    local_probs = jnp.exp(local_scores - max_all) / total_all
    local_low = local_probs.astype(jnp.bfloat16)
    local_grad_probs = jnp.einsum(
        "sqhd,skhd->shqk", grad_mixed_all, values_local, preferred_element_type=jnp.float32
    )
    local_grad_scores = (local_probs * (local_grad_probs - weighted_all)).astype(jnp.bfloat16)
    grad_keys = (
        jnp.einsum(
            "shqk,sqhd->skhd", local_grad_scores, queries_all, preferred_element_type=jnp.float32
        )
        * score_scale
    )
    grad_values = jnp.einsum(
        "shqk,sqhd->skhd", local_low, grad_mixed_all, preferred_element_type=jnp.float32
    )
    flat_local = head_shape[:2] + (model_width,)
    key_grads = jnp.concatenate(
        [grad_keys.reshape(flat_local), grad_values.reshape(flat_local)], -1
    )
    grad_projected = jnp.concatenate(
        [
            unrotate(grad_queries, cosines, sine_table).reshape(head_shape[:2] + (model_width,)),
            unrotate(key_grads[..., :model_width].reshape(head_shape), cosines, sine_table).reshape(
                head_shape[:2] + (model_width,)
            ),
            key_grads[..., model_width:],
        ],
        -1,
    ).astype(jnp.bfloat16)
    acc_in = acc_in + jnp.einsum(
        "sqd,sqe->de", normed, grad_projected, preferred_element_type=jnp.float32
    )
    grad_normed = jnp.einsum(
        "sqe,de->sqd", grad_projected, attention_in, preferred_element_type=jnp.float32
    )
    normed_first = layer_in * scale_first
    scaled_one = grad_normed * attention_gain
    acc_gain_one = acc_gain_one + jnp.sum(grad_normed * normed_first, (0, 1))
    grad_layer = grad_middle + scale_first * (
        scaled_one - normed_first * jnp.mean(scaled_one * normed_first, -1, keepdims=True)
    )
    return (grad_layer, (acc_gain_one, acc_in, acc_out, acc_gain_two, acc_up, acc_down))


def local(
    inputs,
    cotangent,
    positions,
    granularity,
    attention_gain,
    attention_in,
    attention_out,
    feed_gain,
    feed_up,
    feed_down,
):
    sections = lax.axis_size("section")
    section_index = lax.axis_index("section")
    ctx_index = lax.axis_index("ctx")
    seq_local, tok_local, model_width = inputs.shape
    micro_count = granularity.shape[0]
    per_micro = seq_local // micro_count
    pos_local = lax.dynamic_slice_in_dim(positions, ctx_index * tok_local, tok_local, 1)
    shards = (
        attention_gain[0],
        attention_in[0],
        attention_out[0],
        feed_gain[0],
        feed_up[0],
        feed_down[0],
    )
    weights = (
        *sent_together(
            (shards[0], shards[1], shards[2], shards[3], shards[4]), ("dp", "ctx"), 0, 1
        ),
        lax.all_gather(shards[5], ("dp", "ctx"), axis=0, tiled=True),
    )
    tick_count = micro_count + sections - 1
    kept_inputs = jnp.zeros((micro_count, per_micro, tok_local, model_width), jnp.bfloat16)
    hidden_out = jnp.zeros_like(kept_inputs)
    received = jnp.zeros((per_micro, tok_local, model_width), jnp.bfloat16)
    for tick_index in range(tick_count):
        offset = tick_index - section_index
        is_valid = (offset >= 0) & (offset < micro_count)
        slot_index = jnp.clip(offset, 0, micro_count - 1)
        own_rows = lax.dynamic_slice_in_dim(inputs, slot_index * per_micro, per_micro, 0)
        layer_in = jnp.where(section_index == 0, own_rows, received)
        pos_whole = lax.dynamic_slice_in_dim(positions, slot_index * per_micro, per_micro, 0)
        pos_here = lax.dynamic_slice_in_dim(pos_local, slot_index * per_micro, per_micro, 0)
        layer_float = layer_in.astype(jnp.float32)
        parts = attention_inputs(layer_float, pos_here, weights)
        keys_whole, values_whole = side_by_side((parts[3], parts[4]), "ctx", 1, 0)
        attended = attention_core(parts[2], keys_whole, values_whole, pos_here, pos_whole)
        layer_out = block_rest(layer_float, attended[2], granularity[slot_index], weights).astype(
            jnp.bfloat16
        )
        kept_inputs = store(kept_inputs, slot_index, layer_in, is_valid)
        hidden_out = store(hidden_out, slot_index, layer_out, is_valid)
        received = from_behind(layer_out, "section", 1)
    empty_full = tuple((jnp.zeros(weight.shape, jnp.float32) for weight in weights))
    grad_total = empty_full
    grad_shards = tuple((jnp.zeros(shard.shape, jnp.float32) for shard in shards))
    grad_inputs = jnp.zeros_like(kept_inputs)
    received = jnp.zeros((per_micro, tok_local, model_width), jnp.bfloat16)
    for tick_index in range(tick_count):
        offset = tick_index - (sections - 1 - section_index)
        is_valid = (offset >= 0) & (offset < micro_count)
        slot_index = jnp.clip(offset, 0, micro_count - 1)
        own_grad = lax.dynamic_slice_in_dim(cotangent, slot_index * per_micro, per_micro, 0)
        grad_out = jnp.where(section_index == sections - 1, own_grad, received).astype(jnp.float32)
        grad_out = jnp.where(is_valid, grad_out, 0.0)
        pos_whole = lax.dynamic_slice_in_dim(positions, slot_index * per_micro, per_micro, 0)
        pos_here = lax.dynamic_slice_in_dim(pos_local, slot_index * per_micro, per_micro, 0)
        layer_float = lax.dynamic_index_in_dim(kept_inputs, slot_index, 0, keepdims=False).astype(
            jnp.float32
        )
        parts = attention_inputs(layer_float, pos_here, weights)
        keys_whole, values_whole = side_by_side((parts[3], parts[4]), "ctx", 1, 0)
        gran_level = granularity[slot_index]
        grad_layer, grad_total = layer_backward(
            layer_float,
            grad_out,
            parts,
            keys_whole,
            values_whole,
            pos_here,
            pos_whole,
            gran_level,
            weights,
            grad_total,
        )
        grad_low = grad_layer.astype(jnp.bfloat16)
        grad_inputs = store(grad_inputs, slot_index, grad_low, is_valid)
        received = from_behind(grad_low, "section", -1)
    grad_shards = lax.psum_scatter(grad_total, ("dp", "ctx"), scatter_dimension=0, tiled=True)
    hidden_shard = hidden_out.reshape(seq_local, tok_local, model_width)[None]
    grads_shard = grad_inputs.reshape(seq_local, tok_local, model_width)[None]
    return (
        hidden_shard,
        grads_shard,
        grad_shards[0][None],
        grad_shards[1][None],
        grad_shards[2][None],
        grad_shards[3][None],
        grad_shards[4][None],
        grad_shards[5][None],
    )


def solution(mesh):
    in_specs = (
        P("dp", "ctx", None),
        P("dp", "ctx", None),
        P("dp", None),
        P("dp"),
        P("section", ("dp", "ctx")),
        P("section", ("dp", "ctx"), None),
        P("section", ("dp", "ctx"), None),
        P("section", ("dp", "ctx")),
        P("section", ("dp", "ctx"), None),
        P("section", ("dp", "ctx"), None),
    )
    out_specs = (
        P("section", "dp", "ctx", None),
        P("section", "dp", "ctx", None),
        P("section", ("dp", "ctx")),
        P("section", ("dp", "ctx"), None),
        P("section", ("dp", "ctx"), None),
        P("section", ("dp", "ctx")),
        P("section", ("dp", "ctx"), None),
        P("section", ("dp", "ctx"), None),
    )
    return jax.shard_map(local, mesh=mesh, in_specs=in_specs, out_specs=out_specs, check_vma=False)
```

profile of v0, /device:TPU:0, one launch (start us, length us, event | category | flops | bytes accessed | tf_op | source)
XLA Modules:
  0.0 2156.6 jit_solution(4248484543007209097)
XLA Ops:
  13.4 173.3 %all-gather.16.cloned.1.call-done = bf16[1536,12290]{1,0:T(8,128)(2,1)} async-done(((bf16[24,12290]{1,0:T(8,128)(2,1)}), bf16[1536,12290]{1,0:T(8,128)(2,1)}) %all-gather.16.cloned.1.call-update) | async-done | bytes 37754896 | tf_op jit(solution)/shard_map/all_gather | solution.py:30
  205.6 52.7 %all-gather.18.cloned.1.call-done = bf16[2,1024,1536]{2,1,0:T(8,128)(2,1)} async-done(((bf16[2,64,1536]{2,1,0:T(8,128)(2,1)}), bf16[2,1024,1536]{2,1,0:T(8,128)(2,1)}) %all-gather.18.cloned.1.call-update) | async-done | bytes 6291472 | tf_op jit(solution)/shard_map/all_gather | solution.py:22
  278.7 94.4 %all-gather.42.cloned.1.call-done = bf16[1,6144,1536]{2,1,0:T(8,128)(2,1)} async-done(((bf16[1,96,1536]{2,1,0:T(8,128)(2,1)}), bf16[1,6144,1536]{2,1,0:T(8,128)(2,1)}) %all-gather.42.cloned.1.call-update) | async-done | bytes 18874384 | tf_op jit(solution)/shard_map/all_gather | solution.py:308
  373.1 19.6 bitcast_dynamic-update-slice_fusion.15
  392.7 13.7 collective-permute-start
  427.5 56.4 %all-gather.20.cloned.1.call-done = bf16[2,1024,1536]{2,1,0:T(8,128)(2,1)} async-done(((bf16[2,64,1536]{2,1,0:T(8,128)(2,1)}), bf16[2,1024,1536]{2,1,0:T(8,128)(2,1)}) %all-gather.20.cloned.1.call-update) | async-done | bytes 6291472 | tf_op jit(solution)/shard_map/all_gather | solution.py:22
  504.3 19.7 bitcast_dynamic-update-slice_fusion.14
  560.7 44.8 %all-gather.24.cloned.1.call-done = bf16[2,1024,1536]{2,1,0:T(8,128)(2,1)} async-done(((bf16[2,64,1536]{2,1,0:T(8,128)(2,1)}), bf16[2,1024,1536]{2,1,0:T(8,128)(2,1)}) %all-gather.24.cloned.1.call-update) | async-done | bytes 6291472 | tf_op jit(solution)/shard_map/all_gather | solution.py:22
  640.0 12.7 add_convert_fusion.2
  652.7 15.6 multiply_reduce_fusion.5
  717.1 27.0 %all_gather.58 = f32[3,12,1024,1]{1,3,0,2:T(1,128)S(1)} all-gather(f32[3,12,64,1]{1,3,0,2:T(1,128)} %copy.404), channel_id=1, replica_groups=mesh['section'=2,'dp'=4,'ctx'=16] {'ctx'}, dimensions={2}, use_global_device_ids=true | all-gather | bytes 156672 | tf_op jit(solution)/shard_map/all_gather | solution.py:22
  885.3 26.0 %all_gather.62 = f32[3,12,1024,1]{1,3,0,2:T(1,128)S(1)} all-gather(f32[3,12,64,1]{1,3,0,2:T(1,128)S(1)} %copy.426), channel_id=1, replica_groups=mesh['section'=2,'dp'=4,'ctx'=16] {'ctx'}, dimensions={2}, use_global_device_ids=true | all-gather | bytes 156672 | tf_op jit(solution)/shard_map/all_gather | solution.py:22
  1042.6 27.7 %all_gather.66 = f32[3,12,1024,1]{1,3,0,2:T(1,128)S(1)} all-gather(f32[3,12,64,1]{1,3,0,2:T(1,128)S(1)} %copy.448), channel_id=1, replica_groups=mesh['section'=2,'dp'=4,'ctx'=16] {'ctx'}, dimensions={2}, use_global_device_ids=true | all-gather | bytes 156672 | tf_op jit(solution)/shard_map/all_gather | solution.py:22
  1091.3 30.0 %add_add_fusion.2 = f32[1536,4608]{1,0:T(8,128)} fusion(f32[1536,4608]{1,0:T(8,128)} %fusion.622, f32[1536,4608]{1,0:T(8,128)} %fusion.619, bf16[64,4608]{1,0:T(8,128)(2,1)S(1)} %bitcast_dynamic-update-slice_fusion, f32[64]{0:T(128)S(1)} %copy-done.165, f32[1536]{0:T(1024)S(1)} %get-tuple-element.9, bf16[2,1,64,1536]{3,2,1,0:T(8,128)(2,1)S(1)} %get-tuple-element.31, ...), kind=kOutput, calls=%fused_computation.5 | convolution fusion | flops 920518656 | bytes 85729792 | tf_op jit(solution)/shard_map/sqd,sqe->de/dot_general | solution.py:262
  1122.7 15.6 fusion.757
  1138.3 15.6 fusion.758
  1154.0 39.8 %add_add_fusion.1 = f32[1536,6144]{1,0:T(8,128)} fusion(f32[1536,6144]{1,0:T(8,128)} %fusion.757, f32[1536,6144]{1,0:T(8,128)} %fusion.758, bf16[64,6144]{1,0:T(8,128)(2,1)S(1)} %copy-done.81, f32[64,1536]{1,0:T(8,128)S(1)} %copy-done.44, f32[64]{0:T(128)S(1)} %copy-done.178, f32[1536]{0:T(1024)S(1)} %get-tuple-element.8), kind=kOutput, calls=%fused_computation.4 | convolution fusion | flops 1227128832 | bytes 114432256 | tf_op jit(solution)/shard_map/sqd,sqf->df/dot_general | solution.py:161
  1195.2 17.8 fusion.309
  1213.1 16.7 fusion.310
  1229.7 39.5 %add_add_fusion = f32[6144,1536]{1,0:T(8,128)} fusion(f32[6144,1536]{1,0:T(8,128)} %fusion.309, f32[6144,1536]{1,0:T(8,128)} %fusion.310, f32[64,6144]{1,0:T(8,128)S(1)} %copy-done.38, f32[6144]{0:T(1024)} %fusion.630, bf16[1,64,1536]{2,1,0:T(8,128)(2,1)S(1)} %copy-done.48, pred[]{:T(512)S(6)} %and.25), kind=kOutput, calls=%fused_computation.3 | convolution fusion | flops 1253081088 | bytes 115040256 | tf_op jit(solution)/shard_map/sqf,sqd->fd/dot_general | solution.py:154
  1295.0 21.2 fusion.96
  1327.2 325.1 %all-reduce.2 = (f32[1536]{0:T(1024)S(1)}, f32[1536]{0:T(1024)S(1)}) all-reduce(f32[1536]{0:T(1024)S(1)} %add_add_fusion.4, f32[1536]{0:T(1024)S(1)} %add_add_fusion.3), channel_id=3, replica_groups=mesh['section'=2,'dp'=4,'ctx'=16] {'dp','ctx'}, use_global_device_ids=true, to_apply=%region_36.37.clone | all-reduce | flops 3072 | bytes 24576
  1654.6 187.2 %reduce-scatter.9.cloned.1.call-done = f32[24,6144]{1,0:T(8,128)} async-done(((f32[1536,6144]{1,0:T(8,128)}), f32[24,6144]{1,0:T(8,128)}) %reduce-scatter.9.cloned.1.call-update) | async-done | bytes 589840 | tf_op jit(solution)/shard_map/reduce_scatter | solution.py:367
  1841.8 307.4 %reduce-scatter.11.cloned.1.call-done = f32[96,1536]{1,0:T(8,128)} async-done(((f32[6144,1536]{1,0:T(8,128)}), f32[96,1536]{1,0:T(8,128)}) %reduce-scatter.11.cloned.1.call-update) | async-done | bytes 589840 | tf_op jit(solution)/shard_map/reduce_scatter | solution.py:367
  (687 shorter events, 523.5 us)
Async XLA Ops:
  7.2 179.5 %all-gather.16.cloned.1.call-start = ((), (), s32[]{:S(2)}) async-start(), calls=%async_computation.4 | async-start | bytes 38737920 | tf_op jit(solution)/shard_map/all_gather | solution.py:30
  11.2 247.1 %all-gather.18.cloned.1.call-start = ((), (), s32[]{:S(2)}) async-start(), calls=%async_computation.5 | async-start | bytes 6684672 | tf_op jit(solution)/shard_map/all_gather | solution.py:22
  188.2 902.8 %copy-start.74 = (f32[1536]{0:T(1024)}, f32[1536]{0:T(1024)S(1)}, u32[]{:S(2)}) copy-start(f32[1536]{0:T(1024)S(1)} %get-tuple-element.9) | copy-start | bytes 18436
  199.0 174.0 %all-gather.42.cloned.1.call-start = ((), (), s32[]{:S(2)}) async-start(), calls=%async_computation.21 | async-start | bytes 19169280 | tf_op jit(solution)/shard_map/all_gather | solution.py:308
  199.8 284.2 %all-gather.20.cloned.1.call-start = ((), (), s32[]{:S(2)}) async-start(), calls=%async_computation.6 | async-start | bytes 6684672 | tf_op jit(solution)/shard_map/all_gather | solution.py:22
  392.7 18.3 collective-permute-start
  422.6 182.9 %all-gather.24.cloned.1.call-start = ((), (), s32[]{:S(2)}) async-start(), calls=%async_computation.8 | async-start | bytes 6684672 | tf_op jit(solution)/shard_map/all_gather | solution.py:22
  524.0 7.5 collective-permute-start.1
  532.3 558.8 %copy-start = (bf16[2,1,64,1536]{3,2,1,0:T(8,128)(2,1)}, bf16[2,1,64,1536]{3,2,1,0:T(8,128)(2,1)S(1)}, u32[]{:S(2)}) copy-start(bf16[2,1,64,1536]{3,2,1,0:T(8,128)(2,1)S(1)} %get-tuple-element.31) | copy-start | bytes 1179652
  543.6 213.2 %all-gather.30.cloned.1.call-start = ((), (), s32[]{:S(2)}) async-start(), calls=%async_computation.11 | async-start | bytes 6684672 | tf_op jit(solution)/shard_map/all_gather | solution.py:22
  555.2 226.3 %all-gather.26.cloned.1.call-start = ((), (), s32[]{:S(2)}) async-start(), calls=%async_computation.9 | async-start | bytes 3342336 | tf_op jit(solution)/shard_map/all_gather | solution.py:221
  560.2 224.7 %all-gather.28.cloned.1.call-start = ((), (), s32[]{:S(2)}) async-start(), calls=%async_computation.10 | async-start | bytes 3342336 | tf_op jit(solution)/shard_map/all_gather | solution.py:222
  679.5 175.8 %all-gather.36.cloned.1.call-start = ((), (), s32[]{:S(2)}) async-start(), calls=%async_computation.14 | async-start | bytes 6684672 | tf_op jit(solution)/shard_map/all_gather | solution.py:22
  699.0 225.1 %all-gather.32.cloned.1.call-start = ((), (), s32[]{:S(2)}) async-start(), calls=%async_computation.12 | async-start | bytes 3342336 | tf_op jit(solution)/shard_map/all_gather | solution.py:221
  708.3 222.7 %all-gather.34.cloned.1.call-start = ((), (), s32[]{:S(2)}) async-start(), calls=%async_computation.13 | async-start | bytes 3342336 | tf_op jit(solution)/shard_map/all_gather | solution.py:222
  805.3 11.7 collective-permute-start.2
  848.7 225.2 %all-gather.38.cloned.1.call-start = ((), (), s32[]{:S(2)}) async-start(), calls=%async_computation.15 | async-start | bytes 3342336 | tf_op jit(solution)/shard_map/all_gather | solution.py:221
  855.2 226.8 %all-gather.40.cloned.1.call-start = ((), (), s32[]{:S(2)}) async-start(), calls=%async_computation.16 | async-start | bytes 3342336 | tf_op jit(solution)/shard_map/all_gather | solution.py:222
  950.6 11.7 collective-permute-start.3
  993.2 281.2 %all-gather.22.cloned.1.call-start = ((), (), s32[]{:S(2)}) async-start(), calls=%async_computation.7 | async-start | bytes 6684672 | tf_op jit(solution)/shard_map/all_gather | solution.py:22
  1005.0 649.6 %reduce-scatter.7.cloned.1.call-start = ((), (), s32[]{:S(2)}) async-start(), calls=%async_computation.18 | async-start | bytes 9584640 | tf_op jit(solution)/shard_map/reduce_scatter | solution.py:367
  1013.2 641.5 %reduce-scatter.5.cloned.1.call-start = ((), (), s32[]{:S(2)}) async-start(), calls=%async_computation.17 | async-start | bytes 28753920 | tf_op jit(solution)/shard_map/reduce_scatter | solution.py:367
  1121.4 720.4 %reduce-scatter.9.cloned.1.call-start = ((), (), s32[]{:S(2)}) async-start(), calls=%async_computation.19 | async-start | bytes 38338560 | tf_op jit(solution)/shard_map/reduce_scatter | solution.py:367
  1193.9 955.4 %reduce-scatter.11.cloned.1.call-start = ((), (), s32[]{:S(2)}) async-start(), calls=%async_computation.20 | async-start | bytes 38338560 | tf_op jit(solution)/shard_map/reduce_scatter | solution.py:367
  (181 other events, 2168.8 us)
Sparse Core Ops, SparseCore 0:
  11.3 175.3 all-gather.15
  199.1 59.0 all-gather.17
  261.6 111.3 all-gather.41
  422.7 61.1 all-gather.19
  543.7 61.7 all-gather.23
  607.5 60.9 all-gather.29
  670.7 47.7 all-gather.25
  720.7 48.1 all-gather.27
  771.0 60.1 all-gather.35
  833.2 47.6 all-gather.31
  883.2 47.7 all-gather.33
  933.0 46.8 all-gather.37
  993.3 47.8 all-gather.39
  1043.7 62.3 all-gather.21
  1112.3 171.1 reduce-scatter.6
  1291.1 244.4 reduce-scatter.4
  1542.4 299.3 reduce-scatter.8
  1849.8 299.3 reduce-scatter.10
where the time goes:
time: 2160 us
  waiting for transfers between devices  929 us (43%)
  matrix products  568 us (26%)
  blocking collectives  406 us (19%)
  local copies, waits for them, and re-layouts  145 us (7%)
  other arithmetic  52.7 us (2%)
  between operations  33.6 us (2%)
  starting transfers between devices  22.4 us (1%)
    reduce_scatter x4, waiting for transfers between devices, local(): lax.psum_scatter(grad_total, ('dp', 'ctx'), scatter_dimension=0, tiled=True)  495 us
    unnamed x1, blocking collectives  325 us
    all_gather x1, waiting for transfers between devices, sent_together(): out = lax.all_gather(both, axis, axis=dim, tiled=True)  173 us
    dot_general x18, matrix products, project(): return jnp.dot(rows_in, weight, preferred_element_type=jnp.float32)  167 us
    all_gather x6, waiting for transfers between devices, side_by_side(): lax.all_gather(both, axis, axis=dim, tiled=True)  154 us
    all_gather x1, waiting for transfers between devices, local(): lax.all_gather(shards[5], ('dp', 'ctx'), axis=0, tiled=True)  94.4 us
    all_gather x3, blocking collectives, side_by_side(): lax.all_gather(both, axis, axis=dim, tiled=True)  80.7 us
    dot_general x3, matrix products, feed_backward(): jnp.einsum('sqf,sqd->fd', hidden, branch_out, preferred_element_type=jnp....  73.9 us
  transfers between devices with their start and end apart: 22, of which 10 were waited for; matrix products, arithmetic and copies ran while one was open for 30% of the time, Pallas kernels for 0%

commit v1 on v0

v1 whole, which is shorter than its diff:
```python
import math

import jax
import jax.numpy as jnp
from jax import lax
from jax.experimental import pallas as pl
from jax.experimental.pallas import tpu as pltpu
from jax.sharding import Mesh
from jax.sharding import PartitionSpec as P

HEAD = 128
EPS = 1e-05
THETA = 10000.0
MASKED = -1e30
BF = jnp.bfloat16
F32 = jnp.float32
PLANE = ("xh", "core", "y")
EVERY = ("sec", "xh", "core", "y", "z")


def shifted(block, axis, distance):
    n = lax.axis_size(axis)
    return lax.ppermute(block, axis, [(i, (i + distance) % n) for i in range(n)])


def gather_ring(block, axis):
    return [block] + [shifted(block, axis, k) for k in range(1, lax.axis_size(axis))]


def gathered(block, axis):
    return jnp.concatenate(gather_ring(block, axis), 0)


def scattered(blocks, axis):
    total = blocks[0].astype(F32)
    for k in range(1, lax.axis_size(axis)):
        total = total + shifted(blocks[k].astype(BF), axis, -k).astype(F32)
    return total


def rolled(array, axis_name, dim):
    n = lax.axis_size(axis_name)
    me = lax.axis_index(axis_name)
    return jnp.concatenate(
        [lax.dynamic_slice_in_dim(array, lax.rem(me - k + n, n), 1, dim) for k in range(n)], dim
    )


def family(block):
    near = shifted(block, "core", 1)
    far = shifted(block, "sec", 1)
    return jnp.concatenate([block, near, far, shifted(far, "core", 1)], 0)


def place(sec, core, y):
    return (sec * 2 + core) * 4 + y


def brought(pair):
    got = []
    for i in (0, 1):
        route = [
            (place(y // 2, core, y), place(y // 2, y % 2, 2 * core + i))
            for core in (0, 1)
            for y in range(4)
        ]
        got.append(lax.ppermute(pair[i], ("sec", "core", "y"), route))
    return jnp.where(lax.axis_index("y") % 2 == 0, got[0], got[1])


def returned(block, layer):
    got = []
    for i in (0, 1):
        route = [
            (place(sec, core, y), place(layer, y // 2, 2 * sec + core))
            for sec in (0, 1)
            for core in (0, 1)
            for y in (i, i + 2)
        ]
        got.append(lax.ppermute(block, ("sec", "core", "y"), route))
    return jnp.stack(got)


def dot(a, b):
    return jnp.dot(a, b, preferred_element_type=F32)


def dot_t(a, b):
    return lax.dot_general(a, b, (((1,), (1,)), ((), ())), preferred_element_type=F32)


def t_dot(a, b):
    return lax.dot_general(a, b, (((0,), (0,)), ((), ())), preferred_element_type=F32)


def norm_scale(v):
    return lax.rsqrt(jnp.mean(v * v, -1, keepdims=True) + EPS)


def gelu_parts(up):
    phi = 0.5 + 0.5 * lax.erf(up * math.sqrt(0.5))
    density = jnp.exp(-0.5 * up * up) * (1.0 / math.sqrt(2.0 * math.pi))
    return up * phi, phi + up * density


def tied(*arrays):
    return lax.optimization_barrier(arrays)


VMEM = pl.BlockSpec(memory_space=pltpu.VMEM)
SMEM = pl.BlockSpec(memory_space=pltpu.SMEM)


def costs(flops, arrays):
    moved = sum(math.prod(a.shape) * jnp.dtype(a.dtype).itemsize for a in arrays)
    return pl.CostEstimate(flops=int(flops), bytes_accessed=int(moved), transcendentals=0)


def call(kernel, out_shape, flops, here, *args, halves):
    return pl.pallas_call(
        kernel,
        out_shape=out_shape,
        in_specs=[SMEM] + [VMEM] * len(args) + [pl.BlockSpec(memory_space=pl.ANY)] * 2,
        out_specs=[VMEM] * len(out_shape),
        scratch_shapes=fetch_scratch(halves),
        compiler_params=pltpu.CompilerParams(vmem_limit_bytes=56 * 2**20),
        cost_estimate=costs(flops, [*args, *halves, *out_shape]),
    )(here, *args, *halves)


def shape(dims, dtype):
    return jax.ShapeDtypeStruct(dims, dtype)


def part_shapes(features):
    return [shape((64, features), F32)] + [shape((64, features), BF)] * 3


def store_parts(total, refs):
    for k, ref in enumerate(refs):
        ref[...] = total[64 * k : 64 * (k + 1)].astype(ref.dtype)


def summed(parts, received):
    total = parts[0].astype(F32)
    for r in received:
        total = total + r.astype(F32)
    return total


def sent_home(parts):
    return [shifted(parts[k], "z", -k) for k in range(1, 4)]


def swap_halves(v):
    return pltpu.roll(v, HEAD // 2, 1)


def fetches(here_ref, mine_ref, other_ref, whole, sems):
    core = here_ref[0]
    block = mine_ref.shape[1]
    copies = []
    for xh in (0, 1):
        for i, (ref, c) in enumerate(((mine_ref, core), (other_ref, 1 - core))):
            at = pl.multiple_of((2 * xh + c) * block, 16)
            copy = pltpu.make_async_copy(ref.at[xh], whole.at[pl.ds(at, block)], sems.at[2 * xh + i])
            copy.start()
            copies.append(copy)
    return copies


def fetched(copies):
    for copy in copies:
        copy.wait()


def fetch_scratch(halves):
    rows, columns = halves[0].shape[1:]
    return [pltpu.VMEM((4 * rows, columns), BF), pltpu.SemaphoreType.DMA((4,))]


def qkv_kernel(here_ref, n_ref, cos_ref, sin_ref, mine_ref, other_ref, q_ref, kv_ref, whole, sems):
    fetched(fetches(here_ref, mine_ref, other_ref, whole, sems))
    width = q_ref.shape[1]
    cos, sin = cos_ref[...], sin_ref[...]
    for j in (0, 1, 2):
        ref, at = (q_ref, 0) if j == 0 else (kv_ref, (j - 1) * width)
        total = dot(n_ref[...], whole[:, j * width : (j + 1) * width])
        for h in range(0, width, HEAD):
            v = total[:, h : h + HEAD]
            if j < 2:
                v = v * cos + swap_halves(v) * sin
            ref[:, at + h : at + h + HEAD] = v.astype(BF)


def masked_scores(q, k, visible):
    return jnp.where(visible, dot_t(q, k) * (1.0 / math.sqrt(HEAD)), MASKED)


def attend_kernel(
    here_ref, q_ref, kv_ref, pq_ref, pk_ref, mine_ref, other_ref, mixed_ref, lse_ref, *refs
):
    *part_refs, whole, sems = refs
    copies = fetches(here_ref, mine_ref, other_ref, whole, sems)
    width = q_ref.shape[1]
    visible = pk_ref[...] <= pq_ref[...]
    for i in range(width // HEAD):
        h = slice(i * HEAD, (i + 1) * HEAD)
        scores = masked_scores(q_ref[:, h], kv_ref[:, h], visible)
        most = jnp.max(scores, -1, keepdims=True)
        exponent = jnp.exp(scores - most)
        total = jnp.sum(exponent, -1, keepdims=True)
        probs = (exponent / total).astype(BF)
        values = kv_ref[:, width + i * HEAD : width + (i + 1) * HEAD]
        mixed_ref[:, h] = dot(probs, values).astype(BF)
        lse_ref[:, h] = jnp.broadcast_to(most + jnp.log(total), (q_ref.shape[0], HEAD))
    fetched(copies)
    store_parts(dot(mixed_ref[...], whole[...]), part_refs)


def attend_back_kernel(
    here_ref, b_ref, q_ref, kv_ref, lse_ref, pq_ref, pk_ref, cos_ref, sin_ref, mine_ref, other_ref,
    dq_ref, own_ref, send_ref, far_ref, whole, sems,
):
    fetched(fetches(here_ref, mine_ref, other_ref, whole, sems))
    tokens, width = q_ref.shape
    scale = 1.0 / math.sqrt(HEAD)
    visible = pk_ref[...] <= pq_ref[...]
    grad_mixed = dot_t(b_ref[...], whole[...]).astype(BF)
    for i in range(width // HEAD):
        h = slice(i * HEAD, (i + 1) * HEAD)
        vh = slice(width + i * HEAD, width + (i + 1) * HEAD)
        q, k, v, g = q_ref[:, h], kv_ref[:, h], kv_ref[:, vh], grad_mixed[:, h]
        probs = jnp.exp(masked_scores(q, k, visible) - lse_ref[:, i * HEAD : i * HEAD + 1])
        grad_probs = dot_t(g, v)
        weighted = jnp.sum(probs * grad_probs, -1, keepdims=True)
        grad_scores = (probs * (grad_probs - weighted)).astype(BF)
        dq = dot(grad_scores, k) * scale
        dq_ref[:, h] = (dq * cos_ref[...] - swap_halves(dq) * sin_ref[...]).astype(BF)
        for lanes, grad in (
            (h, t_dot(grad_scores, q) * scale),
            (vh, t_dot(probs.astype(BF), g)),
        ):
            own_ref[:, lanes] = grad[:tokens]
            send_ref[:tokens, lanes] = grad[tokens : 2 * tokens].astype(BF)
            far_ref[:, lanes] = grad[2 * tokens : 3 * tokens]
            send_ref[tokens:, lanes] = grad[3 * tokens :].astype(BF)


def project_back_kernel(
    here_ref, dq_ref, own_ref, near_ref, far_ref, cos_ref, sin_ref, mine_ref, other_ref,
    grad_ref, *refs,
):
    *part_refs, whole, sems = refs
    copies = fetches(here_ref, mine_ref, other_ref, whole, sems)
    width = dq_ref.shape[1]
    grad_ref[:, :width] = dq_ref[...]
    for h in range(0, 2 * width, HEAD):
        lanes = slice(h, h + HEAD)
        v = own_ref[:, lanes] + near_ref[:, lanes].astype(F32) + far_ref[:, lanes].astype(F32)
        if h < width:
            v = v * cos_ref[...] - swap_halves(v) * sin_ref[...]
        grad_ref[:, width + h : width + h + HEAD] = v.astype(BF)
    fetched(copies)
    store_parts(dot_t(grad_ref[...], whole[...]), part_refs)


def block_grads(refs):
    for i in range(len(refs) // 4):
        left, left_near, right, right_near = refs[4 * i : 4 * i + 4]
        total = t_dot(left[...], right[...]) + t_dot(left_near[...], right_near[...])
        yield i, total.reshape(4, total.shape[0] // 4, total.shape[1])


def weight_grad_kernel(here_ref, *refs):
    (out_ref,) = refs[-1:]
    for _, total in block_grads(refs[:-1]):
        out_ref[:, 0] = total.astype(BF)


def weight_grad_ring_kernel(here_ref, *refs):
    *refs, o0, o1, o2, o3, hold = refs
    rows = hold.shape[1]
    for i, total in block_grads(refs):
        hold[...] = total
        for k, out in enumerate((o0, o1, o2, o3)):
            out[0, rows * i : rows * (i + 1)] = hold[lax.rem(here_ref[1] + k, 4)].astype(out.dtype)


def weight_grads(here, groups, ring):
    tokens, features = groups[0][0].shape
    columns = groups[0][2].shape[1]
    block = features // 16
    rows = block * len(groups)
    args = [a for group in groups for a in group]
    if ring:
        kernel, scratch = weight_grad_ring_kernel, [pltpu.VMEM((4, block, columns), F32)]
        outs = [shape((2, rows, columns), t) for t in (F32, BF, BF, BF)]
        out_specs = [pl.BlockSpec((1, rows, columns), lambda i, here: (i, 0, 0))] * 4
        first = 2
    else:
        kernel, scratch = weight_grad_kernel, []
        outs = [shape((4, 2, rows, columns), BF)]
        out_specs = [pl.BlockSpec((4, 1, rows, columns), lambda i, here: (0, i, 0, 0))]
        first = 3
    left = pl.BlockSpec(
        (tokens, features // 4), lambda i, here: (0, 2 * lax.rem(i + here[first], 2) + here[0])
    )
    right = pl.BlockSpec((tokens, columns), lambda i, here: (0, 0))
    return pl.pallas_call(
        kernel,
        grid_spec=pltpu.PrefetchScalarGridSpec(
            num_scalar_prefetch=1,
            grid=(2,),
            in_specs=[left, left, right, right] * len(groups),
            out_specs=out_specs,
            scratch_shapes=scratch,
        ),
        out_shape=outs,
        compiler_params=pltpu.CompilerParams(vmem_limit_bytes=56 * 2**20),
        cost_estimate=costs(2 * tokens * features * columns * len(groups), args),
    )(here, *args)


def near(array):
    return shifted(array, "core", 1)


def forward(x, weights, gains, tables, hook):
    w_in, w_out, w_feed = weights
    cos, sin, pos_here, pos_whole, unit_mask, here = tables
    x = x.astype(F32)
    normed = (x * norm_scale(x) * gains[0]).astype(BF)
    normed = gathered(normed, "z")
    tokens, features = normed.shape
    width = 4 * w_out[0].shape[1]
    units = w_feed.shape[1] - features
    queries, kv = call(
        qkv_kernel,
        [shape((tokens, width), BF), shape((tokens, 2 * width), BF)],
        2 * tokens * features * 3 * width,
        here, normed, cos, sin, halves=w_in,
    )
    kv = family(kv)
    mixed, lse, *parts = call(
        attend_kernel,
        [shape((tokens, width), BF), shape((tokens, width), F32), *part_shapes(features)],
        2 * tokens * width * (features + 8 * tokens),
        here, queries, kv, pos_here, pos_whole, halves=w_out,
    )
    parts[0] = hook(1, parts[0])
    middle = x + summed(parts, sent_home(parts))
    normed_two = (middle * norm_scale(middle) * gains[1]).astype(BF)
    normed_two = gathered(normed_two, "z")
    up = dot(normed_two, w_feed[:, :units])
    activated, slope = gelu_parts(up)
    activated = (activated * unit_mask).astype(BF)
    slope = slope * unit_mask
    parts = jnp.split(dot(activated, w_feed[:, units:]), 4, 0)
    parts[0] = hook(2, parts[0])
    received = sent_home([p.astype(BF) for p in parts])
    hidden = (middle + summed(parts, received)).astype(BF)
    lefts = [(a, near(a)) for a in (normed, mixed, normed_two, activated)]
    return hidden, (x, queries, kv, lse, middle, slope, lefts)


def norm_backward(v, grad_normed, gain, straight):
    scale = norm_scale(v)
    n = v * scale
    q = grad_normed * gain
    grad_gain = jnp.sum(grad_normed * n, 0)
    return straight + scale * (q - n * jnp.mean(q * n, -1, keepdims=True)), grad_gain


def backward(grad_out, kept, weights, gains, tables, hook, last):
    x, queries, kv, lse, middle, slope, lefts = kept
    normed, mixed, normed_two, activated = lefts
    w_in, w_out, w_feed = weights
    cos, sin, pos_here, pos_whole, unit_mask, here = tables
    tokens, width = queries.shape
    features = x.shape[1]
    units = slope.shape[1]
    branch = gathered(grad_out, "z")
    grad_out = grad_out.astype(F32)
    grad_up = (dot_t(branch, w_feed[:, units:]) * slope).astype(BF)
    parts = jnp.split(dot_t(grad_up, w_feed[:, :units]), 4, 0)
    received = sent_home([p.astype(BF) for p in parts])
    branch_near, grad_up_near = near(branch), near(grad_up)
    received = hook(1, received)
    grad_middle, grad_gain_two = norm_backward(middle, summed(parts, received), gains[1], grad_out)
    branch_low = grad_middle.astype(BF)
    groups = (
        (*normed_two, grad_up, grad_up_near),
        (*activated, branch, branch_near),
    )
    groups, branch_low = tied(groups, branch_low)
    ring = gather_ring(branch_low, "z")
    feed = weight_grads(here, groups, True)
    ring, feed = tied(ring, feed)
    ring = hook(2, ring, feed)
    branch = jnp.concatenate(ring, 0)
    dq, own, send, far = call(
        attend_back_kernel,
        [
            shape((tokens, width), BF),
            shape((tokens, 2 * width), F32),
            shape((2 * tokens, 2 * width), BF),
            shape((tokens, 2 * width), F32),
        ],
        2 * tokens * width * (features + 20 * tokens),
        here, branch, queries, kv, lse, pos_here, pos_whole, cos, sin, halves=w_out,
    )
    branch_near = near(branch)
    send = near(send)
    far = (far + send[tokens:].astype(F32)).astype(BF)
    far = shifted(far, "sec", 1)
    out = t_dot(jnp.concatenate(mixed, 0), jnp.concatenate([branch, branch_near], 0)).astype(BF)
    out = lax.dynamic_index_in_dim(out.reshape(2, 2, -1, features), here[0], 1, keepdims=False)
    far, out = tied(far, out)
    far = hook(3, far, out)
    grad_projected, *parts = call(
        project_back_kernel,
        [shape((tokens, 3 * width), BF), *part_shapes(features)],
        2 * tokens * width * 3 * features,
        here, dq, own, send[:tokens], far, cos, sin, halves=w_in,
    )
    received = sent_home(parts)
    g_in = weight_grads(here, [(*normed, grad_projected, near(grad_projected))], not last)
    received, g_in = tied(received, g_in)
    received = hook(4, received, g_in)
    grad_x, grad_gain_one = norm_backward(x, summed(parts, received), gains[0], grad_middle)
    return grad_x.astype(BF), (grad_gain_one, grad_gain_two)


def home_route():
    return [
        ((dp * 4 + y) * 4 + z, (y * 4 + z) * 4 + dp)
        for dp in range(4)
        for y in range(4)
        for z in range(4)
    ]


def local(
    inputs,
    cotangent,
    positions,
    granularity,
    attention_gain,
    attention_in,
    attention_out,
    feed_gain,
    feed_up,
    feed_down,
):
    sec = lax.axis_index("sec")
    rows, width_in = attention_in.shape[1:]
    model = attention_out.shape[2]
    units = feed_up.shape[2]

    core = lax.axis_index("core")
    x_0 = brought(inputs)

    def layered(mine):
        other = shifted(mine, "sec", 1)
        return jnp.where(sec == 0, mine, other), jnp.where(sec == 0, other, mine)

    def plane(block):
        each = jnp.broadcast_to(block[None], (8, *block.shape))
        mine = lax.all_to_all(each, ("xh", "y"), 0, 0, tiled=True)
        return mine.reshape(2, -1, block.shape[1])

    w_in = attention_in[0].reshape(rows, 3, 4, width_in // 12).transpose(2, 0, 1, 3)
    w_in = lax.all_to_all(w_in.reshape(4, rows, width_in // 4), "z", 0, 0, tiled=True)
    in_0, in_1 = layered(w_in.reshape(4 * rows, width_in // 4))
    gains = jnp.stack([attention_gain[0], feed_gain[0]])
    gains, in_0, in_1, w_up, w_out = tied(gains, in_0, in_1, feed_up[0], attention_out[0])
    in_0 = plane(in_0)
    gains = jnp.broadcast_to(gains[None], (128, 2, rows))
    gains = lax.all_to_all(gains, EVERY, 0, 0, tiled=True).reshape(2, 64, 2, rows)
    gains = gains.transpose(0, 2, 1, 3).reshape(2, 2, 64 * rows).astype(F32)
    w_up = w_up.reshape(rows, 16, 4, units // 64).transpose(2, 0, 1, 3)
    w_up = lax.all_to_all(w_up.reshape(4, rows, units // 4), "z", 0, 0, tiled=True)
    w_up = w_up.reshape(4 * rows, units // 4)
    w_out = lax.ppermute(w_out, ("xh", "core", "y", "z"), home_route())
    out_0, out_1 = layered(w_out)
    feed_0, feed_1 = layered(jnp.concatenate([w_up, feed_down[0]], 1))
    feed_0 = lax.all_gather(feed_0, PLANE, axis=0, tiled=True)
    feed_1 = lax.all_gather(feed_1, PLANE, axis=0, tiled=True)
    out_0 = plane(out_0)
    weights_0 = ((in_0, near(in_0)), (out_0, near(out_0)), feed_0)

    y = lax.axis_index("y")
    seq = lambda a: lax.dynamic_index_in_dim(a, y, 0, keepdims=False)
    facts = jnp.concatenate([positions, jnp.broadcast_to(granularity[:, None], (2, 128))], 1)
    other = shifted(facts, "core", 1)
    facts = jnp.where(core == 0, jnp.concatenate([facts, other]), jnp.concatenate([other, facts]))
    facts = seq(facts)
    level = facts[-1]
    pos = rolled(facts[:-128].reshape(2, 2, 4, -1), "z", 2)
    pos = rolled(rolled(pos, "core", 1), "sec", 0).reshape(4, -1)
    half = HEAD // 2
    freqs = jnp.exp(-math.log(THETA) * jnp.arange(half, dtype=F32) / half)
    angles = pos[0].astype(F32)[:, None] * freqs
    cos, sin = jnp.cos(angles), jnp.sin(angles)
    unit_width = (units // 32) * lax.shift_left(1, level)
    tables = (
        jnp.concatenate([cos, cos], 1),
        jnp.concatenate([-sin, sin], 1),
        pos[0][:, None],
        pos.reshape(1, -1),
        (jnp.arange(units // 4) < unit_width).astype(F32)[None],
        jnp.stack([core, y, lax.axis_index("xh"), 0]),
    )

    late = [in_1, out_1]

    def weights_hook(point, chain):
        chain, *late[:] = tied(chain, *late)
        if point == 1:
            late[:] = [plane(a) for a in late]
        return chain

    def no_hook(point, chain):
        return chain

    hidden_0, kept_0 = forward(x_0, weights_0, gains[0], tables, weights_hook)
    in_1, out_1 = late
    weights_1 = ((in_1, near(in_1)), (out_1, near(out_1)), feed_1)
    hidden_1, kept_1 = forward(hidden_0, weights_1, gains[1], tables, no_hook)

    def ring_sent(parts, ks):
        return [shifted(parts[k], "y", k) for k in ks]

    def ring_sum(parts, received):
        total = summed(parts, received)
        return total[0], shifted(total[1].astype(BF), "xh", 1)

    def met(block, home):
        return block.astype(F32), lax.ppermute(block.astype(BF), "sec", [(1 - home, home)])

    def total(pair):
        return pair[0] + pair[1].astype(F32)

    def columns_home(block):
        block = block.astype(BF).reshape(4, rows, -1)
        return lax.all_to_all(block, "z", 0, 0, tiled=True).astype(F32)

    def direct(out):
        out = out.reshape(8, rows, model)
        return lax.all_to_all(out, ("xh", "y"), 0, 0, tiled=True)

    at = {}

    def hold(chain, *names):
        values = [at[n] for n in names]
        chain, values = tied(chain, values)
        at.update(zip(names, values))
        return chain

    def hook_1(point, chain, *grads):
        if point == 1:
            at["hidden"] = returned(hidden_0, 0)
        if point == 2:
            at["feed"] = grads[0]
            at["a"] = ring_sent(grads[0], (1, 3))
            chain = hold(chain, "hidden")
        if point == 3:
            at["out"] = grads[0]
            chain = hold(chain, "feed")
            at["b"] = ring_sent(at["feed"], (2,))
        if point == 4:
            at["in"] = grads[0]
            chain = hold(chain, "a", "in", "out")
            at["c"] = ring_sent(at["in"], (1, 2, 3))
        return chain

    def hook_0(point, chain, *grads):
        if point == 1:
            chain = hold(chain, "b")
            at["feed"] = ring_sum(at["feed"], [*at["a"], *at["b"]])
            at["out"] = direct(at["out"])
        if point == 2:
            at["feed0"] = grads[0]
            at["a0"] = ring_sent(grads[0], (1, 3))
            chain = hold(chain, "c", "input_grad")
            at["in"] = ring_sum(at["in"], at["c"])
        if point == 3:
            at["out0"] = grads[0]
            chain = hold(chain, "feed", "feed0", "out")
            at["b0"] = ring_sent(at["feed0"], (2,))
            at["feed"] = met(total(at["feed"]), 1)
            at["out"] = met(jnp.sum(at["out"].astype(F32), 0), 1)
        if point == 4:
            at["in0"] = grads[0]
            chain = hold(chain, "in", "a0", "feed", "out", "in0")
            at["in"] = met(total(at["in"]), 1)
        return chain

    grad_1, gain_1 = backward(
        brought(cotangent), kept_1, weights_1, gains[1], tables, hook_1, False
    )
    at["input_grad"] = returned(grad_1, 1)
    grad_0, gain_0 = backward(grad_1, kept_0, weights_0, gains[0], tables, hook_0, True)
    hidden = jnp.where(sec == 0, at["hidden"], returned(hidden_1, 1))[None]
    input_grads = jnp.where(sec == 0, returned(grad_0, 0), at["input_grad"])[None]
    (in_0,) = at["in0"]
    in_0 = in_0.reshape(4, 2, 4, rows, -1).transpose(1, 0, 2, 3, 4).reshape(32, rows, -1)
    in_0 = lax.all_to_all(in_0, ("xh", "y", "z"), 0, 0, tiled=True).astype(F32)
    in_0 = total(met(jnp.sum(in_0.reshape(8, 4, rows, -1), 0), 0))
    feed_0 = total(met(total(ring_sum(at["feed0"], [*at["a0"], *at["b0"]])), 0))
    out_0 = total(met(jnp.sum(direct(at["out0"]).astype(F32), 0), 0))
    feed_1, in_1, out_1 = total(at["feed"]), total(at["in"]), total(at["out"])
    feed = jnp.where(sec == 0, feed_0, feed_1)
    g_up, g_down = jnp.split(feed, 2, 0)
    g_out = jnp.where(sec == 0, out_0, out_1)
    g_in = jnp.where(sec == 0, in_0, columns_home(in_1))
    g_in = g_in.reshape(4, rows, 3, width_in // 12).transpose(1, 2, 0, 3).reshape(rows, width_in)
    g_up = columns_home(g_up)
    g_up = g_up.reshape(4, rows, 16, units // 64).transpose(1, 2, 0, 3).reshape(rows, units)
    back = [(b, a) for a, b in home_route()]
    g_out = lax.ppermute(g_out.astype(BF), ("xh", "core", "y", "z"), back).astype(F32)

    gain_grads = jnp.stack([*gain_0, *gain_1]).reshape(2, 2, 64, rows).transpose(0, 2, 1, 3)
    gain_grads = gain_grads.reshape(128, 2, rows)
    gain_grads = jnp.sum(lax.all_to_all(gain_grads, EVERY, 0, 0, tiled=True), 0)
    return (
        hidden,
        input_grads,
        gain_grads[:1],
        g_in[None],
        g_out[None],
        gain_grads[1:],
        g_up[None],
        g_down[None],
    )


def solution(mesh):
    fine = Mesh(mesh.devices.reshape(2, 2, 2, 4, 4), EVERY)
    dp, ctx = ("xh", "core"), ("y", "z")
    ranks = dp + ctx
    in_specs = (
        P(dp, ctx, None),
        P(dp, ctx, None),
        P(dp, None),
        P(dp),
        P("sec", ranks),
        P("sec", ranks, None),
        P("sec", ranks, None),
        P("sec", ranks),
        P("sec", ranks, None),
        P("sec", ranks, None),
    )
    out_specs = (
        P("sec", dp, ctx, None),
        P("sec", dp, ctx, None),
        P("sec", ranks),
        P("sec", ranks, None),
        P("sec", ranks, None),
        P("sec", ranks),
        P("sec", ranks, None),
        P("sec", ranks, None),
    )
    return jax.shard_map(local, mesh=fine, in_specs=in_specs, out_specs=out_specs, check_vma=False)
```

time: 2160 us -> 739 us (0.34)
  waiting for transfers between devices: 929 us -> 227 us
  matrix products: 568 us -> 31 us
  blocking collectives: 406 us -> 20.9 us
  starting transfers between devices: 22.4 us -> 252 us
  local copies, waits for them, and re-layouts: 145 us -> 55 us
  Pallas kernels: 0 us -> 74.7 us
    dot_general x69 -> x10, matrix products: 568 us -> 31 us  [the longest x4 16.3 us: dot(): return jnp.dot(a, b, preferred_element_type=F32)]
    reduce_scatter x4 -> x0, waiting for transfers between devices: 495 us -> none  [local(): lax.psum_scatter(grad_total, ('dp', 'ctx'), scatter_dimension=0, tiled=True)]
    all_gather x14 -> x2, waiting for transfers between devices: 425 us -> 0.02 us  [the longest x1 0.02 us: local(): feed_1 = lax.all_gather(feed_1, PLANE, axis=0, tiled=True)]
    unnamed x1 -> x0, blocking collectives: 325 us -> none
    ppermute x4 -> x114, starting transfers between devices: 20.1 us -> 173 us  [the longest x94 126 us: shifted(): lax.ppermute(block, axis, [(i, (i + distance) % n) for i in range(n)])]
    ppermute x4 -> x114, waiting for transfers between devices: 8.42 us -> 158 us  [the longest x94 149 us: shifted(): lax.ppermute(block, axis, [(i, (i + distance) % n) for i in range(n)])]
    all_gather x3 -> x0, blocking collectives: 80.7 us -> none  [side_by_side(): lax.all_gather(both, axis, axis=dim, tiled=True)]
    all_to_all x0 -> x11, starting transfers between devices: none -> 78.8 us  [the longest x4 33.4 us: plane(): mine = lax.all_to_all(each, ('xh', 'y'), 0, 0, tiled=True)]
  transfers between devices with their start and end apart: 22 -> 127, of which waited for: 10 -> 43; matrix products, arithmetic and copies ran while one was open for 30% -> 16% of each run, Pallas kernels for 0% -> 9%
where the time goes in v1:
time: 739 us; the launch traced here: 728 us
  starting transfers between devices  252 us (34%)
  waiting for transfers between devices  227 us (31%)
  Pallas kernels  74.7 us (10%)
  local copies, waits for them, and re-layouts  55 us (7%)
  other arithmetic  51.2 us (7%)
  matrix products  31 us (4%)
  blocking collectives  20.9 us (3%)
  between operations  17.2 us (2%)
    ppermute x94, waiting for transfers between devices, shifted(): lax.ppermute(block, axis, [(i, (i + distance) % n) for i in range(n)])  149 us
    ppermute x94, starting transfers between devices, shifted(): lax.ppermute(block, axis, [(i, (i + distance) % n) for i in range(n)])  126 us
    pallas_call x8, Pallas kernels, call(): pl.pallas_call(kernel, out_shape=out_shape, in_specs=[SMEM] + [VMEM] * le...  48.3 us
    all_to_all x4, waiting for transfers between devices, plane(): mine = lax.all_to_all(each, ('xh', 'y'), 0, 0, tiled=True)  47.4 us
    all_to_all x4, starting transfers between devices, plane(): mine = lax.all_to_all(each, ('xh', 'y'), 0, 0, tiled=True)  33.4 us
    pallas_call x4, Pallas kernels, weight_grads(): pl.pallas_call(kernel, grid_spec=pltpu.PrefetchScalarGridSpec(num_scalar_...  26.4 us
    unnamed x228, local copies, waits for them, and re-layouts  16.7 us
    dot_general x4, matrix products, dot(): return jnp.dot(a, b, preferred_element_type=F32)  16.3 us
  transfers between devices with their start and end apart: 127, of which 43 were waited for; matrix products, arithmetic and copies ran while one was open for 16% of the time, Pallas kernels for 9%

profile of v1, /device:TPU:0, one launch (start us, length us, event | category | flops | bytes accessed | tf_op | source)
XLA Modules:
  0.0 728.3 jit_solution(2801788606978146305)
XLA Ops:
  8.6 11.7 %all_to_all.65 = bf16[4,24,1152]{2,1,0:T(8,128)(2,1)S(1)} all-to-all(bf16[4,24,1152]{2,1,0:T(8,128)(2,1)S(1)} %reshape.187), channel_id=1, replica_groups=mesh['sec'=2,'xh'=2,'core'=2,'y'=4,'z'=4] {'z'}, dimensions={0} | all-to-all | bytes 442368 | tf_op jit(solution)/shard_map/all_to_all | solution.py:474
  27.8 9.2 %all_to_all.66 = bf16[4,24,1536]{2,1,0:T(8,128)(2,1)S(1)} all-to-all(bf16[4,24,1536]{2,1,0:T(8,128)(2,1)S(1)} %reshape.194), channel_id=1, replica_groups=mesh['sec'=2,'xh'=2,'core'=2,'y'=4,'z'=4] {'z'}, dimensions={0} | all-to-all | bytes 589824 | tf_op jit(solution)/shard_map/all_to_all | solution.py:483
  38.7 9.9 %collective-permute-done.20 = bf16[96,3072]{1,0:T(8,128)(2,1)S(1)} collective-permute-done((bf16[96,3072]{1,0:T(8,128)(2,1)S(1)}, bf16[96,3072]{1,0:T(8,128)(2,1)S(1)}, u32[]{:S(2)}, u32[]{:S(2)}) %collective-permute-start.20) | collective-permute-done | bytes 589856 | tf_op jit(solution)/shard_map/ppermute | solution.py:23
  67.9 24.0 %all-to-all-done.2 = bf16[8,96,1152]{2,1,0:T(8,128)(2,1)S(1)} async-done(((bf16[8,96,1152]{2,1,0:T(8,128)(2,1)}), bf16[8,96,1152]{2,1,0:T(8,128)(2,1)S(1)}, u32[]{:S(2)}, u32[]{:S(2)}) %all-to-all-start.2) | async-done | bytes 1769504 | tf_op jit(solution)/shard_map/all_to_all | solution.py:470
  96.9 9.5 %all-to-all-start.1 = ((bf16[128,2,24]{2,1,0:T(2,128)(2,1)}), bf16[128,2,24]{2,1,0:T(2,128)(2,1)}, u32[]{:S(2)}, u32[]{:S(2)}) async-start(bf16[128,2,24]{2,1,0:T(2,128)(2,1)} %broadcast_in_dim.23), calls=%async_computation.1 | async-start | bytes 131072 | tf_op jit(solution)/shard_map/all_to_all | solution.py:480
  130.5 14.9 %all-to-all-start.3 = ((bf16[8,24,1536]{2,1,0:T(8,128)(2,1)}), bf16[8,24,1536]{2,1,0:T(8,128)(2,1)}, u32[]{:S(2)}, u32[]{:S(2)}) async-start(bf16[8,24,1536]{2,1,0:T(8,128)(2,1)} %broadcast_in_dim.26), calls=%async_computation.3 | async-start | bytes 1179648 | tf_op jit(solution)/shard_map/all_to_all | solution.py:470
  157.0 13.6 %collective-permute-done.9 = bf16[256,768]{1,0:T(8,128)(2,1)S(1)} collective-permute-done((bf16[256,768]{1,0:T(8,128)(2,1)}, bf16[256,768]{1,0:T(8,128)(2,1)S(1)}, u32[]{:S(2)}, u32[]{:S(2)}) %collective-permute-start.9) | collective-permute-done | bytes 393248 | tf_op jit(solution)/shard_map/ppermute | solution.py:23
  184.2 9.9 %all-to-all-start.6 = ((bf16[8,24,1536]{2,1,0:T(8,128)(2,1)}), bf16[8,24,1536]{2,1,0:T(8,128)(2,1)S(1)}, u32[]{:S(2)}, u32[]{:S(2)}) async-start(bf16[8,24,1536]{2,1,0:T(8,128)(2,1)} %broadcast_in_dim.28), calls=%async_computation.6 | async-start | bytes 1179648 | tf_op jit(solution)/shard_map/all_to_all | solution.py:470
  194.8 16.6 %all-to-all-done.6 = bf16[8,24,1536]{2,1,0:T(8,128)(2,1)S(1)} async-done(((bf16[8,24,1536]{2,1,0:T(8,128)(2,1)}), bf16[8,24,1536]{2,1,0:T(8,128)(2,1)S(1)}, u32[]{:S(2)}, u32[]{:S(2)}) %all-to-all-start.6) | async-done | bytes 589856 | tf_op jit(solution)/shard_map/all_to_all | solution.py:470
  248.9 6.9 collective-permute-done.21
  264.5 8.1 %collective-permute-done.24 = bf16[64,1536]{1,0:T(8,128)(2,1)S(1)} collective-permute-done((bf16[64,1536]{1,0:T(8,128)(2,1)S(1)}, bf16[64,1536]{1,0:T(8,128)(2,1)S(1)}, u32[]{:S(2)}, u32[]{:S(2)}) %collective-permute-start.24) | collective-permute-done | bytes 196640 | tf_op jit(solution)/shard_map/ppermute | solution.py:23
  281.9 7.9 %collective-permute-start.40 = (bf16[64,1536]{1,0:T(8,128)(2,1)S(1)}, bf16[64,1536]{1,0:T(8,128)(2,1)S(1)}, u32[]{:S(2)}, u32[]{:S(2)}) collective-permute-start(bf16[64,1536]{1,0:T(8,128)(2,1)S(1)} %get-tuple-element.360), channel_id=1, source_target_pairs={{0,4},{4,20},{72,68},{76,84},{16,12},{20,28},{88,76},{92,92},{1,5}... | collective-permute-start | bytes 589832 | tf_op jit(solution)/shard_map/ppermute | solution.py:67
  322.9 7.8 %collective-permute-done.35 = bf16[64,1536]{1,0:T(8,128)(2,1)S(1)} collective-permute-done((bf16[64,1536]{1,0:T(8,128)(2,1)S(1)}, bf16[64,1536]{1,0:T(8,128)(2,1)S(1)}, u32[]{:S(2)}, u32[]{:S(2)}) %collective-permute-start.35) | collective-permute-done | bytes 196640 | tf_op jit(solution)/shard_map/ppermute | solution.py:23
  359.4 8.4 %shard_map.165 = (f32[2,192,1536]{2,1,0:T(8,128)}, bf16[2,192,1536]{2,1,0:T(8,128)(2,1)}, bf16[2,192,1536]{2,1,0:T(8,128)(2,1)}, bf16[2,192,1536]{2,1,0:T(8,128)(2,1)}) custom-call(s32[4]{0:T(128)} %pad_add_fusion.3.here_ref, bf16[256,1536]{1,0:T(8,128)(2,1)} %copy-done.31, bf16[256,1536]{1,0:T(8,128)(2,1)} %copy-done.97, bf16[256,1536]{1,0:T(8,128)(2,1)} %copy-done.91, ...), custom_call_target="tpu_custom_call" | custom-call | flops 2415919104 | bytes 6291456 | tf_op jit(solution)/shard_map/pallas_call | solution.py:310
  369.5 8.1 %shard_map.166 = (bf16[256,384]{1,0:T(8,128)(2,1)}, f32[256,768]{1,0:T(8,128)}, bf16[512,768]{1,0:T(8,128)(2,1)}, f32[256,768]{1,0:T(8,128)}) custom-call(s32[4]{0:T(128)} %pad_add_fusion.3.here_ref, bf16[256,1536]{1,0:T(8,128)(2,1)} %copy-done.59, bf16[256,384]{1,0:T(8,128)(2,1)} %get-tuple-element.178.q_ref, bf16[1024,768]{1,0:T(8,128)(2,1)} %copy-done.13, ...), custom_call_target="tpu_custom_call" | custom-call | flops 1308622848 | bytes 6951936 | tf_op jit(solution)/shard_map/pallas_call | solution.py:120
  478.0 21.2 %collective-permute-start.85 = (bf16[2,96,1152]{2,1,0:T(8,128)(2,1)}, bf16[2,96,1152]{2,1,0:T(8,128)(2,1)S(1)}, u32[]{:S(2)}, u32[]{:S(2)}) collective-permute-start(bf16[2,96,1152]{2,1,0:T(8,128)(2,1)} %get-tuple-element.260), channel_id=1, source_target_pairs={{0,4},{4,8},{8,12},{12,0},{1,5},{5,9},{9,13},{13,1},{2,6},{6,10},{... | collective-permute-start | bytes 1327112 | tf_op jit(solution)/shard_map/ppermute | solution.py:23
  510.1 8.6 %collective-permute-done.82 = bf16[64,1536]{1,0:T(8,128)(2,1)S(1)} collective-permute-done((bf16[64,1536]{1,0:T(8,128)(2,1)S(1)}, bf16[64,1536]{1,0:T(8,128)(2,1)S(1)}, u32[]{:S(2)}, u32[]{:S(2)}) %collective-permute-start.82) | collective-permute-done | bytes 196640 | tf_op jit(solution)/shard_map/ppermute | solution.py:23
  518.8 8.5 %shard_map.169 = (f32[2,192,1536]{2,1,0:T(8,128)}, bf16[2,192,1536]{2,1,0:T(8,128)(2,1)}, bf16[2,192,1536]{2,1,0:T(8,128)(2,1)}, bf16[2,192,1536]{2,1,0:T(8,128)(2,1)}) custom-call(s32[4]{0:T(128)} %pad_add_fusion.3.here_ref, bf16[256,1536]{1,0:T(8,128)(2,1)} %pad_maximum_fusion.1.refs_0_, bf16[256,1536]{1,0:T(8,128)(2,1)} %collective-permute-done.78.refs_1_, ...), custom_call_target="tpu_custom_call" | custom-call | flops 2415919104 | bytes 6291456 | tf_op jit(solution)/shard_map/pallas_call | solution.py:310
  534.2 8.1 %shard_map.170 = (bf16[256,384]{1,0:T(8,128)(2,1)}, f32[256,768]{1,0:T(8,128)}, bf16[512,768]{1,0:T(8,128)(2,1)}, f32[256,768]{1,0:T(8,128)}) custom-call(s32[4]{0:T(128)} %pad_add_fusion.3.here_ref, bf16[256,1536]{1,0:T(8,128)(2,1)} %get-tuple-element.365.b_ref, bf16[256,384]{1,0:T(8,128)(2,1)} %get-tuple-element.164.q_ref, bf16[1024,768]{1,0:T(8,128)(2,1)} %copy-done.14, ...), custom_call_target="tpu_custom_call" | custom-call | flops 1308622848 | bytes 6951936 | tf_op jit(solution)/shard_map/pallas_call | solution.py:120
  615.6 11.1 %all-to-all-start.8 = ((f32[128,2,24]{2,1,0:T(2,128)}), f32[128,2,24]{2,1,0:T(2,128)S(1)}, u32[]{:S(2)}, u32[]{:S(2)}) async-start(f32[128,2,24]{2,1,0:T(2,128)} %bitcast.42), calls=%async_computation.8 | async-start | bytes 262144 | tf_op jit(solution)/shard_map/all_to_all | solution.py:626
  631.9 9.8 %all-to-all-done.8 = f32[128,2,24]{2,1,0:T(2,128)S(1)} async-done(((f32[128,2,24]{2,1,0:T(2,128)}), f32[128,2,24]{2,1,0:T(2,128)S(1)}, u32[]{:S(2)}, u32[]{:S(2)}) %all-to-all-start.8) | async-done | bytes 24608 | tf_op jit(solution)/shard_map/all_to_all | solution.py:626
  641.8 7.2 all-to-all-start.9
  658.7 25.5 %collective-permute-done.112 = bf16[192,1536]{1,0:T(8,128)(2,1)S(1)} collective-permute-done((bf16[192,1536]{1,0:T(8,128)(2,1)S(1)}, bf16[192,1536]{1,0:T(8,128)(2,1)S(1)}, u32[]{:S(2)}, u32[]{:S(2)}) %collective-permute-start.112) | collective-permute-done | bytes 589856 | tf_op jit(solution)/shard_map/ppermute | solution.py:23
  697.0 7.4 %collective-permute-done.113 = bf16[192,1536]{1,0:T(8,128)(2,1)} collective-permute-done((bf16[192,1536]{1,0:T(8,128)(2,1)}, bf16[192,1536]{1,0:T(8,128)(2,1)}, u32[]{:S(2)}, u32[]{:S(2)}) %collective-permute-start.113) | collective-permute-done | bytes 589856 | tf_op jit(solution)/shard_map/ppermute | solution.py:540
  (617 shorter events, 437.4 us)
Async XLA Ops:
  7.2 221.6 %all-gather.3.cloned.1.call-start = ((), (), s32[]{:S(2)}) async-start(), calls=%async_computation.13 | async-start | bytes 10027008 | tf_op jit(solution)/shard_map/all_gather | solution.py:488
  49.8 273.0 %all-gather.5.cloned.1.call-start = ((), (), s32[]{:S(2)}) async-start(), calls=%async_computation.14 | async-start | bytes 10027008 | tf_op jit(solution)/shard_map/all_gather | solution.py:489
  51.5 43.0 %collective-permute-start = (bf16[64,1536]{1,0:T(8,128)(2,1)}, bf16[64,1536]{1,0:T(8,128)(2,1)}, u32[]{:S(2)}, u32[]{:S(2)}) collective-permute-start(bf16[64,1536]{1,0:T(8,128)(2,1)} %get-tuple-element.363), channel_id=1, source_target_pairs={{0,0},{4,16},{72,64},{76,80},{16,8},{20,24},{88,72},{92,88},{1,1},... | collective-permute-start | bytes 589832 | tf_op jit(solution)/shard_map/ppermute | solution.py:67
  54.5 40.0 %collective-permute-start.1 = (bf16[64,1536]{1,0:T(8,128)(2,1)}, bf16[64,1536]{1,0:T(8,128)(2,1)}, u32[]{:S(2)}, u32[]{:S(2)}) collective-permute-start(bf16[64,1536]{1,0:T(8,128)(2,1)} %get-tuple-element.362), channel_id=1, source_target_pairs={{0,4},{4,20},{72,68},{76,84},{16,12},{20,28},{88,76},{92,92},{1,5}... | collective-permute-start | bytes 589832 | tf_op jit(solution)/shard_map/ppermute | solution.py:67
  60.1 31.8 %all-to-all-start.2 = ((bf16[8,96,1152]{2,1,0:T(8,128)(2,1)}), bf16[8,96,1152]{2,1,0:T(8,128)(2,1)S(1)}, u32[]{:S(2)}, u32[]{:S(2)}) async-start(bf16[8,96,1152]{2,1,0:T(8,128)(2,1)} %broadcast_in_dim.25), calls=%async_computation.2 | async-start | bytes 3538944 | tf_op jit(solution)/shard_map/all_to_all | solution.py:470
  91.9 55.7 %collective-permute-start.7 = (bf16[2,384,1152]{2,1,0:T(8,128)(2,1)S(1)}, bf16[2,384,1152]{2,1,0:T(8,128)(2,1)S(1)}, u32[]{:S(2)}, u32[]{:S(2)}) collective-permute-start(bf16[2,384,1152]{2,1,0:T(8,128)(2,1)S(1)} %bitcast.100), channel_id=1, source_target_pairs={{0,16},{16,0},{1,17},{17,1},{2,18},{18,2},{3,19},{19,3},{4,20},{20... | collective-permute-start | bytes 5308424 | tf_op jit(solution)/shard_map/ppermute | solution.py:23
  242.5 31.8 %collective-permute-start.27 = (bf16[2,384,1152]{2,1,0:T(8,128)(2,1)S(1)}, bf16[2,384,1152]{2,1,0:T(8,128)(2,1)S(1)}, u32[]{:S(2)}, u32[]{:S(2)}) collective-permute-start(bf16[2,384,1152]{2,1,0:T(8,128)(2,1)S(1)} %bitcast.103), channel_id=1, source_target_pairs={{0,16},{16,0},{1,17},{17,1},{2,18},{18,2},{3,19},{19,3},{4,20},{20... | collective-permute-start | bytes 5308424 | tf_op jit(solution)/shard_map/ppermute | solution.py:23
  308.0 47.4 %collective-permute-start.46 = (bf16[256,1536]{1,0:T(8,128)(2,1)S(1)}, bf16[256,1536]{1,0:T(8,128)(2,1)}, u32[]{:S(2)}, u32[]{:S(2)}) collective-permute-start(bf16[256,1536]{1,0:T(8,128)(2,1)S(1)} %pad_maximum_fusion.4.refs_6_), channel_id=1, source_target_pairs={{0,16},{16,0},{1,17},{17,1},{2,18},{18,2},{3,19},{19,3},{4,20},{20... | collective-permute-start | bytes 2359304 | tf_op jit(solution)/shard_map/ppermute | solution.py:23
  378.7 43.9 %collective-permute-start.69 = (bf16[2,192,1536]{2,1,0:T(8,128)(2,1)}, bf16[2,192,1536]{2,1,0:T(8,128)(2,1)S(1)}, u32[]{:S(2)}, u32[]{:S(2)}) collective-permute-start(bf16[2,192,1536]{2,1,0:T(8,128)(2,1)} %get-tuple-element.215), channel_id=1, source_target_pairs={{0,4},{4,8},{8,12},{12,0},{1,5},{5,9},{9,13},{13,1},{2,6},{6,10},{... | collective-permute-start | bytes 3538952 | tf_op jit(solution)/shard_map/ppermute | solution.py:23
  380.4 42.2 %collective-permute-start.70 = (bf16[2,192,1536]{2,1,0:T(8,128)(2,1)}, bf16[2,192,1536]{2,1,0:T(8,128)(2,1)S(1)}, u32[]{:S(2)}, u32[]{:S(2)}) collective-permute-start(bf16[2,192,1536]{2,1,0:T(8,128)(2,1)} %get-tuple-element.217), channel_id=1, source_target_pairs={{0,12},{4,0},{8,4},{12,8},{1,13},{5,1},{9,5},{13,9},{2,14},{6,2},{... | collective-permute-start | bytes 3538952 | tf_op jit(solution)/shard_map/ppermute | solution.py:23
  440.2 61.8 %collective-permute-start.78 = (bf16[256,1536]{1,0:T(8,128)(2,1)}, bf16[256,1536]{1,0:T(8,128)(2,1)}, u32[]{:S(2)}, u32[]{:S(2)}) collective-permute-start(bf16[256,1536]{1,0:T(8,128)(2,1)} %pad_maximum_fusion.1.refs_0_), channel_id=1, source_target_pairs={{0,16},{16,0},{1,17},{17,1},{2,18},{18,2},{3,19},{19,3},{4,20},{20... | collective-permute-start | bytes 2359304 | tf_op jit(solution)/shard_map/ppermute | solution.py:23
  440.8 58.3 %collective-permute-start.77 = (bf16[2,192,1536]{2,1,0:T(8,128)(2,1)}, bf16[2,192,1536]{2,1,0:T(8,128)(2,1)S(1)}, u32[]{:S(2)}, u32[]{:S(2)}) collective-permute-start(bf16[2,192,1536]{2,1,0:T(8,128)(2,1)} %get-tuple-element.239), channel_id=1, source_target_pairs={{0,8},{4,12},{8,0},{12,4},{1,9},{5,13},{9,1},{13,5},{2,10},{6,14},... | collective-permute-start | bytes 3538952 | tf_op jit(solution)/shard_map/ppermute | solution.py:23
  442.9 118.5 %all-to-all-start.7 = ((bf16[8,24,1536]{2,1,0:T(8,128)(2,1)}), bf16[8,24,1536]{2,1,0:T(8,128)(2,1)}, u32[]{:S(2)}, u32[]{:S(2)}) async-start(bf16[8,24,1536]{2,1,0:T(8,128)(2,1)} %bitcast.35), calls=%async_computation.7 | async-start | bytes 1179648 | tf_op jit(solution)/shard_map/all_to_all | solution.py:551
  478.0 49.9 %collective-permute-start.85 = (bf16[2,96,1152]{2,1,0:T(8,128)(2,1)}, bf16[2,96,1152]{2,1,0:T(8,128)(2,1)S(1)}, u32[]{:S(2)}, u32[]{:S(2)}) collective-permute-start(bf16[2,96,1152]{2,1,0:T(8,128)(2,1)} %get-tuple-element.260), channel_id=1, source_target_pairs={{0,4},{4,8},{8,12},{12,0},{1,5},{5,9},{9,13},{13,1},{2,6},{6,10},{... | collective-permute-start | bytes 1327112 | tf_op jit(solution)/shard_map/ppermute | solution.py:23
  527.3 51.0 %collective-permute-start.98 = (bf16[256,1536]{1,0:T(8,128)(2,1)S(1)}, bf16[256,1536]{1,0:T(8,128)(2,1)}, u32[]{:S(2)}, u32[]{:S(2)}) collective-permute-start(bf16[256,1536]{1,0:T(8,128)(2,1)S(1)} %copy-done.2), channel_id=1, source_target_pairs={{0,16},{16,0},{1,17},{17,1},{2,18},{18,2},{3,19},{19,3},{4,20},{20... | collective-permute-start | bytes 2359304 | tf_op jit(solution)/shard_map/ppermute | solution.py:23
  527.9 33.5 %collective-permute-start.94 = (bf16[192,1536]{1,0:T(8,128)(2,1)}, bf16[192,1536]{1,0:T(8,128)(2,1)}, u32[]{:S(2)}, u32[]{:S(2)}) collective-permute-start(bf16[192,1536]{1,0:T(8,128)(2,1)} %fusion.48), channel_id=1, source_target_pairs={{0,32},{32,0},{1,33},{33,1},{2,34},{34,2},{3,35},{35,3},{4,36},{36... | collective-permute-start | bytes 1769480 | tf_op jit(solution)/shard_map/ppermute | solution.py:23
  544.8 60.9 %collective-permute-start.101 = (bf16[2,192,1536]{2,1,0:T(8,128)(2,1)}, bf16[2,192,1536]{2,1,0:T(8,128)(2,1)}, u32[]{:S(2)}, u32[]{:S(2)}) collective-permute-start(bf16[2,192,1536]{2,1,0:T(8,128)(2,1)} %get-tuple-element.279), channel_id=1, source_target_pairs={{0,4},{4,8},{8,12},{12,0},{1,5},{5,9},{9,13},{13,1},{2,6},{6,10},{... | collective-permute-start | bytes 3538952 | tf_op jit(solution)/shard_map/ppermute | solution.py:23
  544.9 62.1 %collective-permute-start.102 = (bf16[2,192,1536]{2,1,0:T(8,128)(2,1)}, bf16[2,192,1536]{2,1,0:T(8,128)(2,1)}, u32[]{:S(2)}, u32[]{:S(2)}) collective-permute-start(bf16[2,192,1536]{2,1,0:T(8,128)(2,1)} %get-tuple-element.281), channel_id=1, source_target_pairs={{0,12},{4,0},{8,4},{12,8},{1,13},{5,1},{9,5},{13,9},{2,14},{6,2},{... | collective-permute-start | bytes 3538952 | tf_op jit(solution)/shard_map/ppermute | solution.py:23
  602.7 46.9 %collective-permute-start.111 = (bf16[2,192,1536]{2,1,0:T(8,128)(2,1)}, bf16[2,192,1536]{2,1,0:T(8,128)(2,1)}, u32[]{:S(2)}, u32[]{:S(2)}) collective-permute-start(bf16[2,192,1536]{2,1,0:T(8,128)(2,1)} %get-tuple-element.313), channel_id=1, source_target_pairs={{0,8},{4,12},{8,0},{12,4},{1,9},{5,13},{9,1},{13,5},{2,10},{6,14},... | collective-permute-start | bytes 3538952 | tf_op jit(solution)/shard_map/ppermute | solution.py:23
  609.6 47.4 %collective-permute-start.105 = (bf16[64,1536]{1,0:T(8,128)(2,1)}, bf16[64,1536]{1,0:T(8,128)(2,1)S(1)}, u32[]{:S(2)}, u32[]{:S(2)}) collective-permute-start(bf16[64,1536]{1,0:T(8,128)(2,1)} %fusion.55), channel_id=1, source_target_pairs={{0,0},{8,16},{16,4},{24,20},{64,8},{72,24},{80,12},{88,28},{1,1},{... | collective-permute-start | bytes 589832 | tf_op jit(solution)/shard_map/ppermute | solution.py:80
  611.1 45.8 %collective-permute-start.106 = (bf16[64,1536]{1,0:T(8,128)(2,1)}, bf16[64,1536]{1,0:T(8,128)(2,1)}, u32[]{:S(2)}, u32[]{:S(2)}) collective-permute-start(bf16[64,1536]{1,0:T(8,128)(2,1)} %fusion.55), channel_id=1, source_target_pairs={{4,0},{12,16},{20,4},{28,20},{68,8},{76,24},{84,12},{92,28},{5,1},... | collective-permute-start | bytes 589832 | tf_op jit(solution)/shard_map/ppermute | solution.py:80
  613.1 43.2 %collective-permute-start.110 = (bf16[24,1536]{1,0:T(8,128)(2,1)}, bf16[24,1536]{1,0:T(8,128)(2,1)S(1)}, u32[]{:S(2)}, u32[]{:S(2)}) collective-permute-start(bf16[24,1536]{1,0:T(8,128)(2,1)} %select_convert_fusion), channel_id=1, source_target_pairs={{0,0},{4,1},{8,2},{12,3},{16,4},{20,5},{24,6},{28,7},{32,8},{36,9}... | collective-permute-start | bytes 221192 | tf_op jit(solution)/shard_map/ppermute | solution.py:622
  629.0 58.2 %collective-permute-start.108 = (bf16[96,1152]{1,0:T(8,128)(2,1)S(1)}, bf16[96,1152]{1,0:T(8,128)(2,1)S(1)}, u32[]{:S(2)}, u32[]{:S(2)}) collective-permute-start(bf16[96,1152]{1,0:T(8,128)(2,1)S(1)} %fusion.82), channel_id=1, source_target_pairs={{0,64},{1,65},{2,66},{3,67},{4,68},{5,69},{6,70},{7,71},{8,72},{9,... | collective-permute-start | bytes 663560 | tf_op jit(solution)/shard_map/ppermute | solution.py:540
  641.8 46.3 %all-to-all-start.9 = ((bf16[32,24,1152]{2,1,0:T(8,128)(2,1)}), bf16[32,24,1152]{2,1,0:T(8,128)(2,1)}, u32[]{:S(2)}, u32[]{:S(2)}) async-start(bf16[32,24,1152]{2,1,0:T(8,128)(2,1)} %bitcast.45), calls=%async_computation.9 | async-start | bytes 3538944 | tf_op jit(solution)/shard_map/all_to_all | solution.py:609
  (210 other events, 2735.0 us)
Sparse Core Ops, SparseCore 0:
  49.9 94.5 all-gather.2
  147.6 101.0 all-gather.4

commit v2 on v1

v2 whole, which is shorter than its diff:
```python
import math

import jax
import jax.numpy as jnp
from jax import lax
from jax.experimental import pallas as pl
from jax.experimental.pallas import tpu as pltpu
from jax.sharding import Mesh
from jax.sharding import PartitionSpec as P

HEAD = 128
EPS = 1e-05
THETA = 10000.0
MASKED = -1e30
BF = jnp.bfloat16
F32 = jnp.float32
PLANE = ("xh", "core", "y")
EVERY = ("sec", "xh", "core", "y", "z")


def shifted(block, axis, distance):
    n = lax.axis_size(axis)
    return lax.ppermute(block, axis, [(i, (i + distance) % n) for i in range(n)])


def gather_ring(block, axis):
    return [block] + [shifted(block, axis, k) for k in range(1, lax.axis_size(axis))]


def gathered(block, axis):
    return jnp.concatenate(gather_ring(block, axis), 0)


def scattered(blocks, axis):
    total = blocks[0].astype(F32)
    for k in range(1, lax.axis_size(axis)):
        total = total + shifted(blocks[k].astype(BF), axis, -k).astype(F32)
    return total


def rolled(array, axis_name, dim):
    n = lax.axis_size(axis_name)
    me = lax.axis_index(axis_name)
    return jnp.concatenate(
        [lax.dynamic_slice_in_dim(array, lax.rem(me - k + n, n), 1, dim) for k in range(n)], dim
    )


def family(block):
    near = shifted(block, "core", 1)
    far = shifted(block, "sec", 1)
    return jnp.concatenate([block, near, far, shifted(far, "core", 1)], 0)


def place(sec, core, y):
    return (sec * 2 + core) * 4 + y


def brought(pair):
    got = []
    for i in (0, 1):
        route = [
            (place(y // 2, core, y), place(y // 2, y % 2, 2 * core + i))
            for core in (0, 1)
            for y in range(4)
        ]
        got.append(lax.ppermute(pair[i], ("sec", "core", "y"), route))
    return jnp.where(lax.axis_index("y") % 2 == 0, got[0], got[1])


def returned(block, layer):
    got = []
    for i in (0, 1):
        route = [
            (place(sec, core, y), place(layer, y // 2, 2 * sec + core))
            for sec in (0, 1)
            for core in (0, 1)
            for y in (i, i + 2)
        ]
        got.append(lax.ppermute(block, ("sec", "core", "y"), route))
    return jnp.stack(got, -3)


def dot(a, b):
    return jnp.dot(a, b, preferred_element_type=F32)


def dot_t(a, b):
    return lax.dot_general(a, b, (((1,), (1,)), ((), ())), preferred_element_type=F32)


def t_dot(a, b):
    return lax.dot_general(a, b, (((0,), (0,)), ((), ())), preferred_element_type=F32)


def norm_scale(v):
    return lax.rsqrt(jnp.mean(v * v, -1, keepdims=True) + EPS)


def gelu_parts(up):
    phi = 0.5 + 0.5 * lax.erf(up * math.sqrt(0.5))
    density = jnp.exp(-0.5 * up * up) * (1.0 / math.sqrt(2.0 * math.pi))
    return up * phi, phi + up * density


def tied(*arrays):
    return lax.optimization_barrier(arrays)


VMEM = pl.BlockSpec(memory_space=pltpu.VMEM)
SMEM = pl.BlockSpec(memory_space=pltpu.SMEM)


LIGHT = pl.CostEstimate(flops=1, bytes_accessed=1, transcendentals=0)


def call(kernel, out_shape, here, *args, blocks=()):
    return pl.pallas_call(
        kernel,
        out_shape=out_shape,
        in_specs=[SMEM] + [VMEM] * len(args) + [pl.BlockSpec(memory_space=pl.ANY)] * len(blocks),
        out_specs=[VMEM] * len(out_shape),
        scratch_shapes=fetch_scratch(blocks) if blocks else [],
        compiler_params=pltpu.CompilerParams(vmem_limit_bytes=56 * 2**20),
        cost_estimate=LIGHT,
    )(here, *args, *blocks)


def shape(dims, dtype):
    return jax.ShapeDtypeStruct(dims, dtype)


def part_shapes(features):
    return [shape((64, features), F32)] + [shape((64, features), BF)] * 3


def store_parts(total, refs):
    for k, ref in enumerate(refs):
        ref[...] = total[64 * k : 64 * (k + 1)].astype(ref.dtype)


def summed(parts, received):
    total = parts[0].astype(F32)
    for r in received:
        total = total + r.astype(F32)
    return total


def sent_home(parts):
    return [shifted(parts[k], "z", -k) for k in range(1, 4)]


def swap_halves(v):
    return pltpu.roll(v, HEAD // 2, 1)


def fetches(here_ref, refs, whole, sems, lanes=slice(None)):
    copies = []
    each = len(refs) // 2
    ys = 4 if each > 1 or len(refs[0].shape) == 4 else 1
    for i, ref in enumerate(refs):
        core = here_ref[0] if i < each else 1 - here_ref[0]
        for j in range(ys // each):
            part = ref.at[j] if len(ref.shape) == 4 else ref
            y = j if each == 1 else lax.rem(here_ref[1] + 4 - i % each, 4)
            block = part.shape[1]
            for dx in (0, 1):
                xh = lax.rem(here_ref[2] + dx, 2)
                at = pl.multiple_of(((2 * xh + core) * ys + y) * block, 32)
                copy = pltpu.make_async_copy(
                    part.at[dx, :, lanes], whole.at[pl.ds(at, block), lanes], sems.at[len(copies)]
                )
                copy.start()
                copies.append(copy)
    return copies


def fetched(copies):
    for copy in copies:
        copy.wait()


def fetch_scratch(blocks):
    rows = sum(math.prod(a.shape[:-1]) for a in blocks)
    return [pltpu.VMEM((rows, blocks[0].shape[-1]), BF), pltpu.SemaphoreType.DMA((32,))]


def qkv_kernel(here_ref, n_ref, cos_ref, sin_ref, *refs):
    *refs, q_ref, kv_ref, whole, sems = refs
    fetched(fetches(here_ref, refs, whole, sems))
    width = q_ref.shape[1]
    cos, sin = cos_ref[...], sin_ref[...]
    for j in (0, 1, 2):
        ref, at = (q_ref, 0) if j == 0 else (kv_ref, (j - 1) * width)
        total = dot(n_ref[...], whole[:, j * width : (j + 1) * width])
        for h in range(0, width, HEAD):
            v = total[:, h : h + HEAD]
            if j < 2:
                v = v * cos + swap_halves(v) * sin
            ref[:, at + h : at + h + HEAD] = v.astype(BF)


def masked_scores(q, k, visible):
    return jnp.where(visible, dot_t(q, k) * (1.0 / math.sqrt(HEAD)), MASKED)


def attend_kernel(
    here_ref, q_ref, kv_ref, pq_ref, pk_ref, mine_ref, other_ref, mixed_ref, lse_ref, *refs
):
    *part_refs, whole, sems = refs
    copies = fetches(here_ref, (mine_ref, other_ref), whole, sems)
    width = q_ref.shape[1]
    visible = pk_ref[...] <= pq_ref[...]
    for i in range(width // HEAD):
        h = slice(i * HEAD, (i + 1) * HEAD)
        scores = masked_scores(q_ref[:, h], kv_ref[:, h], visible)
        most = jnp.max(scores, -1, keepdims=True)
        exponent = jnp.exp(scores - most)
        total = jnp.sum(exponent, -1, keepdims=True)
        probs = (exponent / total).astype(BF)
        values = kv_ref[:, width + i * HEAD : width + (i + 1) * HEAD]
        mixed_ref[:, h] = dot(probs, values).astype(BF)
        lse_ref[:, h] = jnp.broadcast_to(most + jnp.log(total), (q_ref.shape[0], HEAD))
    fetched(copies)
    store_parts(dot(mixed_ref[...], whole[...]), part_refs)


def attend_back_kernel(
    here_ref, b_ref, q_ref, kv_ref, lse_ref, pq_ref, pk_ref, cos_ref, sin_ref, mine_ref, other_ref,
    dq_ref, own_ref, send_ref, far_ref, whole, sems,
):
    fetched(fetches(here_ref, (mine_ref, other_ref), whole, sems))
    tokens, width = q_ref.shape
    scale = 1.0 / math.sqrt(HEAD)
    visible = pk_ref[...] <= pq_ref[...]
    grad_mixed = dot_t(b_ref[...], whole[...]).astype(BF)
    for i in range(width // HEAD):
        h = slice(i * HEAD, (i + 1) * HEAD)
        vh = slice(width + i * HEAD, width + (i + 1) * HEAD)
        q, k, v, g = q_ref[:, h], kv_ref[:, h], kv_ref[:, vh], grad_mixed[:, h]
        probs = jnp.exp(masked_scores(q, k, visible) - lse_ref[:, i * HEAD : i * HEAD + 1])
        grad_probs = dot_t(g, v)
        weighted = jnp.sum(probs * grad_probs, -1, keepdims=True)
        grad_scores = (probs * (grad_probs - weighted)).astype(BF)
        dq = dot(grad_scores, k) * scale
        dq_ref[:, h] = (dq * cos_ref[...] - swap_halves(dq) * sin_ref[...]).astype(BF)
        for lanes, grad in (
            (h, t_dot(grad_scores, q) * scale),
            (vh, t_dot(probs.astype(BF), g)),
        ):
            own_ref[:, lanes] = grad[:tokens]
            send_ref[:tokens, lanes] = grad[tokens : 2 * tokens].astype(BF)
            far_ref[:, lanes] = grad[2 * tokens : 3 * tokens]
            send_ref[tokens:, lanes] = grad[3 * tokens :].astype(BF)


def project_back_kernel(here_ref, dq_ref, own_ref, near_ref, far_ref, cos_ref, sin_ref, *refs):
    *refs, grad_ref, p0, p1, p2, p3, whole, sems = refs
    part_refs = (p0, p1, p2, p3)
    copies = fetches(here_ref, refs, whole, sems)
    width = dq_ref.shape[1]
    grad_ref[:, :width] = dq_ref[...]
    for h in range(0, 2 * width, HEAD):
        lanes = slice(h, h + HEAD)
        near = near_ref[: dq_ref.shape[0], lanes]
        v = own_ref[:, lanes] + near.astype(F32) + far_ref[:, lanes].astype(F32)
        if h < width:
            v = v * cos_ref[...] - swap_halves(v) * sin_ref[...]
        grad_ref[:, width + h : width + h + HEAD] = v.astype(BF)
    fetched(copies)
    store_parts(dot_t(grad_ref[...], whole[...]), part_refs)


def feed_kernel(here_ref, n_ref, mask_ref, mine_ref, other_ref, act_ref, slope_ref, *refs):
    *part_refs, whole, sems = refs
    units = act_ref.shape[1]
    pair = (mine_ref, other_ref)
    ups = fetches(here_ref, pair, whole, sems.at[pl.ds(0, 16)], slice(0, units))
    downs = fetches(here_ref, pair, whole, sems.at[pl.ds(16, 16)], slice(units, None))
    fetched(ups)
    step = units // 4
    for at in range(0, units, step):
        lanes = slice(at, at + step)
        value, slope = gelu_parts(dot(n_ref[...], whole[:, lanes]))
        act_ref[:, lanes] = (value * mask_ref[:, lanes]).astype(BF)
        slope_ref[:, lanes] = slope * mask_ref[:, lanes]
    fetched(downs)
    store_parts(dot(act_ref[...], whole[:, units:]), part_refs)


def feed_back_kernel(here_ref, b_ref, slope_ref, mine_ref, other_ref, grad_ref, *refs):
    *part_refs, whole, sems = refs
    units = grad_ref.shape[1]
    pair = (mine_ref, other_ref)
    downs = fetches(here_ref, pair, whole, sems.at[pl.ds(16, 16)], slice(units, None))
    ups = fetches(here_ref, pair, whole, sems.at[pl.ds(0, 16)], slice(0, units))
    fetched(downs)
    grad_ref[...] = (dot_t(b_ref[...], whole[:, units:]) * slope_ref[...]).astype(BF)
    fetched(ups)
    store_parts(dot_t(grad_ref[...], whole[:, :units]), part_refs)


def block_grads(refs):
    for i in range(len(refs) // 4):
        left, left_near, right, right_near = refs[4 * i : 4 * i + 4]
        total = t_dot(left[...], right[...]) + t_dot(left_near[...], right_near[...])
        yield i, total.reshape(4, total.shape[0] // 4, total.shape[1])


def weight_grad_kernel(here_ref, *refs):
    *refs, out_ref = refs
    for i, total in block_grads(refs):
        rows = total.shape[1]
        out_ref[:, 0, rows * i : rows * (i + 1)] = total.astype(BF)


def weight_grads(here, groups):
    tokens, features = groups[0][0].shape
    columns = groups[0][2].shape[1]
    rows = features // 16 * len(groups)
    args = [a for group in groups for a in group]
    left = pl.BlockSpec((tokens, features // 4), lambda i, here: (0, 2 * i + here[0]))
    right = pl.BlockSpec((tokens, columns), lambda i, here: (0, 0))
    return pl.pallas_call(
        weight_grad_kernel,
        grid_spec=pltpu.PrefetchScalarGridSpec(
            num_scalar_prefetch=1,
            grid=(2,),
            in_specs=[left, left, right, right] * len(groups),
            out_specs=pl.BlockSpec((4, 1, rows, columns), lambda i, here: (0, i, 0, 0)),
        ),
        out_shape=shape((4, 2, rows, columns), BF),
        compiler_params=pltpu.CompilerParams(vmem_limit_bytes=56 * 2**20),
        cost_estimate=LIGHT,
    )(here, *args)


def near(array):
    return shifted(array, "core", 1)


def with_near(arrays):
    return [*arrays, *(near(a) for a in arrays)]


def layer_pairs(shard):
    sec = lax.axis_index("sec")
    places = [(sec, xh) for sec in (0, 1) for xh in (0, 1)]
    across = [(2 * s + x, 2 * (1 - s) + 1 - x) for s, x in places]
    own = jnp.stack([shard, shifted(shard, "xh", 1)])
    other = jnp.stack([shifted(shard, "sec", 1), lax.ppermute(shard, ("sec", "xh"), across)])
    return jnp.where(sec == 0, own, other), jnp.where(sec == 0, other, own)


def y_gathered(pair):
    return lax.all_gather(pair, "y", axis=0, tiled=False)


def scaled(v):
    return (v * norm_scale(v)).astype(BF)


def attention(x, normed, w_out, tables, hook):
    cos, sin, pos_here, pos_whole, unit_mask, here = tables
    x = x.astype(F32)
    w_in, normed = hook(0, normed)
    normed = jnp.concatenate(normed, 0)
    tokens, features = normed.shape
    width = w_in[0].shape[-1] // 3
    queries, kv = call(
        qkv_kernel,
        [shape((tokens, width), BF), shape((tokens, 2 * width), BF)],
        here, normed, cos, sin, blocks=w_in,
    )
    kv = hook(1, kv)
    kv = family(kv)
    kv = hook(2, kv)
    mixed, lse, *parts = call(
        attend_kernel,
        [shape((tokens, width), BF), shape((tokens, width), F32), *part_shapes(features)],
        here, queries, kv, pos_here, pos_whole, blocks=w_out(),
    )
    parts[0] = hook(3, parts[0])
    middle = x + summed(parts, sent_home(parts))
    return middle, (x, queries, kv, lse, middle), [(a, near(a)) for a in (normed, mixed)], w_in


def feed_forward(middle, w_feed, tables, hook):
    features = middle.shape[1]
    mask, here = tables[4:]
    tokens, units = 4 * middle.shape[0], mask.shape[1]
    normed = gathered(scaled(middle), "z")
    normed = hook(4, normed)
    activated, slope, *parts = call(
        feed_kernel,
        [shape((tokens, units), BF), shape((tokens, units), F32), *part_shapes(features)],
        here, normed, mask, blocks=w_feed(),
    )
    parts[0] = hook(5, parts[0])
    return parts, slope, [(a, near(a)) for a in (normed, activated)]


def arrived(middle, parts, received):
    return (middle + summed(parts, received)).astype(BF)


def norm_backward(v, q, straight):
    scale = norm_scale(v)
    n = v * scale
    return straight + scale * (q - n * jnp.mean(q * n, -1, keepdims=True))


def backward(grad_out, branch, kept, slope, lefts, weights, tables, hook):
    x, queries, kv, lse, middle = kept
    normed, mixed, normed_two, activated = lefts
    w_in, w_out, w_feed = weights
    cos, sin, pos_here, pos_whole, unit_mask, here = tables
    tokens, width = queries.shape
    features = x.shape[1]
    units = slope.shape[1]
    branch = jnp.concatenate(hook(0, branch), 0)
    grad_out = grad_out.astype(F32)
    grad_up, *parts = call(
        feed_back_kernel,
        [shape((tokens, units), BF), *part_shapes(features)],
        here, branch, slope, blocks=w_feed,
    )
    received = sent_home(parts)
    branch_near, grad_up_near = near(branch), near(grad_up)
    received = hook(1, received)
    grad_middle = norm_backward(middle, summed(parts, received), grad_out)
    branch_low = grad_middle.astype(BF)
    groups = (
        (*normed_two, grad_up, grad_up_near),
        (*activated, branch, branch_near),
    )
    groups, branch_low = tied(groups, branch_low)
    ring = gather_ring(branch_low, "z")
    feed = weight_grads(here, groups)
    ring, feed = tied(ring, feed)
    ring = hook(2, ring, feed)
    branch = jnp.concatenate(ring, 0)
    dq, own, send, far = call(
        attend_back_kernel,
        [
            shape((tokens, width), BF),
            shape((tokens, 2 * width), F32),
            shape((2 * tokens, 2 * width), BF),
            shape((tokens, 2 * width), F32),
        ],
        here, branch, queries, kv, lse, pos_here, pos_whole, cos, sin, blocks=w_out,
    )
    dq, own, send, far = hook(6, (dq, own, send, far))
    branch_near = near(branch)
    send = near(send)
    far = (far + send[tokens:].astype(F32)).astype(BF)
    far = shifted(far, "sec", 1)
    out = t_dot(jnp.concatenate(mixed, 0), jnp.concatenate([branch, branch_near], 0)).astype(BF)
    out = lax.dynamic_index_in_dim(out.reshape(2, 2, -1, features), here[0], 1, keepdims=False)
    out = out.reshape(2, 4, -1, features).transpose(1, 0, 2, 3)
    far, out = tied(far, out)
    far = hook(3, far, out)
    grad_projected, *parts = call(
        project_back_kernel,
        [shape((tokens, 3 * width), BF), *part_shapes(features)],
        here, dq, own, send, far, cos, sin, blocks=w_in,
    )
    parts = hook(5, parts)
    received = sent_home(parts)
    g_in = weight_grads(here, [(*normed, grad_projected, near(grad_projected))])
    received, g_in = tied(received, g_in)
    received = hook(4, received, g_in)
    return norm_backward(x, summed(parts, received), grad_middle).astype(BF)


def home_route():
    return [
        ((dp * 4 + y) * 4 + z, (y * 4 + z) * 4 + dp)
        for dp in range(4)
        for y in range(4)
        for z in range(4)
    ]


def local(
    inputs,
    cotangent,
    positions,
    granularity,
    attention_gain,
    attention_in,
    attention_out,
    feed_gain,
    feed_up,
    feed_down,
):
    sec = lax.axis_index("sec")
    rows, width_in = attention_in.shape[1:]
    model = attention_out.shape[2]
    units = feed_up.shape[2]

    core = lax.axis_index("core")

    def layered(mine):
        other = shifted(mine, "sec", 1)
        return jnp.where(sec == 0, mine, other), jnp.where(sec == 0, other, mine)

    def with_gain(weight, gain):
        return (weight.astype(F32) * gain.astype(F32)[:, None]).astype(BF)

    w_in = with_gain(attention_in[0], attention_gain[0])
    w_up = with_gain(feed_up[0], feed_gain[0])
    w_in = w_in.reshape(rows, 3, 4, width_in // 12).transpose(2, 0, 1, 3)
    w_up = w_up.reshape(rows, 16, 4, units // 64).transpose(2, 0, 1, 3)
    both = [w_in.reshape(4, rows, width_in // 4), w_up.reshape(4, rows, units // 4)]
    both = lax.all_to_all(jnp.concatenate(both, 2), "z", 0, 0, tiled=True)
    outs = lax.ppermute(attention_out[0], ("xh", "core", "y", "z"), home_route())
    both, inputs, positions, outs = tied(both.reshape(4 * rows, -1), inputs, positions, outs)
    in_0, in_1 = layer_pairs(both[:, : width_in // 4])
    outs = jnp.stack(layer_pairs(outs))
    feed = jnp.concatenate([both[:, width_in // 4 :], feed_down[0]], 1)
    x_0 = brought(inputs)
    feed, in_0, in_1, outs, x_0 = tied(feed, in_0, in_1, outs, x_0)
    in_0 = gather_ring(in_0, "y")
    outs = y_gathered(outs).transpose(1, 2, 0, 3, 4).reshape(2, 2, 4 * rows, model)
    feed_0, feed_1 = layer_pairs(feed)
    normed_0 = gather_ring(scaled(x_0.astype(F32)), "z")
    in_0, feed_0, feed_1, normed_0 = tied(in_0, feed_0, feed_1, normed_0)
    feed_0 = y_gathered(feed_0)
    outs = [with_near([a]) for a in outs]

    y = lax.axis_index("y")
    seq = lambda a: lax.dynamic_index_in_dim(a, y, 0, keepdims=False)
    facts = jnp.concatenate([positions, jnp.broadcast_to(granularity[:, None], (2, 128))], 1)
    other = shifted(facts, "core", 1)
    facts = jnp.where(core == 0, jnp.concatenate([facts, other]), jnp.concatenate([other, facts]))
    facts = seq(facts)
    level = facts[-1]
    pos = rolled(facts[:-128].reshape(2, 2, 4, -1), "z", 2)
    pos = rolled(rolled(pos, "core", 1), "sec", 0).reshape(4, -1)
    here = jnp.stack([core, y, lax.axis_index("xh"), 0])
    half = HEAD // 2
    freqs = jnp.exp(-math.log(THETA) * jnp.arange(half, dtype=F32) / half)
    angles = pos[0].astype(F32)[:, None] * freqs
    cos, sin = jnp.cos(angles), jnp.sin(angles)
    unit_width = (units // 32) * lax.shift_left(1, level)
    tables = (
        jnp.concatenate([cos, cos], 1),
        jnp.concatenate([-sin, sin], 1),
        pos[0][:, None],
        pos.reshape(1, -1),
        (jnp.arange(units // 4) < unit_width).astype(F32)[None],
        here,
    )

    at = {"in_0": in_0, "in": in_1, "feed": feed_1, "cotangent": cotangent, "feed_0": feed_0}
    at["outs"] = outs

    def hold(chain, *names):
        values = [at[n] for n in names]
        chain, values = tied(chain, values)
        at.update(zip(names, values))
        return chain

    def forward_0(point, chain, *more):
        if point == 0:
            chain = hold(chain, "in_0")
            return with_near(at["in_0"]), chain
        if point == 1:
            chain = hold(chain, "outs")
        if point == 2:
            chain = hold(chain, "in", "feed")
            at["in"], at["feed"] = y_gathered(at["in"]), y_gathered(at["feed"])
        if point == 3:
            chain = hold(chain, "cotangent", "feed_0")
            at["feed_0"] = with_near([at["feed_0"]])
            at["cotangent"] = brought(at["cotangent"])
        if point == 5:
            chain = hold(chain, "in", "cotangent")
            at["in"] = with_near([at["in"]])
        return chain

    def forward_1(point, chain, *more):
        if point == 0:
            chain = hold(chain, "in")
            return at["in"], chain
        if point == 1:
            at["branch"] = gather_ring(at["cotangent"], "z")
        if point == 3:
            chain = hold(chain, "branch", "feed")
            at["feed"] = with_near([at["feed"]])
        return chain

    middle_0, kept_0, lefts_0, in_0 = attention(
        x_0, normed_0, lambda: at["outs"][0], tables, forward_0
    )
    parts, slope_0, more = feed_forward(middle_0, lambda: at["feed_0"], tables, forward_0)
    lefts_0 += more
    hidden_0 = arrived(middle_0, parts, sent_home(parts))
    middle_1, kept_1, lefts_1, in_1 = attention(
        hidden_0, gather_ring(scaled(hidden_0.astype(F32)), "z"), lambda: at["outs"][1], tables, forward_1
    )
    parts_1, slope_1, more = feed_forward(middle_1, lambda: at["feed"], tables, forward_1)
    lefts_1 += more
    feed_0, feed_1, cotangent = at["feed_0"], at["feed"], at["cotangent"]
    out_0, out_1 = at["outs"]

    def y_sum(grads):
        flat = grads.reshape(-1, grads.shape[-1])
        flat = lax.psum_scatter(flat, "y", scatter_dimension=0, tiled=True)
        return flat.reshape(grads.shape[1:])

    def x_sum(zero, one):
        both = jnp.concatenate([zero, one], 0)
        both = lax.all_to_all(both, ("sec", "xh"), 0, 0, tiled=True)
        return jnp.sum(both.astype(F32), 0)

    at["parts"] = parts_1

    def backward_1(point, chain, *grads):
        if point == 2:
            at["feed1"] = y_sum(grads[0])
            chain = hold(chain, "parts")
            at["received"] = sent_home(at["parts"])
        if point == 6:
            chain = hold(chain, "received")
        if point == 3:
            at["out1"] = y_sum(grads[0])
        if point == 4:
            chain = hold(chain, "feed1")
            at["in1"] = y_sum(grads[0])
        return chain

    def attention_pair(grad_in, out):
        return jnp.concatenate([grad_in, out.reshape(2, -1, width_in // 4)], 1)

    def backward_0(point, chain, *grads):
        if point == 2:
            chain = hold(chain, "out1", "in1")
            at["feed0"] = y_sum(grads[0])
        if point == 3:
            at["out0"] = y_sum(grads[0])
        if point == 5:
            chain = hold(chain, "feed0")
            at["up"], at["down"] = (
                x_sum(at["feed0"][:, a : a + 4 * rows], at["feed1"][:, a : a + 4 * rows])
                for a in (0, 4 * rows)
            )
        if point == 4:
            at["in0"] = y_sum(grads[0])
        return chain

    grad_1 = backward(
        cotangent, at["branch"], kept_1, slope_1, lefts_1,
        (in_1, out_1, feed_1), tables, backward_1,
    )
    at["to_1"] = jnp.stack([arrived(middle_1, at["parts"], at["received"]), grad_1])
    grad_0 = backward(
        grad_1, gather_ring(grad_1, "z"), kept_0, slope_0, lefts_0,
        (in_0, out_0, feed_0), tables, backward_0,
    )
    def columns_home(block):
        block = block.astype(BF).reshape(4, rows, -1)
        return lax.all_to_all(block, "z", 0, 0, tiled=True).astype(F32)

    to_0, to_1 = returned(jnp.stack([hidden_0, grad_0]), 0), returned(at["to_1"], 1)
    hidden, input_grads = (jnp.where(sec == 0, a, b)[None] for a, b in zip(to_0, to_1))
    g_up, g_down = columns_home(at["up"]), at["down"]
    attn = x_sum(attention_pair(at["in0"], at["out0"]), attention_pair(at["in1"], at["out1"]))
    g_in, g_out = columns_home(attn[: 4 * rows]), attn[4 * rows :].reshape(rows, model)
    g_in = g_in.reshape(4, rows, 3, width_in // 12).transpose(1, 2, 0, 3).reshape(rows, width_in)
    g_up = g_up.reshape(4, rows, 16, units // 64).transpose(1, 2, 0, 3).reshape(rows, units)
    back = [(b, a) for a, b in home_route()]
    g_out = lax.ppermute(g_out.astype(BF), ("xh", "core", "y", "z"), back).astype(F32)


    def home(grad, weight, gain):
        return grad * gain.astype(F32)[:, None], jnp.sum(grad * weight.astype(F32), 1)

    g_in, g_gain = home(g_in, attention_in[0], attention_gain[0])
    g_up, g_gain_two = home(g_up, feed_up[0], feed_gain[0])
    return (
        hidden,
        input_grads,
        g_gain[None],
        g_in[None],
        g_out[None],
        g_gain_two[None],
        g_up[None],
        g_down[None],
    )


def solution(mesh):
    fine = Mesh(mesh.devices.reshape(2, 2, 2, 4, 4), EVERY)
    dp, ctx = ("xh", "core"), ("y", "z")
    ranks = dp + ctx
    in_specs = (
        P(dp, ctx, None),
        P(dp, ctx, None),
        P(dp, None),
        P(dp),
        P("sec", ranks),
        P("sec", ranks, None),
        P("sec", ranks, None),
        P("sec", ranks),
        P("sec", ranks, None),
        P("sec", ranks, None),
    )
    out_specs = (
        P("sec", dp, ctx, None),
        P("sec", dp, ctx, None),
        P("sec", ranks),
        P("sec", ranks, None),
        P("sec", ranks, None),
        P("sec", ranks),
        P("sec", ranks, None),
        P("sec", ranks, None),
    )
    return jax.shard_map(local, mesh=fine, in_specs=in_specs, out_specs=out_specs, check_vma=False)
```

time: 739 us -> 619 us (0.84)
  starting transfers between devices: 252 us -> 142 us
  Pallas kernels: 74.7 us -> 108 us
  matrix products: 31 us -> 1.6 us
  waiting for transfers between devices: 227 us -> 255 us
  blocking collectives: 20.9 us -> 0 us
  local copies, waits for them, and re-layouts: 55 us -> 36.4 us
    all_to_all x9 -> x4, starting transfers between devices: 70.3 us -> 17.5 us  [the longest x3 12 us: x_sum(): both = lax.all_to_all(both, ('sec', 'xh'), 0, 0, tiled=True)]
    ppermute x94 -> x93, starting transfers between devices: 126 us -> 88.9 us  [shifted(): lax.ppermute(block, axis, [(i, (i + distance) % n) for i in range(n)])]
    pallas_call x8 -> x12, Pallas kernels: 48.3 us -> 84.7 us  [call(): pl.pallas_call(kernel, out_shape=out_shape, in_specs=[SMEM] + [VMEM] * le...]
    all_to_all x9 -> x4, waiting for transfers between devices: 63.4 us -> 31.8 us  [the longest x3 23.1 us: x_sum(): both = lax.all_to_all(both, ('sec', 'xh'), 0, 0, tiled=True)]
    dot_general x8 -> x0, matrix products: 28.3 us -> none  [the longest x4 16.3 us: dot(): return jnp.dot(a, b, preferred_element_type=F32)]
    reduce_scatter x0 -> x6, waiting for transfers between devices: none -> 22.5 us  [y_sum(): flat = lax.psum_scatter(flat, 'y', scatter_dimension=0, tiled=True)]
    all_to_all x2 -> x0, blocking collectives: 20.9 us -> none  [the longest x1 11.7 us: local(): lax.all_to_all(w_in.reshape(4, rows, width_in // 4), 'z', 0, 0, tiled=True)]
    ppermute x94 -> x93, waiting for transfers between devices: 149 us -> 169 us  [shifted(): lax.ppermute(block, axis, [(i, (i + distance) % n) for i in range(n)])]
  transfers between devices with their start and end apart: 127 -> 122, of which waited for: 43 -> 59; matrix products, arithmetic and copies ran while one was open for 16% -> 9% of each run, Pallas kernels for 9% -> 15%
where the time goes in v2:
time: 619 us; the launch traced here: 607 us
  waiting for transfers between devices  255 us (41%)
  starting transfers between devices  142 us (23%)
  Pallas kernels  108 us (17%)
  other arithmetic  46.7 us (8%)
  local copies, waits for them, and re-layouts  36.4 us (6%)
  between operations  17 us (3%)
    ppermute x93, waiting for transfers between devices, shifted(): lax.ppermute(block, axis, [(i, (i + distance) % n) for i in range(n)])  169 us
    ppermute x93, starting transfers between devices, shifted(): lax.ppermute(block, axis, [(i, (i + distance) % n) for i in range(n)])  88.9 us
    pallas_call x12, Pallas kernels, call(): pl.pallas_call(kernel, out_shape=out_shape, in_specs=[SMEM] + [VMEM] * le...  84.7 us
    pallas_call x4, Pallas kernels, weight_grads(): pl.pallas_call(weight_grad_kernel, grid_spec=pltpu.PrefetchScalarGridSpec...  23.7 us
    all_to_all x3, waiting for transfers between devices, x_sum(): both = lax.all_to_all(both, ('sec', 'xh'), 0, 0, tiled=True)  23.1 us
    reduce_scatter x6, waiting for transfers between devices, y_sum(): flat = lax.psum_scatter(flat, 'y', scatter_dimension=0, tiled=True)  22.5 us
    unnamed x180, local copies, waits for them, and re-layouts  18.7 us
    all_gather x4, waiting for transfers between devices, y_gathered(): return lax.all_gather(pair, 'y', axis=0, tiled=False)  14.7 us
  transfers between devices with their start and end apart: 122, of which 59 were waited for; matrix products, arithmetic and copies ran while one was open for 9% of the time, Pallas kernels for 15%

profile of v2, /device:TPU:0, one launch (start us, length us, event | category | flops | bytes accessed | tf_op | source)
XLA Modules:
  0.0 607.1 jit_solution(11566953549028750604)
XLA Ops:
  17.9 8.7 %all-to-all-done = bf16[4,24,2688]{2,1,0:T(8,128)(2,1)S(1)} async-done(((bf16[4,24,2688]{2,1,0:T(8,128)(2,1)}), bf16[4,24,2688]{2,1,0:T(8,128)(2,1)S(1)}, u32[]{:S(2)}, u32[]{:S(2)}) %all-to-all-start) | async-done | bytes 516128 | tf_op jit(solution)/shard_map/all_to_all | solution.py:516
  70.4 10.0 %collective-permute-done.13 = bf16[96,3072]{1,0:T(8,128)(2,1)S(1)} collective-permute-done((bf16[96,3072]{1,0:T(8,128)(2,1)S(1)}, bf16[96,3072]{1,0:T(8,128)(2,1)S(1)}, u32[]{:S(2)}, u32[]{:S(2)}) %collective-permute-start.13) | collective-permute-done | bytes 589856 | tf_op jit(solution)/shard_map/ppermute | solution.py:23
  108.8 10.5 %collective-permute-done.26 = bf16[256,768]{1,0:T(8,128)(2,1)S(1)} collective-permute-done((bf16[256,768]{1,0:T(8,128)(2,1)}, bf16[256,768]{1,0:T(8,128)(2,1)S(1)}, u32[]{:S(2)}, u32[]{:S(2)}) %collective-permute-start.26) | collective-permute-done | bytes 393248 | tf_op jit(solution)/shard_map/ppermute | solution.py:23
  130.1 14.6 %all-gather.11.cloned.1.call-done = bf16[8,96,3072]{2,1,0:T(8,128)(2,1)} async-done(((bf16[2,96,3072]{2,1,0:T(8,128)(2,1)}), bf16[8,96,3072]{2,1,0:T(8,128)(2,1)}) %all-gather.11.cloned.1.call-update) | async-done | bytes 4718608 | tf_op jit(solution)/shard_map/all_gather | solution.py:356
  151.3 7.1 %collective-permute-done.28 = bf16[64,1536]{1,0:T(8,128)(2,1)S(1)} collective-permute-done((bf16[64,1536]{1,0:T(8,128)(2,1)}, bf16[64,1536]{1,0:T(8,128)(2,1)S(1)}, u32[]{:S(2)}, u32[]{:S(2)}) %collective-permute-start.28) | collective-permute-done | bytes 196640 | tf_op jit(solution)/shard_map/ppermute | solution.py:23
  167.5 8.3 %collective-permute-done.31 = bf16[64,1536]{1,0:T(8,128)(2,1)S(1)} collective-permute-done((bf16[64,1536]{1,0:T(8,128)(2,1)S(1)}, bf16[64,1536]{1,0:T(8,128)(2,1)S(1)}, u32[]{:S(2)}, u32[]{:S(2)}) %collective-permute-start.31) | collective-permute-done | bytes 196640 | tf_op jit(solution)/shard_map/ppermute | solution.py:23
  181.7 8.4 %shard_map.163 = (bf16[256,1536]{1,0:T(8,128)(2,1)}, f32[256,1536]{1,0:T(8,128)}, f32[64,1536]{1,0:T(8,128)}, bf16[64,1536]{1,0:T(8,128)(2,1)}, bf16[64,1536]{1,0:T(8,128)(2,1)}, /*index=5*/bf16[64,1536]{1,0:T(8,128)(2,1)}) custom-call(s32[4]{0:T(128)} %pad_add_fusion.3.here_ref, bf16[256,1536]{1,0:T(8,128)(2,1)} %pad_maximum_fusion.5.n_ref.refs_0_, ...), custom_call_target="tpu_custom_call" | custom-call | flops 1 | bytes 1 | tf_op jit(solution)/shard_map/pallas_call | solution.py:118
  209.5 9.1 %collective-permute-done.40 = bf16[64,1536]{1,0:T(8,128)(2,1)S(1)} collective-permute-done((bf16[64,1536]{1,0:T(8,128)(2,1)S(1)}, bf16[64,1536]{1,0:T(8,128)(2,1)S(1)}, u32[]{:S(2)}, u32[]{:S(2)}) %collective-permute-start.40) | collective-permute-done | bytes 196640 | tf_op jit(solution)/shard_map/ppermute | solution.py:23
  227.5 10.1 %collective-permute-done.45 = bf16[256,768]{1,0:T(8,128)(2,1)S(1)} collective-permute-done((bf16[256,768]{1,0:T(8,128)(2,1)}, bf16[256,768]{1,0:T(8,128)(2,1)S(1)}, u32[]{:S(2)}, u32[]{:S(2)}) %collective-permute-start.45) | collective-permute-done | bytes 393248 | tf_op jit(solution)/shard_map/ppermute | solution.py:23
  254.7 8.4 %collective-permute-done.50 = bf16[64,1536]{1,0:T(8,128)(2,1)S(1)} collective-permute-done((bf16[64,1536]{1,0:T(8,128)(2,1)}, bf16[64,1536]{1,0:T(8,128)(2,1)S(1)}, u32[]{:S(2)}, u32[]{:S(2)}) %collective-permute-start.50) | collective-permute-done | bytes 196640 | tf_op jit(solution)/shard_map/ppermute | solution.py:23
  271.5 8.3 %collective-permute-done.53 = bf16[64,1536]{1,0:T(8,128)(2,1)S(1)} collective-permute-done((bf16[64,1536]{1,0:T(8,128)(2,1)S(1)}, bf16[64,1536]{1,0:T(8,128)(2,1)S(1)}, u32[]{:S(2)}, u32[]{:S(2)}) %collective-permute-start.53) | collective-permute-done | bytes 196640 | tf_op jit(solution)/shard_map/ppermute | solution.py:23
  283.5 8.4 %shard_map.166 = (bf16[256,1536]{1,0:T(8,128)(2,1)}, f32[256,1536]{1,0:T(8,128)}, f32[64,1536]{1,0:T(8,128)}, bf16[64,1536]{1,0:T(8,128)(2,1)}, bf16[64,1536]{1,0:T(8,128)(2,1)}, /*index=5*/bf16[64,1536]{1,0:T(8,128)(2,1)}) custom-call(s32[4]{0:T(128)} %pad_add_fusion.3.here_ref, bf16[256,1536]{1,0:T(8,128)(2,1)} %pad_maximum_fusion.6.n_ref.refs_0_, ...), custom_call_target="tpu_custom_call" | custom-call | flops 1 | bytes 1 | tf_op jit(solution)/shard_map/pallas_call | solution.py:118
  292.0 8.2 %shard_map.167 = (bf16[256,1536]{1,0:T(8,128)(2,1)}, f32[64,1536]{1,0:T(8,128)}, bf16[64,1536]{1,0:T(8,128)(2,1)}, bf16[64,1536]{1,0:T(8,128)(2,1)}, bf16[64,1536]{1,0:T(8,128)(2,1)}) custom-call(s32[4]{0:T(128)} %pad_add_fusion.3.here_ref, bf16[256,1536]{1,0:T(8,128)(2,1)} %copy-done.15, f32[256,1536]{1,0:T(8,128)} %get-tuple-element.256.slope_ref, ...), custom_call_target="tpu_custom_call" | custom-call | flops 1 | bytes 1 | tf_op jit(solution)/shard_map/pallas_call | solution.py:118
  304.3 7.4 %collective-permute-done.57 = bf16[64,1536]{1,0:T(8,128)(2,1)S(1)} collective-permute-done((bf16[64,1536]{1,0:T(8,128)(2,1)}, bf16[64,1536]{1,0:T(8,128)(2,1)S(1)}, u32[]{:S(2)}, u32[]{:S(2)}) %collective-permute-start.57) | collective-permute-done | bytes 196640 | tf_op jit(solution)/shard_map/ppermute | solution.py:23
  320.7 7.3 %shard_map.168 = bf16[4,2,192,1536]{3,2,1,0:T(8,128)(2,1)} custom-call(s32[4]{0:T(128)} %pad_add_fusion.3.here_ref, bf16[256,1536]{1,0:T(8,128)(2,1)} %pad_maximum_fusion.6.n_ref.refs_0_, bf16[256,1536]{1,0:T(8,128)(2,1)} %copy-done.46, bf16[256,1536]{1,0:T(8,128)(2,1)} %get-tuple-element.266.refs_2_, bf16[256,1536]{1,0:T(8,128)(2,1)} %copy-done.48, ...), custom_call_target="tpu_custom_call" | custom-call | flops 1 | bytes 1 | tf_op jit(solution)/shard_map/pallas_call | solution.py:324
  334.8 8.3 %shard_map.169 = (bf16[256,384]{1,0:T(8,128)(2,1)}, f32[256,768]{1,0:T(8,128)}, bf16[512,768]{1,0:T(8,128)(2,1)}, f32[256,768]{1,0:T(8,128)}) custom-call(s32[4]{0:T(128)} %pad_add_fusion.3.here_ref, bf16[256,1536]{1,0:T(8,128)(2,1)} %copy-done.31, bf16[256,384]{1,0:T(8,128)(2,1)} %get-tuple-element.241.q_ref, bf16[1024,768]{1,0:T(8,128)(2,1)} %copy-done.1, ...), custom_call_target="tpu_custom_call" | custom-call | flops 1 | bytes 1 | tf_op jit(solution)/shard_map/pallas_call | solution.py:118
  351.3 8.7 %collective-permute-done.71.far_ref = bf16[256,768]{1,0:T(8,128)(2,1)S(1)} collective-permute-done((bf16[256,768]{1,0:T(8,128)(2,1)S(1)}, bf16[256,768]{1,0:T(8,128)(2,1)S(1)}, u32[]{:S(2)}, u32[]{:S(2)}) %collective-permute-start.71) | collective-permute-done | bytes 393248 | tf_op jit(solution)/shard_map/ppermute | solution.py:23
  397.5 8.2 %shard_map.172 = (bf16[256,1536]{1,0:T(8,128)(2,1)}, f32[64,1536]{1,0:T(8,128)}, bf16[64,1536]{1,0:T(8,128)(2,1)}, bf16[64,1536]{1,0:T(8,128)(2,1)}, bf16[64,1536]{1,0:T(8,128)(2,1)}) custom-call(s32[4]{0:T(128)} %pad_add_fusion.3.here_ref, bf16[256,1536]{1,0:T(8,128)(2,1)} %pad_maximum_fusion.7.b_ref.refs_6_, f32[256,1536]{1,0:T(8,128)} %get-tuple-element.310.slope_ref, ...), custom_call_target="tpu_custom_call" | custom-call | flops 1 | bytes 1 | tf_op jit(solution)/shard_map/pallas_call | solution.py:118
  426.2 7.3 %shard_map.173 = bf16[4,2,192,1536]{3,2,1,0:T(8,128)(2,1)} custom-call(s32[4]{0:T(128)} %pad_add_fusion.3.here_ref, bf16[256,1536]{1,0:T(8,128)(2,1)} %pad_maximum_fusion.5.n_ref.refs_0_, bf16[256,1536]{1,0:T(8,128)(2,1)} %copy-done.44, bf16[256,1536]{1,0:T(8,128)(2,1)} %get-tuple-element.320.refs_2_, bf16[256,1536]{1,0:T(8,128)(2,1)} %copy-done.51, ...), custom_call_target="tpu_custom_call" | custom-call | flops 1 | bytes 1 | tf_op jit(solution)/shard_map/pallas_call | solution.py:324
  436.6 8.3 %shard_map.174 = (bf16[256,384]{1,0:T(8,128)(2,1)}, f32[256,768]{1,0:T(8,128)}, bf16[512,768]{1,0:T(8,128)(2,1)}, f32[256,768]{1,0:T(8,128)}) custom-call(s32[4]{0:T(128)} %pad_add_fusion.3.here_ref, bf16[256,1536]{1,0:T(8,128)(2,1)} %copy-done.32, bf16[256,384]{1,0:T(8,128)(2,1)} %get-tuple-element.210.q_ref, bf16[1024,768]{1,0:T(8,128)(2,1)} %pad_maximum_fusion.kv_ref, ...), custom_call_target="tpu_custom_call" | custom-call | flops 1 | bytes 1 | tf_op jit(solution)/shard_map/pallas_call | solution.py:118
  451.8 8.7 %collective-permute-done.93.far_ref = bf16[256,768]{1,0:T(8,128)(2,1)S(1)} collective-permute-done((bf16[256,768]{1,0:T(8,128)(2,1)S(1)}, bf16[256,768]{1,0:T(8,128)(2,1)S(1)}, u32[]{:S(2)}, u32[]{:S(2)}) %collective-permute-start.93) | collective-permute-done | bytes 393248 | tf_op jit(solution)/shard_map/ppermute | solution.py:23
  468.4 20.6 %reduce-scatter.13.cloned.1.call-done = bf16[384,1536]{1,0:T(8,128)(2,1)} async-done(((bf16[1536,1536]{1,0:T(8,128)(2,1)}), bf16[384,1536]{1,0:T(8,128)(2,1)}) %reduce-scatter.13.cloned.1.call-update) | async-done | bytes 1179664 | tf_op jit(solution)/shard_map/reduce_scatter | solution.py:610
  567.6 13.5 %all-to-all-done.1 = bf16[4,128,1152]{2,1,0:T(8,128)(2,1)S(1)} async-done(((bf16[4,128,1152]{2,1,0:T(8,128)(2,1)}), bf16[4,128,1152]{2,1,0:T(8,128)(2,1)S(1)}, u32[]{:S(2)}, u32[]{:S(2)}) %all-to-all-start.1) | async-done | bytes 1179680 | tf_op jit(solution)/shard_map/all_to_all | solution.py:615
  584.2 7.0 %all-to-all-start.2 = ((bf16[4,24,1152]{2,1,0:T(8,128)(2,1)}), bf16[4,24,1152]{2,1,0:T(8,128)(2,1)S(1)}, u32[]{:S(2)}, u32[]{:S(2)}) async-start(bf16[4,24,1152]{2,1,0:T(8,128)(2,1)} %bitcast.63), calls=%async_computation.8 | async-start | bytes 442368 | tf_op jit(solution)/shard_map/all_to_all | solution.py:664
  (539 shorter events, 364.4 us)
Async XLA Ops:
  17.2 77.7 %all-gather.9.cloned.1.call-start = ((), (), s32[]{:S(2)}) async-start(), calls=%async_computation.18 | async-start | bytes 1474560 | tf_op jit(solution)/shard_map/all_gather | solution.py:356
  49.8 94.9 %all-gather.11.cloned.1.call-start = ((), (), s32[]{:S(2)}) async-start(), calls=%async_computation.19 | async-start | bytes 5898240 | tf_op jit(solution)/shard_map/all_gather | solution.py:356
  53.7 26.7 %collective-permute-start.13 = (bf16[96,3072]{1,0:T(8,128)(2,1)S(1)}, bf16[96,3072]{1,0:T(8,128)(2,1)S(1)}, u32[]{:S(2)}, u32[]{:S(2)}) collective-permute-start(bf16[96,3072]{1,0:T(8,128)(2,1)S(1)} %pad_maximum_fusion.8), channel_id=1, source_target_pairs={{0,64},{64,0},{1,65},{65,1},{2,66},{66,2},{3,67},{67,3},{4,68},{68... | collective-permute-start | bytes 1769480 | tf_op jit(solution)/shard_map/ppermute | solution.py:23
  53.7 29.6 %collective-permute-start.14 = (bf16[96,3072]{1,0:T(8,128)(2,1)S(1)}, bf16[96,3072]{1,0:T(8,128)(2,1)S(1)}, u32[]{:S(2)}, u32[]{:S(2)}) collective-permute-start(bf16[96,3072]{1,0:T(8,128)(2,1)S(1)} %pad_maximum_fusion.8), channel_id=1, source_target_pairs={{0,96},{32,64},{64,32},{96,0},{1,97},{33,65},{65,33},{97,1},{2,98}... | collective-permute-start | bytes 1769480 | tf_op jit(solution)/shard_map/ppermute | solution.py:351
  55.4 34.8 %collective-permute-start.10 = (bf16[2,96,1152]{2,1,0:T(8,128)(2,1)S(1)}, bf16[2,96,1152]{2,1,0:T(8,128)(2,1)}, u32[]{:S(2)}, u32[]{:S(2)}) collective-permute-start(bf16[2,96,1152]{2,1,0:T(8,128)(2,1)S(1)} %get-tuple-element.206.refs_0_), channel_id=1, source_target_pairs={{0,8},{4,12},{8,0},{12,4},{1,9},{5,13},{9,1},{13,5},{2,10},{6,14},... | collective-permute-start | bytes 1327112 | tf_op jit(solution)/shard_map/ppermute | solution.py:23
  63.5 26.7 %collective-permute-start.11 = (bf16[2,96,1152]{2,1,0:T(8,128)(2,1)S(1)}, bf16[2,96,1152]{2,1,0:T(8,128)(2,1)S(1)}, u32[]{:S(2)}, u32[]{:S(2)}) collective-permute-start(bf16[2,96,1152]{2,1,0:T(8,128)(2,1)S(1)} %get-tuple-element.206.refs_0_), channel_id=1, source_target_pairs={{0,12},{4,0},{8,4},{12,8},{1,13},{5,1},{9,5},{13,9},{2,14},{6,2},{... | collective-permute-start | bytes 1327112 | tf_op jit(solution)/shard_map/ppermute | solution.py:23
  67.6 22.7 %collective-permute-start.9 = (bf16[2,96,1152]{2,1,0:T(8,128)(2,1)S(1)}, bf16[2,96,1152]{2,1,0:T(8,128)(2,1)}, u32[]{:S(2)}, u32[]{:S(2)}) collective-permute-start(bf16[2,96,1152]{2,1,0:T(8,128)(2,1)S(1)} %get-tuple-element.206.refs_0_), channel_id=1, source_target_pairs={{0,4},{4,8},{8,12},{12,0},{1,5},{5,9},{9,13},{13,1},{2,6},{6,10},{... | collective-permute-start | bytes 1327112 | tf_op jit(solution)/shard_map/ppermute | solution.py:23
  91.1 99.1 %all-gather.13.cloned.1.call-start = ((), (), s32[]{:S(2)}) async-start(), calls=%async_computation.20 | async-start | bytes 2211840 | tf_op jit(solution)/shard_map/all_gather | solution.py:356
  123.3 126.5 %all-gather.15.cloned.1.call-start = ((), (), s32[]{:S(2)}) async-start(), calls=%async_computation.21 | async-start | bytes 5898240 | tf_op jit(solution)/shard_map/all_gather | solution.py:356
  144.7 37.0 %collective-permute-start.34 = (bf16[4,2,96,3072]{3,2,1,0:T(8,128)(2,1)}, bf16[4,2,96,3072]{3,2,1,0:T(8,128)(2,1)}, u32[]{:S(2)}, u32[]{:S(2)}) collective-permute-start(bf16[4,2,96,3072]{3,2,1,0:T(8,128)(2,1)} %bitcast.109), channel_id=1, source_target_pairs={{0,16},{16,0},{1,17},{17,1},{2,18},{18,2},{3,19},{19,3},{4,20},{20... | collective-permute-start | bytes 14155784 | tf_op jit(solution)/shard_map/ppermute | solution.py:23
  144.8 238.0 %reduce-scatter.7.cloned.1.call-start = ((), (), s32[]{:S(2)}) async-start(), calls=%async_computation.12 | async-start | bytes 5898240 | tf_op jit(solution)/shard_map/reduce_scatter | solution.py:610
  190.2 29.0 %collective-permute-start.43 = (bf16[4,2,96,1152]{3,2,1,0:T(8,128)(2,1)}, bf16[4,2,96,1152]{3,2,1,0:T(8,128)(2,1)S(1)}, u32[]{:S(2)}, u32[]{:S(2)}) collective-permute-start(bf16[4,2,96,1152]{3,2,1,0:T(8,128)(2,1)} %bitcast.115), channel_id=1, source_target_pairs={{0,16},{16,0},{1,17},{17,1},{2,18},{18,2},{3,19},{19,3},{4,20},{20... | collective-permute-start | bytes 5308424 | tf_op jit(solution)/shard_map/ppermute | solution.py:23
  251.6 29.7 %collective-permute-start.56 = (bf16[4,2,96,3072]{3,2,1,0:T(8,128)(2,1)}, bf16[4,2,96,3072]{3,2,1,0:T(8,128)(2,1)S(1)}, u32[]{:S(2)}, u32[]{:S(2)}) collective-permute-start(bf16[4,2,96,3072]{3,2,1,0:T(8,128)(2,1)} %bitcast.112), channel_id=1, source_target_pairs={{0,16},{16,0},{1,17},{17,1},{2,18},{18,2},{3,19},{19,3},{4,20},{20... | collective-permute-start | bytes 14155784 | tf_op jit(solution)/shard_map/ppermute | solution.py:23
  330.0 105.4 %reduce-scatter.9.cloned.1.call-start = ((), (), s32[]{:S(2)}) async-start(), calls=%async_computation.13 | async-start | bytes 737280 | tf_op jit(solution)/shard_map/reduce_scatter | solution.py:610
  361.0 74.6 %reduce-scatter.11.cloned.1.call-start = ((), (), s32[]{:S(2)}) async-start(), calls=%async_computation.14 | async-start | bytes 2211840 | tf_op jit(solution)/shard_map/reduce_scatter | solution.py:610
  381.1 107.9 %reduce-scatter.13.cloned.1.call-start = ((), (), s32[]{:S(2)}) async-start(), calls=%async_computation.15 | async-start | bytes 5898240 | tf_op jit(solution)/shard_map/reduce_scatter | solution.py:610
  435.3 106.0 %reduce-scatter.17.cloned.1.call-start = ((), (), s32[]{:S(2)}) async-start(), calls=%async_computation.17 | async-start | bytes 737280 | tf_op jit(solution)/shard_map/reduce_scatter | solution.py:610
  461.4 98.9 %reduce-scatter.15.cloned.1.call-start = ((), (), s32[]{:S(2)}) async-start(), calls=%async_computation.16 | async-start | bytes 2211840 | tf_op jit(solution)/shard_map/reduce_scatter | solution.py:610
  461.5 34.1 %collective-permute-start.99 = (bf16[256,1536]{1,0:T(8,128)(2,1)S(1)}, bf16[256,1536]{1,0:T(8,128)(2,1)S(1)}, u32[]{:S(2)}, u32[]{:S(2)}) collective-permute-start(bf16[256,1536]{1,0:T(8,128)(2,1)S(1)} %copy-done.10), channel_id=1, source_target_pairs={{0,16},{16,0},{1,17},{17,1},{2,18},{18,2},{3,19},{19,3},{4,20},{20... | collective-permute-start | bytes 2359304 | tf_op jit(solution)/shard_map/ppermute | solution.py:23
  467.9 27.7 %collective-permute-start.100 = (bf16[256,1152]{1,0:T(8,128)(2,1)}, bf16[256,1152]{1,0:T(8,128)(2,1)}, u32[]{:S(2)}, u32[]{:S(2)}) collective-permute-start(bf16[256,1152]{1,0:T(8,128)(2,1)} %get-tuple-element.352.refs_2_), channel_id=1, source_target_pairs={{0,16},{16,0},{1,17},{17,1},{2,18},{18,2},{3,19},{19,3},{4,20},{20... | collective-permute-start | bytes 1769480 | tf_op jit(solution)/shard_map/ppermute | solution.py:23
  507.8 20.8 %all-to-all-start.3 = ((bf16[4,96,1536]{2,1,0:T(8,128)(2,1)}), bf16[4,96,1536]{2,1,0:T(8,128)(2,1)S(1)}, u32[]{:S(2)}, u32[]{:S(2)}) async-start(bf16[4,96,1536]{2,1,0:T(8,128)(2,1)} %pad_maximum_fusion.3), calls=%async_computation.9 | async-start | bytes 2359296 | tf_op jit(solution)/shard_map/all_to_all | solution.py:615
  514.0 38.0 %collective-permute-start.103 = (bf16[2,64,1536]{2,1,0:T(8,128)(2,1)}, bf16[2,64,1536]{2,1,0:T(8,128)(2,1)}, u32[]{:S(2)}, u32[]{:S(2)}) collective-permute-start(bf16[2,64,1536]{2,1,0:T(8,128)(2,1)} %pad_maximum_fusion.15), channel_id=1, source_target_pairs={{0,64},{8,80},{16,68},{24,84},{64,72},{72,88},{80,76},{88,92},{1,6... | collective-permute-start | bytes 1179656 | tf_op jit(solution)/shard_map/ppermute | solution.py:80
  518.6 33.3 %collective-permute-start.104 = (bf16[2,64,1536]{2,1,0:T(8,128)(2,1)}, bf16[2,64,1536]{2,1,0:T(8,128)(2,1)}, u32[]{:S(2)}, u32[]{:S(2)}) collective-permute-start(bf16[2,64,1536]{2,1,0:T(8,128)(2,1)} %pad_maximum_fusion.15), channel_id=1, source_target_pairs={{4,64},{12,80},{20,68},{28,84},{68,72},{76,88},{84,76},{92,92},{5,... | collective-permute-start | bytes 1179656 | tf_op jit(solution)/shard_map/ppermute | solution.py:80
  528.6 20.0 %all-to-all-start.5 = ((bf16[4,96,1536]{2,1,0:T(8,128)(2,1)}), bf16[4,96,1536]{2,1,0:T(8,128)(2,1)S(1)}, u32[]{:S(2)}, u32[]{:S(2)}) async-start(bf16[4,96,1536]{2,1,0:T(8,128)(2,1)} %pad_maximum_fusion.4), calls=%async_computation.11 | async-start | bytes 2359296 | tf_op jit(solution)/shard_map/all_to_all | solution.py:615
  (178 other events, 1517.1 us)
Sparse Core Ops, SparseCore 0:
  49.9 37.1 all-gather.8
  91.2 53.4 all-gather.10
  147.0 29.0 all-gather.12
  177.6 55.2 all-gather.14
  330.1 52.6 reduce-scatter.6
  385.0 21.3 reduce-scatter.8
  408.8 26.7 reduce-scatter.10
  438.1 50.8 reduce-scatter.12
  492.1 21.3 reduce-scatter.16
  515.9 26.9 reduce-scatter.14

commit v3 on v2

--- a/solution.py
+++ b/solution.py
@@ -114,13 +114,13 @@
 LIGHT = pl.CostEstimate(flops=1, bytes_accessed=1, transcendentals=0)
 
 
-def call(kernel, out_shape, here, *args, blocks=()):
+def call(kernel, out_shape, here, *args, rows, blocks):
     return pl.pallas_call(
         kernel,
         out_shape=out_shape,
         in_specs=[SMEM] + [VMEM] * len(args) + [pl.BlockSpec(memory_space=pl.ANY)] * len(blocks),
         out_specs=[VMEM] * len(out_shape),
-        scratch_shapes=fetch_scratch(blocks) if blocks else [],
+        scratch_shapes=fetch_scratch(rows, blocks),
         compiler_params=pltpu.CompilerParams(vmem_limit_bytes=56 * 2**20),
         cost_estimate=LIGHT,
     )(here, *args, *blocks)
@@ -163,12 +163,14 @@
         for j in range(ys // each):
             part = ref.at[j] if len(ref.shape) == 4 else ref
             y = j if each == 1 else lax.rem(here_ref[1] + 4 - i % each, 4)
-            block = part.shape[1]
+            block = whole.shape[0] // (4 * ys)
             for dx in (0, 1):
                 xh = lax.rem(here_ref[2] + dx, 2)
                 at = pl.multiple_of(((2 * xh + core) * ys + y) * block, 32)
                 copy = pltpu.make_async_copy(
-                    part.at[dx, :, lanes], whole.at[pl.ds(at, block), lanes], sems.at[len(copies)]
+                    part.at[dx, pl.ds(0, block), lanes],
+                    whole.at[pl.ds(at, block), lanes],
+                    sems.at[len(copies)],
                 )
                 copy.start()
                 copies.append(copy)
@@ -180,8 +182,7 @@
         copy.wait()
 
 
-def fetch_scratch(blocks):
-    rows = sum(math.prod(a.shape[:-1]) for a in blocks)
+def fetch_scratch(rows, blocks):
     return [pltpu.VMEM((rows, blocks[0].shape[-1]), BF), pltpu.SemaphoreType.DMA((32,))]
 
 
@@ -300,6 +301,25 @@
     store_parts(dot_t(grad_ref[...], whole[:, :units]), part_refs)
 
 
+def feed_both_kernel(here_ref, n_ref, mask_ref, b_ref, mine_ref, other_ref, act_ref, grad_ref, *refs):
+    *part_refs, whole, sems = refs
+    units = act_ref.shape[1]
+    pair = (mine_ref, other_ref)
+    ups = fetches(here_ref, pair, whole, sems.at[pl.ds(0, 16)], slice(0, units))
+    downs = fetches(here_ref, pair, whole, sems.at[pl.ds(16, 16)], slice(units, None))
+    fetched(ups)
+    fetched(downs)
+    step = units // 4
+    for at in range(0, units, step):
+        lanes = slice(at, at + step)
+        value, slope = gelu_parts(dot(n_ref[...], whole[:, lanes]))
+        act_ref[:, lanes] = (value * mask_ref[:, lanes]).astype(BF)
+        back = dot_t(b_ref[...], whole[at : at + step, units:])
+        grad_ref[:, lanes] = (back * (slope * mask_ref[:, lanes])).astype(BF)
+    store_parts(dot_t(grad_ref[...], whole[:, :units]), part_refs[4:])
+    store_parts(dot(act_ref[...], whole[:, units:]), part_refs[:4])
+
+
 def block_grads(refs):
     for i in range(len(refs) // 4):
         left, left_near, right, right_near = refs[4 * i : 4 * i + 4]
@@ -309,16 +329,21 @@
 
 def weight_grad_kernel(here_ref, *refs):
     *refs, out_ref = refs
-    for i, total in block_grads(refs):
+    done = 0
+    for i, total in block_grads(refs[: len(refs) // 4 * 4]):
         rows = total.shape[1]
-        out_ref[:, 0, rows * i : rows * (i + 1)] = total.astype(BF)
-
-
-def weight_grads(here, groups):
+        out_ref[:, 0, done : done + rows] = total.astype(BF)
+        done += rows
+    for ref in refs[len(refs) // 4 * 4 :]:
+        out_ref[:, 0, done:] = ref[:, 0]
+
+
+def weight_grads(here, groups, below=()):
     tokens, features = groups[0][0].shape
     columns = groups[0][2].shape[1]
-    rows = features // 16 * len(groups)
+    rows = features // 16 * len(groups) + sum(a.shape[2] for a in below)
     args = [a for group in groups for a in group]
+    by_xh = lambda n: pl.BlockSpec((4, 1, n, columns), lambda i, here: (0, i, 0, 0))
     left = pl.BlockSpec((tokens, features // 4), lambda i, here: (0, 2 * i + here[0]))
     right = pl.BlockSpec((tokens, columns), lambda i, here: (0, 0))
     return pl.pallas_call(
@@ -326,13 +351,13 @@
         grid_spec=pltpu.PrefetchScalarGridSpec(
             num_scalar_prefetch=1,
             grid=(2,),
-            in_specs=[left, left, right, right] * len(groups),
-            out_specs=pl.BlockSpec((4, 1, rows, columns), lambda i, here: (0, i, 0, 0)),
+            in_specs=[left, left, right, right] * len(groups) + [by_xh(a.shape[2]) for a in below],
+            out_specs=by_xh(rows),
         ),
         out_shape=shape((4, 2, rows, columns), BF),
         compiler_params=pltpu.CompilerParams(vmem_limit_bytes=56 * 2**20),
         cost_estimate=LIGHT,
-    )(here, *args)
+    )(here, *args, *below)
 
 
 def near(array):
@@ -370,7 +395,7 @@
     queries, kv = call(
         qkv_kernel,
         [shape((tokens, width), BF), shape((tokens, 2 * width), BF)],
-        here, normed, cos, sin, blocks=w_in,
+        here, normed, cos, sin, rows=features, blocks=w_in,
     )
     kv = hook(1, kv)
     kv = family(kv)
@@ -378,26 +403,24 @@
     mixed, lse, *parts = call(
         attend_kernel,
         [shape((tokens, width), BF), shape((tokens, width), F32), *part_shapes(features)],
-        here, queries, kv, pos_here, pos_whole, blocks=w_out(),
-    )
-    parts[0] = hook(3, parts[0])
-    middle = x + summed(parts, sent_home(parts))
+        here, queries, kv, pos_here, pos_whole, rows=width, blocks=w_out(),
+    )
+    parts = hook(3, parts)
+    received = hook(7, sent_home(parts))
+    middle = x + summed(parts, received)
     return middle, (x, queries, kv, lse, middle), [(a, near(a)) for a in (normed, mixed)], w_in
 
 
-def feed_forward(middle, w_feed, tables, hook):
-    features = middle.shape[1]
-    mask, here = tables[4:]
-    tokens, units = 4 * middle.shape[0], mask.shape[1]
-    normed = gathered(scaled(middle), "z")
-    normed = hook(4, normed)
-    activated, slope, *parts = call(
-        feed_kernel,
-        [shape((tokens, units), BF), shape((tokens, units), F32), *part_shapes(features)],
-        here, normed, mask, blocks=w_feed(),
-    )
-    parts[0] = hook(5, parts[0])
-    return parts, slope, [(a, near(a)) for a in (normed, activated)]
+def feed_gathered(middle, hook):
+    return jnp.concatenate(hook(4, gather_ring(scaled(middle), "z")), 0)
+
+
+def lefts_of(normed, activated):
+    return [(a, near(a)) for a in (normed, activated)]
+
+
+def feed_shapes(features, mask, *types):
+    return [shape((256, mask.shape[1]), t) for t in types] + part_shapes(features)
 
 
 def arrived(middle, parts, received):
@@ -410,35 +433,25 @@
     return straight + scale * (q - n * jnp.mean(q * n, -1, keepdims=True))
 
 
-def backward(grad_out, branch, kept, slope, lefts, weights, tables, hook):
+def backward(grad_out, branch, kept, feed_back, lefts, weights, tables, hook):
     x, queries, kv, lse, middle = kept
     normed, mixed, normed_two, activated = lefts
-    w_in, w_out, w_feed = weights
+    w_in, w_out = weights
     cos, sin, pos_here, pos_whole, unit_mask, here = tables
     tokens, width = queries.shape
     features = x.shape[1]
-    units = slope.shape[1]
-    branch = jnp.concatenate(hook(0, branch), 0)
     grad_out = grad_out.astype(F32)
-    grad_up, *parts = call(
-        feed_back_kernel,
-        [shape((tokens, units), BF), *part_shapes(features)],
-        here, branch, slope, blocks=w_feed,
-    )
+    grad_up, *parts = feed_back
     received = sent_home(parts)
-    branch_near, grad_up_near = near(branch), near(grad_up)
-    received = hook(1, received)
+    feed = weight_grads(
+        here,
+        [(*normed_two, grad_up, near(grad_up)), (*activated, branch, near(branch))],
+    )
+    received, feed = tied(received, feed)
+    received = hook(1, received, feed)
     grad_middle = norm_backward(middle, summed(parts, received), grad_out)
-    branch_low = grad_middle.astype(BF)
-    groups = (
-        (*normed_two, grad_up, grad_up_near),
-        (*activated, branch, branch_near),
-    )
-    groups, branch_low = tied(groups, branch_low)
-    ring = gather_ring(branch_low, "z")
-    feed = weight_grads(here, groups)
-    ring, feed = tied(ring, feed)
-    ring = hook(2, ring, feed)
+    ring = gather_ring(grad_middle.astype(BF), "z")
+    ring = hook(2, ring)
     branch = jnp.concatenate(ring, 0)
     dq, own, send, far = call(
         attend_back_kernel,
@@ -448,7 +461,7 @@
             shape((2 * tokens, 2 * width), BF),
             shape((tokens, 2 * width), F32),
         ],
-        here, branch, queries, kv, lse, pos_here, pos_whole, cos, sin, blocks=w_out,
+        here, branch, queries, kv, lse, pos_here, pos_whole, cos, sin, rows=width, blocks=w_out,
     )
     dq, own, send, far = hook(6, (dq, own, send, far))
     branch_near = near(branch)
@@ -459,15 +472,16 @@
     out = lax.dynamic_index_in_dim(out.reshape(2, 2, -1, features), here[0], 1, keepdims=False)
     out = out.reshape(2, 4, -1, features).transpose(1, 0, 2, 3)
     far, out = tied(far, out)
-    far = hook(3, far, out)
+    far = hook(3, far)
     grad_projected, *parts = call(
         project_back_kernel,
         [shape((tokens, 3 * width), BF), *part_shapes(features)],
-        here, dq, own, send, far, cos, sin, blocks=w_in,
+        here, dq, own, send, far, cos, sin, rows=features, blocks=w_in,
     )
     parts = hook(5, parts)
     received = sent_home(parts)
-    g_in = weight_grads(here, [(*normed, grad_projected, near(grad_projected))])
+    out = out.reshape(4, 2, -1, 3 * width)
+    g_in = weight_grads(here, [(*normed, grad_projected, near(grad_projected))], [out])
     received, g_in = tied(received, g_in)
     received = hook(4, received, g_in)
     return norm_backward(x, summed(parts, received), grad_middle).astype(BF)
@@ -515,19 +529,24 @@
     both = [w_in.reshape(4, rows, width_in // 4), w_up.reshape(4, rows, units // 4)]
     both = lax.all_to_all(jnp.concatenate(both, 2), "z", 0, 0, tiled=True)
     outs = lax.ppermute(attention_out[0], ("xh", "core", "y", "z"), home_route())
-    both, inputs, positions, outs = tied(both.reshape(4 * rows, -1), inputs, positions, outs)
-    in_0, in_1 = layer_pairs(both[:, : width_in // 4])
-    outs = jnp.stack(layer_pairs(outs))
+    streams = jnp.stack([inputs, cotangent], 1)
+    both, streams, positions, outs = tied(both.reshape(4 * rows, -1), streams, positions, outs)
+    attn = jnp.concatenate([both[:, : width_in // 4], outs.reshape(-1, width_in // 4)], 0)
+    attn_0, attn_1 = layer_pairs(attn)
+    streams = brought(streams)
     feed = jnp.concatenate([both[:, width_in // 4 :], feed_down[0]], 1)
-    x_0 = brought(inputs)
-    feed, in_0, in_1, outs, x_0 = tied(feed, in_0, in_1, outs, x_0)
-    in_0 = gather_ring(in_0, "y")
-    outs = y_gathered(outs).transpose(1, 2, 0, 3, 4).reshape(2, 2, 4 * rows, model)
+    attn_0, attn_1, (x_0, cotangent) = tied(attn_0, attn_1, streams)
+    attn_0 = y_gathered(attn_0)
     feed_0, feed_1 = layer_pairs(feed)
-    normed_0 = gather_ring(scaled(x_0.astype(F32)), "z")
-    in_0, feed_0, feed_1, normed_0 = tied(in_0, feed_0, feed_1, normed_0)
+    ring = gather_ring(jnp.stack([scaled(x_0.astype(F32)), cotangent]), "z")
+    feed_0, feed_1, ring = tied(feed_0, feed_1, ring)
+    normed_0, branch_1 = ([a[i] for a in ring] for i in (0, 1))
+    branch_1 = jnp.concatenate(branch_1, 0)
     feed_0 = y_gathered(feed_0)
-    outs = [with_near([a]) for a in outs]
+
+    def out_rows(attn):
+        out = attn[:, :, 4 * rows :].reshape(4, 2, rows, model)
+        return with_near([out.transpose(1, 0, 2, 3).reshape(2, 4 * rows, model)])
 
     y = lax.axis_index("y")
     seq = lambda a: lax.dynamic_index_in_dim(a, y, 0, keepdims=False)
@@ -553,8 +572,7 @@
         here,
     )
 
-    at = {"in_0": in_0, "in": in_1, "feed": feed_1, "cotangent": cotangent, "feed_0": feed_0}
-    at["outs"] = outs
+    at = {"attn_0": attn_0, "attn_1": attn_1, "feed_0": feed_0, "feed": feed_1}
 
     def hold(chain, *names):
         values = [at[n] for n in names]
@@ -564,110 +582,139 @@
 
     def forward_0(point, chain, *more):
         if point == 0:
-            chain = hold(chain, "in_0")
-            return with_near(at["in_0"]), chain
+            chain = hold(chain, "attn_0")
+            return with_near([at["attn_0"]]), chain
         if point == 1:
-            chain = hold(chain, "outs")
+            at["out_0"] = out_rows(at["attn_0"])
         if point == 2:
-            chain = hold(chain, "in", "feed")
-            at["in"], at["feed"] = y_gathered(at["in"]), y_gathered(at["feed"])
-        if point == 3:
-            chain = hold(chain, "cotangent", "feed_0")
+            chain = hold(chain, "attn_1", "feed", "out_0")
+            at["attn_1"], at["feed"] = y_gathered(at["attn_1"]), y_gathered(at["feed"])
+        if point == 7:
+            chain = hold(chain, "feed_0")
             at["feed_0"] = with_near([at["feed_0"]])
-            at["cotangent"] = brought(at["cotangent"])
-        if point == 5:
-            chain = hold(chain, "in", "cotangent")
-            at["in"] = with_near([at["in"]])
+        if point == 8:
+            chain = hold(chain, "attn_1")
+            at["in_1"] = with_near([at["attn_1"]])
         return chain
 
     def forward_1(point, chain, *more):
         if point == 0:
-            chain = hold(chain, "in")
-            return at["in"], chain
+            chain = hold(chain, "in_1")
+            return at["in_1"], chain
         if point == 1:
-            at["branch"] = gather_ring(at["cotangent"], "z")
+            at["out_1"] = out_rows(at["attn_1"])
+        if point == 2:
+            chain = hold(chain, "out_1")
         if point == 3:
-            chain = hold(chain, "branch", "feed")
+            chain = hold(chain, "feed")
             at["feed"] = with_near([at["feed"]])
         return chain
 
+    mask = tables[4]
     middle_0, kept_0, lefts_0, in_0 = attention(
-        x_0, normed_0, lambda: at["outs"][0], tables, forward_0
-    )
-    parts, slope_0, more = feed_forward(middle_0, lambda: at["feed_0"], tables, forward_0)
-    lefts_0 += more
-    hidden_0 = arrived(middle_0, parts, sent_home(parts))
+        x_0, normed_0, lambda: at["out_0"], tables, forward_0
+    )
+    normed = feed_gathered(middle_0, forward_0)
+    feed_0 = at["feed_0"]
+    activated, slope_0, *parts = call(
+        feed_kernel, feed_shapes(model, mask, BF, F32), here, normed, mask, rows=model, blocks=feed_0
+    )
+    lefts_0 += lefts_of(normed, activated)
+    hidden_0 = arrived(middle_0, parts, forward_0(8, sent_home(parts)))
     middle_1, kept_1, lefts_1, in_1 = attention(
-        hidden_0, gather_ring(scaled(hidden_0.astype(F32)), "z"), lambda: at["outs"][1], tables, forward_1
-    )
-    parts_1, slope_1, more = feed_forward(middle_1, lambda: at["feed"], tables, forward_1)
-    lefts_1 += more
-    feed_0, feed_1, cotangent = at["feed_0"], at["feed"], at["cotangent"]
-    out_0, out_1 = at["outs"]
+        hidden_0, gather_ring(scaled(hidden_0.astype(F32)), "z"), lambda: at["out_1"], tables, forward_1
+    )
+    normed = feed_gathered(middle_1, forward_1)
+    activated, grad_up, *parts = call(
+        feed_both_kernel,
+        feed_shapes(model, mask, BF, BF) + part_shapes(model),
+        here, normed, mask, branch_1, rows=model, blocks=at["feed"],
+    )
+    lefts_1 += lefts_of(normed, activated)
+    parts_1, feed_back_1 = parts[:4], [grad_up, *parts[4:]]
+    out_0, out_1 = at["out_0"], at["out_1"]
 
     def y_sum(grads):
         flat = grads.reshape(-1, grads.shape[-1])
         flat = lax.psum_scatter(flat, "y", scatter_dimension=0, tiled=True)
         return flat.reshape(grads.shape[1:])
 
-    def x_sum(zero, one):
-        both = jnp.concatenate([zero, one], 0)
-        both = lax.all_to_all(both, ("sec", "xh"), 0, 0, tiled=True)
-        return jnp.sum(both.astype(F32), 0)
+    def x_terms(blocks):
+        xh = here[2]
+        pick = lambda l, x: lax.dynamic_index_in_dim(
+            lax.dynamic_index_in_dim(blocks, l, 0, keepdims=False), x, 0, keepdims=False
+        )
+        places = [(a, x) for a in (0, 1) for x in (0, 1)]
+        across = [(2 * a + x, 2 * (1 - a) + 1 - x) for a, x in places]
+        return [
+            pick(sec, xh),
+            shifted(pick(sec, 1 - xh), "xh", 1),
+            shifted(pick(1 - sec, xh), "sec", 1),
+            lax.ppermute(pick(1 - sec, 1 - xh), ("sec", "xh"), across),
+        ]
+
+    def terms(blocks):
+        return sum(a.astype(F32) for a in blocks)
 
     at["parts"] = parts_1
 
     def backward_1(point, chain, *grads):
+        if point == 1:
+            at["feed1"] = y_sum(grads[0])
         if point == 2:
-            at["feed1"] = y_sum(grads[0])
             chain = hold(chain, "parts")
             at["received"] = sent_home(at["parts"])
-        if point == 6:
+        if point == 3:
             chain = hold(chain, "received")
-        if point == 3:
-            at["out1"] = y_sum(grads[0])
         if point == 4:
             chain = hold(chain, "feed1")
             at["in1"] = y_sum(grads[0])
         return chain
 
-    def attention_pair(grad_in, out):
-        return jnp.concatenate([grad_in, out.reshape(2, -1, width_in // 4)], 1)
-
     def backward_0(point, chain, *grads):
-        if point == 2:
-            chain = hold(chain, "out1", "in1")
+        if point == 1:
+            chain = hold(chain, "in1")
             at["feed0"] = y_sum(grads[0])
-        if point == 3:
-            at["out0"] = y_sum(grads[0])
         if point == 5:
             chain = hold(chain, "feed0")
+            feeds = jnp.stack([at["feed0"], at["feed1"]])
             at["up"], at["down"] = (
-                x_sum(at["feed0"][:, a : a + 4 * rows], at["feed1"][:, a : a + 4 * rows])
-                for a in (0, 4 * rows)
+                x_terms(feeds[:, :, a : a + 4 * rows]) for a in (0, 4 * rows)
             )
         if point == 4:
             at["in0"] = y_sum(grads[0])
         return chain
 
     grad_1 = backward(
-        cotangent, at["branch"], kept_1, slope_1, lefts_1,
-        (in_1, out_1, feed_1), tables, backward_1,
-    )
-    at["to_1"] = jnp.stack([arrived(middle_1, at["parts"], at["received"]), grad_1])
+        cotangent, branch_1, kept_1, feed_back_1, lefts_1, (in_1, out_1), tables, backward_1
+    )
+    hidden_1 = arrived(middle_1, at["parts"], at["received"])
+    branch_0 = gathered(grad_1, "z")
+    feed_back_0 = call(
+        feed_back_kernel, feed_shapes(model, mask, BF), here, branch_0, slope_0, rows=model, blocks=feed_0
+    )
     grad_0 = backward(
-        grad_1, gather_ring(grad_1, "z"), kept_0, slope_0, lefts_0,
-        (in_0, out_0, feed_0), tables, backward_0,
+        grad_1, branch_0, kept_0, feed_back_0, lefts_0, (in_0, out_0), tables, backward_0
     )
     def columns_home(block):
-        block = block.astype(BF).reshape(4, rows, -1)
-        return lax.all_to_all(block, "z", 0, 0, tiled=True).astype(F32)
-
-    to_0, to_1 = returned(jnp.stack([hidden_0, grad_0]), 0), returned(at["to_1"], 1)
+        z = lax.axis_index("z")
+        pick = lambda k: lax.dynamic_index_in_dim(block, lax.rem(z + k, 4), 0, keepdims=False)
+        got = [pick(0)] + [shifted(pick(k), "z", k) for k in (1, 2, 3)]
+        return rolled(jnp.stack(got), "z", 0)
+
+    g_up, g_down = terms(at["up"]), terms(at["down"])
+    g_up = columns_home(g_up.astype(BF).reshape(4, rows, -1)).astype(F32)
+    g_in, g_out = (
+        jnp.stack([at[n][:, rows_of] for n in ("in0", "in1")])
+        for rows_of in (slice(0, 4 * rows), slice(4 * rows, None))
+    )
+    g_in = lax.all_to_all(g_in.reshape(16, rows, -1), ("sec", "xh", "z"), 0, 0, tiled=True)
+    g_out = terms(x_terms(g_out.reshape(2, 2, rows, model)))
+    g_in, grad_0 = tied(g_in, grad_0)
+    g_in = jnp.sum(g_in.reshape(4, 4, rows, -1).astype(F32), 0)
+    to_0 = returned(jnp.stack([hidden_0, grad_0]), 0)
+    to_1 = returned(jnp.stack([hidden_1, grad_1]), 1)
     hidden, input_grads = (jnp.where(sec == 0, a, b)[None] for a, b in zip(to_0, to_1))
-    g_up, g_down = columns_home(at["up"]), at["down"]
-    attn = x_sum(attention_pair(at["in0"], at["out0"]), attention_pair(at["in1"], at["out1"]))
-    g_in, g_out = columns_home(attn[: 4 * rows]), attn[4 * rows :].reshape(rows, model)
     g_in = g_in.reshape(4, rows, 3, width_in // 12).transpose(1, 2, 0, 3).reshape(rows, width_in)
     g_up = g_up.reshape(4, rows, 16, units // 64).transpose(1, 2, 0, 3).reshape(rows, units)
     back = [(b, a) for a, b in home_route()]

time: 619 us -> 563 us (0.910)
  the two profiles are of different devices: /device:TPU:0 before, /device:TPU:1 now
where the time goes in v3:
time: 563 us; the launch traced here: 553 us
  waiting for transfers between devices  193 us (34%)
  starting transfers between devices  156 us (28%)
  Pallas kernels  105 us (19%)
  other arithmetic  45.9 us (8%)
  local copies, waits for them, and re-layouts  35.9 us (6%)
  between operations  16.8 us (3%)
    ppermute x91, waiting for transfers between devices, shifted(): lax.ppermute(block, axis, [(i, (i + distance) % n) for i in range(n)])  151 us
    ppermute x91, starting transfers between devices, shifted(): lax.ppermute(block, axis, [(i, (i + distance) % n) for i in range(n)])  105 us
    pallas_call x11, Pallas kernels, call(): pl.pallas_call(kernel, out_shape=out_shape, in_specs=[SMEM] + [VMEM] * le...  80.4 us
    pallas_call x4, Pallas kernels, weight_grads(): pl.pallas_call(weight_grad_kernel, grid_spec=pltpu.PrefetchScalarGridSpec...  24.2 us
    unnamed x166, local copies, waits for them, and re-layouts  14.9 us
    all_gather x4, waiting for transfers between devices, y_gathered(): return lax.all_gather(pair, 'y', axis=0, tiled=False)  13.4 us
  transfers between devices with their start and end apart: 114, of which 50 were waited for; matrix products, arithmetic and copies ran while one was open for 11% of the time, Pallas kernels for 19%

profile of v3, /device:TPU:1, one launch (start us, length us, event | category | flops | bytes accessed | tf_op | source)
XLA Modules:
  0.0 553.3 jit_solution(16645870168742960309)
XLA Ops:
  32.1 8.9 %collective-permute-start.4 = (bf16[2,64,1536]{2,1,0:T(8,128)(2,1)S(1)}, bf16[2,64,1536]{2,1,0:T(8,128)(2,1)S(1)}, u32[]{:S(2)}, u32[]{:S(2)}) collective-permute-start(bf16[2,64,1536]{2,1,0:T(8,128)(2,1)S(1)} %get-tuple-element.360), channel_id=1, source_target_pairs={{0,0},{4,16},{72,64},{76,80},{16,8},{20,24},{88,72},{92,88},{1,1},... | collective-permute-start | bytes 1179656 | tf_op jit(solution)/shard_map/ppermute | solution.py:67
  59.9 7.6 %collective-permute-done.6 = bf16[96,3072]{1,0:T(8,128)(2,1)S(1)} collective-permute-done((bf16[96,3072]{1,0:T(8,128)(2,1)S(1)}, bf16[96,3072]{1,0:T(8,128)(2,1)S(1)}, u32[]{:S(2)}, u32[]{:S(2)}) %collective-permute-start.6) | collective-permute-done | bytes 589856 | tf_op jit(solution)/shard_map/ppermute | solution.py:23
  67.7 11.6 %collective-permute-done.7 = bf16[96,3072]{1,0:T(8,128)(2,1)S(1)} collective-permute-done((bf16[96,3072]{1,0:T(8,128)(2,1)S(1)}, bf16[96,3072]{1,0:T(8,128)(2,1)S(1)}, u32[]{:S(2)}, u32[]{:S(2)}) %collective-permute-start.7) | collective-permute-done | bytes 589856 | tf_op jit(solution)/shard_map/ppermute | solution.py:23
  99.8 7.7 %collective-permute-done.15 = bf16[256,768]{1,0:T(8,128)(2,1)S(1)} collective-permute-done((bf16[256,768]{1,0:T(8,128)(2,1)}, bf16[256,768]{1,0:T(8,128)(2,1)S(1)}, u32[]{:S(2)}, u32[]{:S(2)}) %collective-permute-start.15) | collective-permute-done | bytes 393248 | tf_op jit(solution)/shard_map/ppermute | solution.py:23
  125.6 6.3 %collective-permute-done.18 = bf16[64,1536]{1,0:T(8,128)(2,1)S(1)} collective-permute-done((bf16[64,1536]{1,0:T(8,128)(2,1)}, bf16[64,1536]{1,0:T(8,128)(2,1)S(1)}, u32[]{:S(2)}, u32[]{:S(2)}) %collective-permute-start.18) | collective-permute-done | bytes 196640 | tf_op jit(solution)/shard_map/ppermute | solution.py:23
  155.6 8.5 %shard_map.163 = (bf16[256,1536]{1,0:T(8,128)(2,1)}, f32[256,1536]{1,0:T(8,128)}, f32[64,1536]{1,0:T(8,128)}, bf16[64,1536]{1,0:T(8,128)(2,1)}, bf16[64,1536]{1,0:T(8,128)(2,1)}, /*index=5*/bf16[64,1536]{1,0:T(8,128)(2,1)}) custom-call(s32[4]{0:T(128)} %pad_add_fusion.3.here_ref, bf16[256,1536]{1,0:T(8,128)(2,1)} %pad_maximum_fusion.6.n_ref.refs_0_, ...), custom_call_target="tpu_custom_call" | custom-call | flops 1 | bytes 1 | tf_op jit(solution)/shard_map/pallas_call | solution.py:118
  167.0 6.8 %all-gather.13.cloned.1.call-done = bf16[8,128,1152]{2,1,0:T(8,128)(2,1)} async-done(((bf16[2,128,1152]{2,1,0:T(8,128)(2,1)}), bf16[8,128,1152]{2,1,0:T(8,128)(2,1)}) %all-gather.13.cloned.1.call-update) | async-done | bytes 2359312 | tf_op jit(solution)/shard_map/all_gather | solution.py:381
  183.7 9.2 %collective-permute-done.28 = bf16[64,1536]{1,0:T(8,128)(2,1)S(1)} collective-permute-done((bf16[64,1536]{1,0:T(8,128)(2,1)S(1)}, bf16[64,1536]{1,0:T(8,128)(2,1)S(1)}, u32[]{:S(2)}, u32[]{:S(2)}) %collective-permute-start.28) | collective-permute-done | bytes 196640 | tf_op jit(solution)/shard_map/ppermute | solution.py:23
  232.5 7.7 %collective-permute-done.36 = bf16[64,1536]{1,0:T(8,128)(2,1)S(1)} collective-permute-done((bf16[64,1536]{1,0:T(8,128)(2,1)}, bf16[64,1536]{1,0:T(8,128)(2,1)S(1)}, u32[]{:S(2)}, u32[]{:S(2)}) %collective-permute-start.36) | collective-permute-done | bytes 196640 | tf_op jit(solution)/shard_map/ppermute | solution.py:23
  249.5 7.5 %collective-permute-done.39 = bf16[64,1536]{1,0:T(8,128)(2,1)S(1)} collective-permute-done((bf16[64,1536]{1,0:T(8,128)(2,1)S(1)}, bf16[64,1536]{1,0:T(8,128)(2,1)S(1)}, u32[]{:S(2)}, u32[]{:S(2)}) %collective-permute-start.39) | collective-permute-done | bytes 196640 | tf_op jit(solution)/shard_map/ppermute | solution.py:23
  259.3 12.3 %shard_map.166 = (bf16[256,1536]{1,0:T(8,128)(2,1)}, bf16[256,1536]{1,0:T(8,128)(2,1)}, f32[64,1536]{1,0:T(8,128)}, bf16[64,1536]{1,0:T(8,128)(2,1)}, bf16[64,15...) custom-call(s32[4]{0:T(128)} %pad_add_fusion.3.here_ref, ...), custom_call_target="tpu_custom_call" | custom-call | flops 1 | bytes 1 | tf_op jit(solution)/shard_map/pallas_call | solution.py:118
  276.9 7.3 %shard_map.167 = bf16[4,2,192,1536]{3,2,1,0:T(8,128)(2,1)} custom-call(s32[4]{0:T(128)} %pad_add_fusion.3.here_ref, bf16[256,1536]{1,0:T(8,128)(2,1)} %copy-done.9, bf16[256,1536]{1,0:T(8,128)(2,1)} %copy-done.45, bf16[256,1536]{1,0:T(8,128)(2,1)} %get-tuple-element.220.refs_2_, bf16[256,1536]{1,0:T(8,128)(2,1)} %copy-done.46, ...), custom_call_target="tpu_custom_call" | custom-call | flops 1 | bytes 1 | tf_op jit(solution)/shard_map/pallas_call | solution.py:349
  292.0 8.6 %collective-permute-done.50 = bf16[64,1536]{1,0:T(8,128)(2,1)S(1)} collective-permute-done((bf16[64,1536]{1,0:T(8,128)(2,1)S(1)}, bf16[64,1536]{1,0:T(8,128)(2,1)S(1)}, u32[]{:S(2)}, u32[]{:S(2)}) %collective-permute-start.50) | collective-permute-done | bytes 196640 | tf_op jit(solution)/shard_map/ppermute | solution.py:23
  301.8 8.4 %shard_map.168 = (bf16[256,384]{1,0:T(8,128)(2,1)}, f32[256,768]{1,0:T(8,128)}, bf16[512,768]{1,0:T(8,128)(2,1)}, f32[256,768]{1,0:T(8,128)}) custom-call(s32[4]{0:T(128)} %pad_add_fusion.3.here_ref, bf16[256,1536]{1,0:T(8,128)(2,1)} %copy-done.29, bf16[256,384]{1,0:T(8,128)(2,1)} %get-tuple-element.201.q_ref, bf16[1024,768]{1,0:T(8,128)(2,1)} %pad_maximum_fusion.1.kv_ref, ...), custom_call_target="tpu_custom_call" | custom-call | flops 1 | bytes 1 | tf_op jit(solution)/shard_map/pallas_call | solution.py:118
  321.8 7.7 %collective-permute-done.54.far_ref = bf16[256,768]{1,0:T(8,128)(2,1)S(1)} collective-permute-done((bf16[256,768]{1,0:T(8,128)(2,1)S(1)}, bf16[256,768]{1,0:T(8,128)(2,1)S(1)}, u32[]{:S(2)}, u32[]{:S(2)}) %collective-permute-start.54) | collective-permute-done | bytes 393248 | tf_op jit(solution)/shard_map/ppermute | solution.py:23
  330.3 6.2 %shard_map.169 = (bf16[256,1152]{1,0:T(8,128)(2,1)}, f32[64,1536]{1,0:T(8,128)}, bf16[64,1536]{1,0:T(8,128)(2,1)}, bf16[64,1536]{1,0:T(8,128)(2,1)}, bf16[64,1536]{1,0:T(8,128)(2,1)}) custom-call(s32[4]{0:T(128)} %pad_add_fusion.3.here_ref, bf16[256,384]{1,0:T(8,128)(2,1)} %get-tuple-element.234.dq_ref, f32[256,768]{1,0:T(8,128)} %get-tuple-element.235.own_ref, ...), custom_call_target="tpu_custom_call" | custom-call | flops 1 | bytes 1 | tf_op jit(solution)/shard_map/pallas_call | solution.py:118
  359.9 6.4 %collective-permute-done.65 = bf16[64,1536]{1,0:T(8,128)(2,1)S(1)} collective-permute-done((bf16[64,1536]{1,0:T(8,128)(2,1)S(1)}, bf16[64,1536]{1,0:T(8,128)(2,1)S(1)}, u32[]{:S(2)}, u32[]{:S(2)}) %collective-permute-start.65) | collective-permute-done | bytes 196640 | tf_op jit(solution)/shard_map/ppermute | solution.py:23
  367.6 8.2 %shard_map.171 = (bf16[256,1536]{1,0:T(8,128)(2,1)}, f32[64,1536]{1,0:T(8,128)}, bf16[64,1536]{1,0:T(8,128)(2,1)}, bf16[64,1536]{1,0:T(8,128)(2,1)}, bf16[64,1536]{1,0:T(8,128)(2,1)}) custom-call(s32[4]{0:T(128)} %pad_add_fusion.3.here_ref, bf16[256,1536]{1,0:T(8,128)(2,1)} %pad_maximum_fusion.9.b_ref.refs_6_, f32[256,1536]{1,0:T(8,128)} %get-tuple-element.257.slope_ref, ...), custom_call_target="tpu_custom_call" | custom-call | flops 1 | bytes 1 | tf_op jit(solution)/shard_map/pallas_call | solution.py:118
  382.3 7.3 %shard_map.172 = bf16[4,2,192,1536]{3,2,1,0:T(8,128)(2,1)} custom-call(s32[4]{0:T(128)} %pad_add_fusion.3.here_ref, bf16[256,1536]{1,0:T(8,128)(2,1)} %pad_maximum_fusion.6.n_ref.refs_0_, bf16[256,1536]{1,0:T(8,128)(2,1)} %copy-done.43, bf16[256,1536]{1,0:T(8,128)(2,1)} %get-tuple-element.262.refs_2_, bf16[256,1536]{1,0:T(8,128)(2,1)} %copy-done.47, ...), custom_call_target="tpu_custom_call" | custom-call | flops 1 | bytes 1 | tf_op jit(solution)/shard_map/pallas_call | solution.py:349
  400.8 8.0 %collective-permute-done.75 = bf16[64,1536]{1,0:T(8,128)(2,1)S(1)} collective-permute-done((bf16[64,1536]{1,0:T(8,128)(2,1)S(1)}, bf16[64,1536]{1,0:T(8,128)(2,1)S(1)}, u32[]{:S(2)}, u32[]{:S(2)}) %collective-permute-start.75) | collective-permute-done | bytes 196640 | tf_op jit(solution)/shard_map/ppermute | solution.py:23
  409.8 8.5 %shard_map.173 = (bf16[256,384]{1,0:T(8,128)(2,1)}, f32[256,768]{1,0:T(8,128)}, bf16[512,768]{1,0:T(8,128)(2,1)}, f32[256,768]{1,0:T(8,128)}) custom-call(s32[4]{0:T(128)} %pad_add_fusion.3.here_ref, bf16[256,1536]{1,0:T(8,128)(2,1)} %pad_maximum_fusion.10.b_ref, bf16[256,384]{1,0:T(8,128)(2,1)} %get-tuple-element.170.q_ref, ...), custom_call_target="tpu_custom_call" | custom-call | flops 1 | bytes 1 | tf_op jit(solution)/shard_map/pallas_call | solution.py:118
  424.4 8.3 %collective-permute-done.79.far_ref = bf16[256,768]{1,0:T(8,128)(2,1)S(1)} collective-permute-done((bf16[256,768]{1,0:T(8,128)(2,1)S(1)}, bf16[256,768]{1,0:T(8,128)(2,1)S(1)}, u32[]{:S(2)}, u32[]{:S(2)}) %collective-permute-start.79) | collective-permute-done | bytes 393248 | tf_op jit(solution)/shard_map/ppermute | solution.py:23
  519.4 7.3 %collective-permute-done.94 = bf16[24,1536]{1,0:T(8,128)(2,1)S(1)} collective-permute-done((bf16[24,1536]{1,0:T(8,128)(2,1)S(1)}, bf16[24,1536]{1,0:T(8,128)(2,1)S(1)}, u32[]{:S(2)}, u32[]{:S(2)}) %collective-permute-start.94) | collective-permute-done | bytes 73760 | tf_op jit(solution)/shard_map/ppermute | solution.py:721
  533.0 8.7 %collective-permute-done.87 = bf16[2,64,1536]{2,1,0:T(8,128)(2,1)S(1)} collective-permute-done((bf16[2,64,1536]{2,1,0:T(8,128)(2,1)S(1)}, bf16[2,64,1536]{2,1,0:T(8,128)(2,1)S(1)}, u32[]{:S(2)}, u32[]{:S(2)}) %collective-permute-start.87) | collective-permute-done | bytes 393248 | tf_op jit(solution)/shard_map/ppermute | solution.py:80
  (525 shorter events, 341.4 us)
Async XLA Ops:
  17.6 66.9 %all-gather.9.cloned.1.call-start = ((), (), s32[]{:S(2)}) async-start(), calls=%async_computation.10 | async-start | bytes 2949120 | tf_op jit(solution)/shard_map/all_gather | solution.py:381
  32.1 17.4 %collective-permute-start.4 = (bf16[2,64,1536]{2,1,0:T(8,128)(2,1)S(1)}, bf16[2,64,1536]{2,1,0:T(8,128)(2,1)S(1)}, u32[]{:S(2)}, u32[]{:S(2)}) collective-permute-start(bf16[2,64,1536]{2,1,0:T(8,128)(2,1)S(1)} %get-tuple-element.360), channel_id=1, source_target_pairs={{0,0},{4,16},{72,64},{76,80},{16,8},{20,24},{88,72},{92,88},{1,1},... | collective-permute-start | bytes 1179656 | tf_op jit(solution)/shard_map/ppermute | solution.py:67
  50.5 87.7 %all-gather.11.cloned.1.call-start = ((), (), s32[]{:S(2)}) async-start(), calls=%async_computation.11 | async-start | bytes 5898240 | tf_op jit(solution)/shard_map/all_gather | solution.py:381
  52.7 26.6 %collective-permute-start.7 = (bf16[96,3072]{1,0:T(8,128)(2,1)S(1)}, bf16[96,3072]{1,0:T(8,128)(2,1)S(1)}, u32[]{:S(2)}, u32[]{:S(2)}) collective-permute-start(bf16[96,3072]{1,0:T(8,128)(2,1)S(1)} %get-tuple-element.362), channel_id=1, source_target_pairs={{0,64},{64,0},{1,65},{65,1},{2,66},{66,2},{3,67},{67,3},{4,68},{68... | collective-permute-start | bytes 1769480 | tf_op jit(solution)/shard_map/ppermute | solution.py:23
  52.9 26.9 %collective-permute-start.8 = (bf16[96,3072]{1,0:T(8,128)(2,1)S(1)}, bf16[96,3072]{1,0:T(8,128)(2,1)S(1)}, u32[]{:S(2)}, u32[]{:S(2)}) collective-permute-start(bf16[96,3072]{1,0:T(8,128)(2,1)S(1)} %get-tuple-element.362), channel_id=1, source_target_pairs={{0,96},{32,64},{64,32},{96,0},{1,97},{33,65},{65,33},{97,1},{2,98}... | collective-permute-start | bytes 1769480 | tf_op jit(solution)/shard_map/ppermute | solution.py:376
  54.4 27.1 %collective-permute-start.10 = (bf16[2,64,1536]{2,1,0:T(8,128)(2,1)S(1)}, bf16[2,64,1536]{2,1,0:T(8,128)(2,1)S(1)}, u32[]{:S(2)}, u32[]{:S(2)}) collective-permute-start(bf16[2,64,1536]{2,1,0:T(8,128)(2,1)S(1)} %pad_maximum_fusion.17), channel_id=1, source_target_pairs={{0,2},{1,3},{2,0},{3,1},{4,6},{5,7},{6,4},{7,5},{8,10},{9,11},{10,... | collective-permute-start | bytes 1179656 | tf_op jit(solution)/shard_map/ppermute | solution.py:23
  59.9 21.6 %collective-permute-start.11 = (bf16[2,64,1536]{2,1,0:T(8,128)(2,1)S(1)}, bf16[2,64,1536]{2,1,0:T(8,128)(2,1)S(1)}, u32[]{:S(2)}, u32[]{:S(2)}) collective-permute-start(bf16[2,64,1536]{2,1,0:T(8,128)(2,1)S(1)} %pad_maximum_fusion.17), channel_id=1, source_target_pairs={{0,3},{1,0},{2,1},{3,2},{4,7},{5,4},{6,5},{7,6},{8,11},{9,8},{10,9... | collective-permute-start | bytes 1179656 | tf_op jit(solution)/shard_map/ppermute | solution.py:23
  81.6 92.3 %all-gather.13.cloned.1.call-start = ((), (), s32[]{:S(2)}) async-start(), calls=%async_computation.12 | async-start | bytes 2949120 | tf_op jit(solution)/shard_map/all_gather | solution.py:381
  111.0 117.1 %all-gather.15.cloned.1.call-start = ((), (), s32[]{:S(2)}) async-start(), calls=%async_computation.13 | async-start | bytes 5898240 | tf_op jit(solution)/shard_map/all_gather | solution.py:381
  138.1 17.5 %collective-permute-start.24 = (bf16[4,2,96,3072]{3,2,1,0:T(8,128)(2,1)}, bf16[4,2,96,3072]{3,2,1,0:T(8,128)(2,1)}, u32[]{:S(2)}, u32[]{:S(2)}) collective-permute-start(bf16[4,2,96,3072]{3,2,1,0:T(8,128)(2,1)} %bitcast.202), channel_id=1, source_target_pairs={{0,16},{16,0},{1,17},{17,1},{2,18},{18,2},{3,19},{19,3},{4,20},{20... | collective-permute-start | bytes 14155784 | tf_op jit(solution)/shard_map/ppermute | solution.py:23
  138.8 213.2 %reduce-scatter.5.cloned.1.call-start = ((), (), s32[]{:S(2)}) async-start(), calls=%async_computation.6 | async-start | bytes 5898240 | tf_op jit(solution)/shard_map/reduce_scatter | solution.py:639
  228.1 31.2 %collective-permute-start.42 = (bf16[4,2,96,3072]{3,2,1,0:T(8,128)(2,1)}, bf16[4,2,96,3072]{3,2,1,0:T(8,128)(2,1)}, u32[]{:S(2)}, u32[]{:S(2)}) collective-permute-start(bf16[4,2,96,3072]{3,2,1,0:T(8,128)(2,1)} %bitcast.228), channel_id=1, source_target_pairs={{0,16},{16,0},{1,17},{17,1},{2,18},{18,2},{3,19},{19,3},{4,20},{20... | collective-permute-start | bytes 14155784 | tf_op jit(solution)/shard_map/ppermute | solution.py:23
  248.3 26.1 %collective-permute-start.49 = (bf16[256,1536]{1,0:T(8,128)(2,1)S(1)}, bf16[256,1536]{1,0:T(8,128)(2,1)S(1)}, u32[]{:S(2)}, u32[]{:S(2)}) collective-permute-start(bf16[256,1536]{1,0:T(8,128)(2,1)S(1)} %pad_maximum_fusion.8.b_ref.refs_6_), channel_id=1, source_target_pairs={{0,16},{16,0},{1,17},{17,1},{2,18},{18,2},{3,19},{19,3},{4,20},{20... | collective-permute-start | bytes 2359304 | tf_op jit(solution)/shard_map/ppermute | solution.py:23
  286.8 106.3 %reduce-scatter.7.cloned.1.call-start = ((), (), s32[]{:S(2)}) async-start(), calls=%async_computation.7 | async-start | bytes 2949120 | tf_op jit(solution)/shard_map/reduce_scatter | solution.py:639
  311.9 32.2 %collective-permute-start.63 = (bf16[256,1536]{1,0:T(8,128)(2,1)S(1)}, bf16[256,1536]{1,0:T(8,128)(2,1)}, u32[]{:S(2)}, u32[]{:S(2)}) collective-permute-start(bf16[256,1536]{1,0:T(8,128)(2,1)S(1)} %copy-done.17), channel_id=1, source_target_pairs={{0,16},{16,0},{1,17},{17,1},{2,18},{18,2},{3,19},{19,3},{4,20},{20... | collective-permute-start | bytes 2359304 | tf_op jit(solution)/shard_map/ppermute | solution.py:23
  352.0 89.7 %reduce-scatter.9.cloned.1.call-start = ((), (), s32[]{:S(2)}) async-start(), calls=%async_computation.8 | async-start | bytes 5898240 | tf_op jit(solution)/shard_map/reduce_scatter | solution.py:639
  358.3 21.5 %collective-permute-start.71 = (bf16[256,1536]{1,0:T(8,128)(2,1)S(1)}, bf16[256,1536]{1,0:T(8,128)(2,1)S(1)}, u32[]{:S(2)}, u32[]{:S(2)}) collective-permute-start(bf16[256,1536]{1,0:T(8,128)(2,1)S(1)} %copy-done.11), channel_id=1, source_target_pairs={{0,16},{16,0},{1,17},{17,1},{2,18},{18,2},{3,19},{19,3},{4,20},{20... | collective-permute-start | bytes 2359304 | tf_op jit(solution)/shard_map/ppermute | solution.py:23
  359.8 20.3 %collective-permute-start.73 = (bf16[256,1536]{1,0:T(8,128)(2,1)S(1)}, bf16[256,1536]{1,0:T(8,128)(2,1)S(1)}, u32[]{:S(2)}, u32[]{:S(2)}) collective-permute-start(bf16[256,1536]{1,0:T(8,128)(2,1)S(1)} %copy-done.41), channel_id=1, source_target_pairs={{0,16},{16,0},{1,17},{17,1},{2,18},{18,2},{3,19},{19,3},{4,20},{20... | collective-permute-start | bytes 2359304 | tf_op jit(solution)/shard_map/ppermute | solution.py:23
  393.2 104.5 %reduce-scatter.11.cloned.1.call-start = ((), (), s32[]{:S(2)}) async-start(), calls=%async_computation.9 | async-start | bytes 2949120 | tf_op jit(solution)/shard_map/reduce_scatter | solution.py:639
  399.7 48.0 %collective-permute-start.85 = (bf16[256,1536]{1,0:T(8,128)(2,1)S(1)}, bf16[256,1536]{1,0:T(8,128)(2,1)}, u32[]{:S(2)}, u32[]{:S(2)}) collective-permute-start(bf16[256,1536]{1,0:T(8,128)(2,1)S(1)} %copy-done.15), channel_id=1, source_target_pairs={{0,16},{16,0},{1,17},{17,1},{2,18},{18,2},{3,19},{19,3},{4,20},{20... | collective-permute-start | bytes 2359304 | tf_op jit(solution)/shard_map/ppermute | solution.py:23
  400.8 22.7 %collective-permute-start.80 = (bf16[256,384]{1,0:T(8,128)(2,1)}, bf16[256,384]{1,0:T(8,128)(2,1)S(1)}, u32[]{:S(2)}, u32[]{:S(2)}) collective-permute-start(bf16[256,384]{1,0:T(8,128)(2,1)} %get-tuple-element.276), channel_id=1, source_target_pairs={{0,16},{16,0},{1,17},{17,1},{2,18},{18,2},{3,19},{19,3},{4,20},{20... | collective-permute-start | bytes 589832 | tf_op jit(solution)/shard_map/ppermute | solution.py:23
  447.7 85.2 %collective-permute-start.89 = (bf16[2,64,1536]{2,1,0:T(8,128)(2,1)}, bf16[2,64,1536]{2,1,0:T(8,128)(2,1)}, u32[]{:S(2)}, u32[]{:S(2)}) collective-permute-start(bf16[2,64,1536]{2,1,0:T(8,128)(2,1)} %pad_maximum_fusion.19), channel_id=1, source_target_pairs={{0,64},{8,80},{16,68},{24,84},{64,72},{72,88},{80,76},{88,92},{1,6... | collective-permute-start | bytes 1179656 | tf_op jit(solution)/shard_map/ppermute | solution.py:80
  452.6 80.4 %collective-permute-start.90 = (bf16[2,64,1536]{2,1,0:T(8,128)(2,1)}, bf16[2,64,1536]{2,1,0:T(8,128)(2,1)}, u32[]{:S(2)}, u32[]{:S(2)}) collective-permute-start(bf16[2,64,1536]{2,1,0:T(8,128)(2,1)} %pad_maximum_fusion.19), channel_id=1, source_target_pairs={{4,64},{12,80},{20,68},{28,84},{68,72},{76,88},{84,76},{92,92},{5,... | collective-permute-start | bytes 1179656 | tf_op jit(solution)/shard_map/ppermute | solution.py:80
  505.8 21.6 %all-to-all-start.1 = ((bf16[16,24,1152]{2,1,0:T(8,128)(2,1)}), bf16[16,24,1152]{2,1,0:T(8,128)(2,1)S(1)}, u32[]{:S(2)}, u32[]{:S(2)}) async-start(bf16[16,24,1152]{2,1,0:T(8,128)(2,1)} %bitcast.60), calls=%async_computation.5 | async-start | bytes 1769472 | tf_op jit(solution)/shard_map/all_to_all | solution.py:711
  (166 other events, 1405.5 us)
Sparse Core Ops, SparseCore 0:
  50.6 33.1 all-gather.8
  85.4 52.6 all-gather.10
  140.4 33.4 all-gather.12
  175.3 52.6 all-gather.14
  287.0 49.2 reduce-scatter.4
  352.1 30.5 reduce-scatter.6
  392.7 48.9 reduce-scatter.8
  459.0 32.7 reduce-scatter.10

commit v4 on v3

--- a/solution.py
+++ b/solution.py
@@ -49,7 +49,7 @@
 def family(block):
     near = shifted(block, "core", 1)
     far = shifted(block, "sec", 1)
-    return jnp.concatenate([block, near, far, shifted(far, "core", 1)], 0)
+    return [block, near, far, shifted(far, "core", 1)]
 
 
 def place(sec, core, y):
@@ -114,13 +114,13 @@
 LIGHT = pl.CostEstimate(flops=1, bytes_accessed=1, transcendentals=0)
 
 
-def call(kernel, out_shape, here, *args, rows, blocks):
+def call(kernel, out_shape, here, *args, rows, blocks, scratch=()):
     return pl.pallas_call(
         kernel,
         out_shape=out_shape,
         in_specs=[SMEM] + [VMEM] * len(args) + [pl.BlockSpec(memory_space=pl.ANY)] * len(blocks),
         out_specs=[VMEM] * len(out_shape),
-        scratch_shapes=fetch_scratch(rows, blocks),
+        scratch_shapes=[*scratch, *fetch_scratch(rows, blocks)],
         compiler_params=pltpu.CompilerParams(vmem_limit_bytes=56 * 2**20),
         cost_estimate=LIGHT,
     )(here, *args, *blocks)
@@ -148,6 +148,12 @@
 
 def sent_home(parts):
     return [shifted(parts[k], "z", -k) for k in range(1, 4)]
+
+
+def stacked(refs, whole):
+    rows = refs[0].shape[0]
+    for k, ref in enumerate(refs):
+        whole[rows * k : rows * (k + 1)] = ref[...]
 
 
 def swap_halves(v):
@@ -186,9 +192,11 @@
     return [pltpu.VMEM((rows, blocks[0].shape[-1]), BF), pltpu.SemaphoreType.DMA((32,))]
 
 
-def qkv_kernel(here_ref, n_ref, cos_ref, sin_ref, *refs):
-    *refs, q_ref, kv_ref, whole, sems = refs
-    fetched(fetches(here_ref, refs, whole, sems))
+def qkv_kernel(here_ref, n0, n1, n2, n3, cos_ref, sin_ref, *refs):
+    *refs, n_ref, q_ref, kv_ref, whole, sems = refs
+    copies = fetches(here_ref, refs, whole, sems)
+    stacked((n0, n1, n2, n3), n_ref)
+    fetched(copies)
     width = q_ref.shape[1]
     cos, sin = cos_ref[...], sin_ref[...]
     for j in (0, 1, 2):
@@ -206,10 +214,12 @@
 
 
 def attend_kernel(
-    here_ref, q_ref, kv_ref, pq_ref, pk_ref, mine_ref, other_ref, mixed_ref, lse_ref, *refs
+    here_ref, q_ref, kv0, kv1, kv2, kv3, pq_ref, pk_ref, mine_ref, other_ref, mixed_ref, lse_ref,
+    *refs,
 ):
-    *part_refs, whole, sems = refs
+    *part_refs, kv_ref, whole, sems = refs
     copies = fetches(here_ref, (mine_ref, other_ref), whole, sems)
+    stacked((kv0, kv1, kv2, kv3), kv_ref)
     width = q_ref.shape[1]
     visible = pk_ref[...] <= pq_ref[...]
     for i in range(width // HEAD):
@@ -227,10 +237,13 @@
 
 
 def attend_back_kernel(
-    here_ref, b_ref, q_ref, kv_ref, lse_ref, pq_ref, pk_ref, cos_ref, sin_ref, mine_ref, other_ref,
-    dq_ref, own_ref, send_ref, far_ref, whole, sems,
+    here_ref, b0, b1, b2, b3, q_ref, kv0, kv1, kv2, kv3, lse_ref, pq_ref, pk_ref, cos_ref, sin_ref,
+    mine_ref, other_ref, b_ref, dq_ref, own_ref, send_ref, far_ref, kv_ref, whole, sems,
 ):
-    fetched(fetches(here_ref, (mine_ref, other_ref), whole, sems))
+    copies = fetches(here_ref, (mine_ref, other_ref), whole, sems)
+    stacked((b0, b1, b2, b3), b_ref)
+    stacked((kv0, kv1, kv2, kv3), kv_ref)
+    fetched(copies)
     tokens, width = q_ref.shape
     scale = 1.0 / math.sqrt(HEAD)
     visible = pk_ref[...] <= pq_ref[...]
@@ -251,7 +264,7 @@
         ):
             own_ref[:, lanes] = grad[:tokens]
             send_ref[:tokens, lanes] = grad[tokens : 2 * tokens].astype(BF)
-            far_ref[:, lanes] = grad[2 * tokens : 3 * tokens]
+            far_ref[:, lanes] = grad[2 * tokens : 3 * tokens].astype(BF)
             send_ref[tokens:, lanes] = grad[3 * tokens :].astype(BF)
 
 
@@ -272,12 +285,15 @@
     store_parts(dot_t(grad_ref[...], whole[...]), part_refs)
 
 
-def feed_kernel(here_ref, n_ref, mask_ref, mine_ref, other_ref, act_ref, slope_ref, *refs):
+def feed_kernel(
+    here_ref, n0, n1, n2, n3, mask_ref, mine_ref, other_ref, n_ref, act_ref, slope_ref, *refs
+):
     *part_refs, whole, sems = refs
     units = act_ref.shape[1]
     pair = (mine_ref, other_ref)
     ups = fetches(here_ref, pair, whole, sems.at[pl.ds(0, 16)], slice(0, units))
     downs = fetches(here_ref, pair, whole, sems.at[pl.ds(16, 16)], slice(units, None))
+    stacked((n0, n1, n2, n3), n_ref)
     fetched(ups)
     step = units // 4
     for at in range(0, units, step):
@@ -289,24 +305,30 @@
     store_parts(dot(act_ref[...], whole[:, units:]), part_refs)
 
 
-def feed_back_kernel(here_ref, b_ref, slope_ref, mine_ref, other_ref, grad_ref, *refs):
+def feed_back_kernel(
+    here_ref, b0, b1, b2, b3, slope_ref, mine_ref, other_ref, b_ref, grad_ref, *refs
+):
     *part_refs, whole, sems = refs
     units = grad_ref.shape[1]
     pair = (mine_ref, other_ref)
     downs = fetches(here_ref, pair, whole, sems.at[pl.ds(16, 16)], slice(units, None))
     ups = fetches(here_ref, pair, whole, sems.at[pl.ds(0, 16)], slice(0, units))
+    stacked((b0, b1, b2, b3), b_ref)
     fetched(downs)
     grad_ref[...] = (dot_t(b_ref[...], whole[:, units:]) * slope_ref[...]).astype(BF)
     fetched(ups)
     store_parts(dot_t(grad_ref[...], whole[:, :units]), part_refs)
 
 
-def feed_both_kernel(here_ref, n_ref, mask_ref, b_ref, mine_ref, other_ref, act_ref, grad_ref, *refs):
+def feed_both_kernel(
+    here_ref, n0, n1, n2, n3, mask_ref, b_ref, mine_ref, other_ref, n_ref, act_ref, grad_ref, *refs
+):
     *part_refs, whole, sems = refs
     units = act_ref.shape[1]
     pair = (mine_ref, other_ref)
     ups = fetches(here_ref, pair, whole, sems.at[pl.ds(0, 16)], slice(0, units))
     downs = fetches(here_ref, pair, whole, sems.at[pl.ds(16, 16)], slice(units, None))
+    stacked((n0, n1, n2, n3), n_ref)
     fetched(ups)
     fetched(downs)
     step = units // 4
@@ -389,13 +411,12 @@
     cos, sin, pos_here, pos_whole, unit_mask, here = tables
     x = x.astype(F32)
     w_in, normed = hook(0, normed)
-    normed = jnp.concatenate(normed, 0)
-    tokens, features = normed.shape
+    tokens, features = 4 * x.shape[0], x.shape[1]
     width = w_in[0].shape[-1] // 3
-    queries, kv = call(
+    normed, queries, kv = call(
         qkv_kernel,
-        [shape((tokens, width), BF), shape((tokens, 2 * width), BF)],
-        here, normed, cos, sin, rows=features, blocks=w_in,
+        [shape((tokens, features), BF), shape((tokens, width), BF), shape((tokens, 2 * width), BF)],
+        here, *normed, cos, sin, rows=features, blocks=w_in,
     )
     kv = hook(1, kv)
     kv = family(kv)
@@ -403,7 +424,8 @@
     mixed, lse, *parts = call(
         attend_kernel,
         [shape((tokens, width), BF), shape((tokens, width), F32), *part_shapes(features)],
-        here, queries, kv, pos_here, pos_whole, rows=width, blocks=w_out(),
+        here, queries, *kv, pos_here, pos_whole, rows=width, blocks=w_out(),
+        scratch=[pltpu.VMEM((4 * tokens, 2 * width), BF)],
     )
     parts = hook(3, parts)
     received = hook(7, sent_home(parts))
@@ -411,16 +433,13 @@
     return middle, (x, queries, kv, lse, middle), [(a, near(a)) for a in (normed, mixed)], w_in
 
 
-def feed_gathered(middle, hook):
-    return jnp.concatenate(hook(4, gather_ring(scaled(middle), "z")), 0)
-
-
 def lefts_of(normed, activated):
     return [(a, near(a)) for a in (normed, activated)]
 
 
 def feed_shapes(features, mask, *types):
-    return [shape((256, mask.shape[1]), t) for t in types] + part_shapes(features)
+    by_unit = [shape((256, mask.shape[1]), t) for t in types]
+    return [shape((256, features), BF), *by_unit, *part_shapes(features)]
 
 
 def arrived(middle, parts, received):
@@ -433,7 +452,7 @@
     return straight + scale * (q - n * jnp.mean(q * n, -1, keepdims=True))
 
 
-def backward(grad_out, branch, kept, feed_back, lefts, weights, tables, hook):
+def backward(grad_out, branch, kept, feed_back, lefts, weights, tables, hook, last):
     x, queries, kv, lse, middle = kept
     normed, mixed, normed_two, activated = lefts
     w_in, w_out = weights
@@ -452,25 +471,27 @@
     grad_middle = norm_backward(middle, summed(parts, received), grad_out)
     ring = gather_ring(grad_middle.astype(BF), "z")
     ring = hook(2, ring)
-    branch = jnp.concatenate(ring, 0)
-    dq, own, send, far = call(
+    branch, dq, own, send, far = call(
         attend_back_kernel,
         [
+            shape((tokens, features), BF),
             shape((tokens, width), BF),
             shape((tokens, 2 * width), F32),
             shape((2 * tokens, 2 * width), BF),
-            shape((tokens, 2 * width), F32),
+            shape((tokens, 2 * width), BF),
         ],
-        here, branch, queries, kv, lse, pos_here, pos_whole, cos, sin, rows=width, blocks=w_out,
+        here, *ring, queries, *kv, lse, pos_here, pos_whole, cos, sin, rows=width, blocks=w_out,
+        scratch=[pltpu.VMEM((4 * tokens, 2 * width), BF)],
     )
     dq, own, send, far = hook(6, (dq, own, send, far))
     branch_near = near(branch)
     send = near(send)
-    far = (far + send[tokens:].astype(F32)).astype(BF)
+    far = (far.astype(F32) + send[tokens:].astype(F32)).astype(BF)
     far = shifted(far, "sec", 1)
     out = t_dot(jnp.concatenate(mixed, 0), jnp.concatenate([branch, branch_near], 0)).astype(BF)
     out = lax.dynamic_index_in_dim(out.reshape(2, 2, -1, features), here[0], 1, keepdims=False)
     out = out.reshape(2, 4, -1, features).transpose(1, 0, 2, 3)
+    out = out.reshape(4, 2, -1, 3 * width)
     far, out = tied(far, out)
     far = hook(3, far)
     grad_projected, *parts = call(
@@ -478,12 +499,14 @@
         [shape((tokens, 3 * width), BF), *part_shapes(features)],
         here, dq, own, send, far, cos, sin, rows=features, blocks=w_in,
     )
-    parts = hook(5, parts)
-    received = sent_home(parts)
-    out = out.reshape(4, 2, -1, 3 * width)
+    parts, grad_projected = hook(5, (parts, grad_projected))
     g_in = weight_grads(here, [(*normed, grad_projected, near(grad_projected))], [out])
-    received, g_in = tied(received, g_in)
-    received = hook(4, received, g_in)
+    if last:
+        hook(4, None, g_in)
+        received = sent_home(parts)
+    else:
+        received, g_in = tied(sent_home(parts), g_in)
+        received = hook(4, received, g_in)
     return norm_backward(x, summed(parts, received), grad_middle).astype(BF)
 
 
@@ -605,7 +628,7 @@
             at["out_1"] = out_rows(at["attn_1"])
         if point == 2:
             chain = hold(chain, "out_1")
-        if point == 3:
+        if point == 7:
             chain = hold(chain, "feed")
             at["feed"] = with_near([at["feed"]])
         return chain
@@ -614,21 +637,21 @@
     middle_0, kept_0, lefts_0, in_0 = attention(
         x_0, normed_0, lambda: at["out_0"], tables, forward_0
     )
-    normed = feed_gathered(middle_0, forward_0)
+    normed = forward_0(4, gather_ring(scaled(middle_0), "z"))
     feed_0 = at["feed_0"]
-    activated, slope_0, *parts = call(
-        feed_kernel, feed_shapes(model, mask, BF, F32), here, normed, mask, rows=model, blocks=feed_0
+    normed, activated, slope_0, *parts = call(
+        feed_kernel, feed_shapes(model, mask, BF, F32), here, *normed, mask, rows=model, blocks=feed_0
     )
     lefts_0 += lefts_of(normed, activated)
-    hidden_0 = arrived(middle_0, parts, forward_0(8, sent_home(parts)))
+    hidden_0 = forward_0(8, arrived(middle_0, parts, sent_home(parts)))
     middle_1, kept_1, lefts_1, in_1 = attention(
         hidden_0, gather_ring(scaled(hidden_0.astype(F32)), "z"), lambda: at["out_1"], tables, forward_1
     )
-    normed = feed_gathered(middle_1, forward_1)
-    activated, grad_up, *parts = call(
+    normed = forward_1(4, gather_ring(scaled(middle_1), "z"))
+    normed, activated, grad_up, *parts = call(
         feed_both_kernel,
         feed_shapes(model, mask, BF, BF) + part_shapes(model),
-        here, normed, mask, branch_1, rows=model, blocks=at["feed"],
+        here, *normed, mask, branch_1, rows=model, blocks=at["feed"],
     )
     lefts_1 += lefts_of(normed, activated)
     parts_1, feed_back_1 = parts[:4], [grad_up, *parts[4:]]
@@ -678,23 +701,25 @@
         if point == 5:
             chain = hold(chain, "feed0")
             feeds = jnp.stack([at["feed0"], at["feed1"]])
-            at["up"], at["down"] = (
-                x_terms(feeds[:, :, a : a + 4 * rows]) for a in (0, 4 * rows)
-            )
+            at["up"], down = tied(x_terms(feeds[:, :, : 4 * rows]), feeds[:, :, 4 * rows :])
+            at["down"] = x_terms(down)
         if point == 4:
-            at["in0"] = y_sum(grads[0])
+            g_in, at["to_1"] = tied(grads[0], at["to_1"])
+            at["in0"] = y_sum(g_in)
         return chain
 
     grad_1 = backward(
-        cotangent, branch_1, kept_1, feed_back_1, lefts_1, (in_1, out_1), tables, backward_1
+        cotangent, branch_1, kept_1, feed_back_1, lefts_1, (in_1, out_1), tables, backward_1, False
     )
     hidden_1 = arrived(middle_1, at["parts"], at["received"])
-    branch_0 = gathered(grad_1, "z")
-    feed_back_0 = call(
-        feed_back_kernel, feed_shapes(model, mask, BF), here, branch_0, slope_0, rows=model, blocks=feed_0
+    at["to_1"] = jnp.stack([hidden_1, grad_1])
+    branch_0, *feed_back_0 = call(
+        feed_back_kernel,
+        feed_shapes(model, mask, BF),
+        here, *gather_ring(grad_1, "z"), slope_0, rows=model, blocks=feed_0,
     )
     grad_0 = backward(
-        grad_1, branch_0, kept_0, feed_back_0, lefts_0, (in_0, out_0), tables, backward_0
+        grad_1, branch_0, kept_0, feed_back_0, lefts_0, (in_0, out_0), tables, backward_0, True
     )
     def columns_home(block):
         z = lax.axis_index("z")
@@ -702,18 +727,18 @@
         got = [pick(0)] + [shifted(pick(k), "z", k) for k in (1, 2, 3)]
         return rolled(jnp.stack(got), "z", 0)
 
-    g_up, g_down = terms(at["up"]), terms(at["down"])
-    g_up = columns_home(g_up.astype(BF).reshape(4, rows, -1)).astype(F32)
+    g_up = columns_home(terms(at["up"]).astype(BF).reshape(4, rows, -1))
     g_in, g_out = (
         jnp.stack([at[n][:, rows_of] for n in ("in0", "in1")])
         for rows_of in (slice(0, 4 * rows), slice(4 * rows, None))
     )
     g_in = lax.all_to_all(g_in.reshape(16, rows, -1), ("sec", "xh", "z"), 0, 0, tiled=True)
     g_out = terms(x_terms(g_out.reshape(2, 2, rows, model)))
-    g_in, grad_0 = tied(g_in, grad_0)
+    g_in, grad_0, g_up, at["down"] = tied(g_in, grad_0, g_up, at["down"])
+    g_up, g_down = g_up.astype(F32), terms(at["down"])
     g_in = jnp.sum(g_in.reshape(4, 4, rows, -1).astype(F32), 0)
     to_0 = returned(jnp.stack([hidden_0, grad_0]), 0)
-    to_1 = returned(jnp.stack([hidden_1, grad_1]), 1)
+    to_1 = returned(at["to_1"], 1)
     hidden, input_grads = (jnp.where(sec == 0, a, b)[None] for a, b in zip(to_0, to_1))
     g_in = g_in.reshape(4, rows, 3, width_in // 12).transpose(1, 2, 0, 3).reshape(rows, width_in)
     g_up = g_up.reshape(4, rows, 16, units // 64).transpose(1, 2, 0, 3).reshape(rows, units)

time: 563 us -> 544 us (0.966)
  the two profiles are of different devices: /device:TPU:1 before, /device:TPU:0 now
where the time goes in v4:
time: 544 us; the launch traced here: 534 us
  waiting for transfers between devices  200 us (37%)
  starting transfers between devices  137 us (25%)
  Pallas kernels  105 us (19%)
  other arithmetic  35.8 us (7%)
  local copies, waits for them, and re-layouts  35.4 us (7%)
  between operations  16.6 us (3%)
    ppermute x91, waiting for transfers between devices, shifted(): lax.ppermute(block, axis, [(i, (i + distance) % n) for i in range(n)])  164 us
    ppermute x91, starting transfers between devices, shifted(): lax.ppermute(block, axis, [(i, (i + distance) % n) for i in range(n)])  97.4 us
    pallas_call x11, Pallas kernels, call(): pl.pallas_call(kernel, out_shape=out_shape, in_specs=[SMEM] + [VMEM] * le...  81.1 us
    pallas_call x4, Pallas kernels, weight_grads(): pl.pallas_call(weight_grad_kernel, grid_spec=pltpu.PrefetchScalarGridSpec...  24 us
    unnamed x193, local copies, waits for them, and re-layouts  17.3 us
  transfers between devices with their start and end apart: 114, of which 60 were waited for; matrix products, arithmetic and copies ran while one was open for 9% of the time, Pallas kernels for 19%

profile of v4, /device:TPU:0, one launch (start us, length us, event | category | flops | bytes accessed | tf_op | source)
XLA Modules:
  0.0 534.0 jit_solution(2484323906875930819)
XLA Ops:
  18.0 8.6 %all-to-all-done = bf16[4,24,2688]{2,1,0:T(8,128)(2,1)S(1)} async-done(((bf16[4,24,2688]{2,1,0:T(8,128)(2,1)}), bf16[4,24,2688]{2,1,0:T(8,128)(2,1)S(1)}, u32[]{:S(2)}, u32[]{:S(2)}) %all-to-all-start) | async-done | bytes 516128 | tf_op jit(solution)/shard_map/all_to_all | solution.py:553
  52.9 7.4 %collective-permute-start.10 = (bf16[2,64,1536]{2,1,0:T(8,128)(2,1)S(1)}, bf16[2,64,1536]{2,1,0:T(8,128)(2,1)S(1)}, u32[]{:S(2)}, u32[]{:S(2)}) collective-permute-start(bf16[2,64,1536]{2,1,0:T(8,128)(2,1)S(1)} %pad_maximum_fusion.12), channel_id=1, source_target_pairs={{0,2},{1,3},{2,0},{3,1},{4,6},{5,7},{6,4},{7,5},{8,10},{9,11},{10,... | collective-permute-start | bytes 1179656 | tf_op jit(solution)/shard_map/ppermute | solution.py:23
  68.8 9.7 %collective-permute-done.7 = bf16[96,3072]{1,0:T(8,128)(2,1)S(1)} collective-permute-done((bf16[96,3072]{1,0:T(8,128)(2,1)S(1)}, bf16[96,3072]{1,0:T(8,128)(2,1)S(1)}, u32[]{:S(2)}, u32[]{:S(2)}) %collective-permute-start.7) | collective-permute-done | bytes 589856 | tf_op jit(solution)/shard_map/ppermute | solution.py:23
  90.4 6.0 %shard_map.161 = (bf16[256,1536]{1,0:T(8,128)(2,1)}, bf16[256,384]{1,0:T(8,128)(2,1)}, bf16[256,768]{1,0:T(8,128)(2,1)}) custom-call(s32[4]{0:T(128)} %pad_add_fusion.3.here_ref, bf16[64,1536]{1,0:T(8,128)(2,1)} %get-tuple-element.183.n0, bf16[64,1536]{1,0:T(8,128)(2,1)} %get-tuple-element.184.n1, bf16[64,1536]{1,0:T(8,128)(2,1)} %get-tuple-element.185.n2, ...), custom_call_target="tpu_custom_call" | custom-call | flops 1 | bytes 1 | tf_op jit(solution)/shard_map/pallas_call | solution.py:118
  100.2 8.0 %collective-permute-done.15.kv2 = bf16[256,768]{1,0:T(8,128)(2,1)S(1)} collective-permute-done((bf16[256,768]{1,0:T(8,128)(2,1)}, bf16[256,768]{1,0:T(8,128)(2,1)S(1)}, u32[]{:S(2)}, u32[]{:S(2)}) %collective-permute-start.15) | collective-permute-done | bytes 393248 | tf_op jit(solution)/shard_map/ppermute | solution.py:23
  124.4 6.5 %collective-permute-done.18 = bf16[64,1536]{1,0:T(8,128)(2,1)S(1)} collective-permute-done((bf16[64,1536]{1,0:T(8,128)(2,1)}, bf16[64,1536]{1,0:T(8,128)(2,1)S(1)}, u32[]{:S(2)}, u32[]{:S(2)}) %collective-permute-start.18) | collective-permute-done | bytes 196640 | tf_op jit(solution)/shard_map/ppermute | solution.py:23
  154.8 8.6 %shard_map.163 = (bf16[256,1536]{1,0:T(8,128)(2,1)}, bf16[256,1536]{1,0:T(8,128)(2,1)}, f32[256,1536]{1,0:T(8,128)}, f32[64,1536]{1,0:T(8,128)}, bf16[64,1536]{1...) custom-call(s32[4]{0:T(128)} %pad_add_fusion.3.here_ref, bf16[64,1536]{1,0:T(8,128)(2,1)} %copy-done.42, ...), custom_call_target="tpu_custom_call" | custom-call | flops 1 | bytes 1 | tf_op jit(solution)/shard_map/pallas_call | solution.py:118
  167.4 7.0 %collective-permute-done.25 = bf16[64,1536]{1,0:T(8,128)(2,1)S(1)} collective-permute-done((bf16[64,1536]{1,0:T(8,128)(2,1)}, bf16[64,1536]{1,0:T(8,128)(2,1)S(1)}, u32[]{:S(2)}, u32[]{:S(2)}) %collective-permute-start.25) | collective-permute-done | bytes 196640 | tf_op jit(solution)/shard_map/ppermute | solution.py:23
  183.2 9.0 %collective-permute-done.29.n1 = bf16[64,1536]{1,0:T(8,128)(2,1)S(1)} collective-permute-done((bf16[64,1536]{1,0:T(8,128)(2,1)S(1)}, bf16[64,1536]{1,0:T(8,128)(2,1)S(1)}, u32[]{:S(2)}, u32[]{:S(2)}) %collective-permute-start.29) | collective-permute-done | bytes 196640 | tf_op jit(solution)/shard_map/ppermute | solution.py:23
  204.6 7.0 %collective-permute-done.34.kv2 = bf16[256,768]{1,0:T(8,128)(2,1)S(1)} collective-permute-done((bf16[256,768]{1,0:T(8,128)(2,1)}, bf16[256,768]{1,0:T(8,128)(2,1)S(1)}, u32[]{:S(2)}, u32[]{:S(2)}) %collective-permute-start.34) | collective-permute-done | bytes 393248 | tf_op jit(solution)/shard_map/ppermute | solution.py:23
  240.3 9.2 %collective-permute-done.40.n1 = bf16[64,1536]{1,0:T(8,128)(2,1)S(1)} collective-permute-done((bf16[64,1536]{1,0:T(8,128)(2,1)S(1)}, bf16[64,1536]{1,0:T(8,128)(2,1)S(1)}, u32[]{:S(2)}, u32[]{:S(2)}) %collective-permute-start.40) | collective-permute-done | bytes 196640 | tf_op jit(solution)/shard_map/ppermute | solution.py:23
  250.7 12.3 %shard_map.166 = (bf16[256,1536]{1,0:T(8,128)(2,1)}, bf16[256,1536]{1,0:T(8,128)(2,1)}, bf16[256,1536]{1,0:T(8,128)(2,1)}, f32[64,1536]{1,0:T(8,128)}, bf16[64,1...) custom-call(s32[4]{0:T(128)} %pad_add_fusion.3.here_ref, ...), custom_call_target="tpu_custom_call" | custom-call | flops 1 | bytes 1 | tf_op jit(solution)/shard_map/pallas_call | solution.py:118
  268.8 7.3 %shard_map.167 = bf16[4,2,192,1536]{3,2,1,0:T(8,128)(2,1)} custom-call(s32[4]{0:T(128)} %pad_add_fusion.3.here_ref, bf16[256,1536]{1,0:T(8,128)(2,1)} %get-tuple-element.243.refs_0_, bf16[256,1536]{1,0:T(8,128)(2,1)} %copy-done.48, bf16[256,1536]{1,0:T(8,128)(2,1)} %get-tuple-element.244.refs_2_, bf16[256,1536]{1,0:T(8,128)(2,1)} %copy-done.49, ...), custom_call_target="tpu_custom_call" | custom-call | flops 1 | bytes 1 | tf_op jit(solution)/shard_map/pallas_call | solution.py:371
  284.4 8.6 %collective-permute-done.51.b1 = bf16[64,1536]{1,0:T(8,128)(2,1)S(1)} collective-permute-done((bf16[64,1536]{1,0:T(8,128)(2,1)S(1)}, bf16[64,1536]{1,0:T(8,128)(2,1)S(1)}, u32[]{:S(2)}, u32[]{:S(2)}) %collective-permute-start.51) | collective-permute-done | bytes 196640 | tf_op jit(solution)/shard_map/ppermute | solution.py:23
  294.3 8.4 %shard_map.168 = (bf16[256,1536]{1,0:T(8,128)(2,1)}, bf16[256,384]{1,0:T(8,128)(2,1)}, f32[256,768]{1,0:T(8,128)}, bf16[512,768]{1,0:T(8,128)(2,1)}, bf16[256,768]{1,0:T(8,128)(2,1)}) custom-call(s32[4]{0:T(128)} %pad_add_fusion.3.here_ref, bf16[64,1536]{1,0:T(8,128)(2,1)} %copy-done.38, bf16[64,1536]{1,0:T(8,128)(2,1)} %copy-done.67, ...), custom_call_target="tpu_custom_call" | custom-call | flops 1 | bytes 1 | tf_op jit(solution)/shard_map/pallas_call | solution.py:118
  324.5 6.2 %shard_map.169 = (bf16[256,1152]{1,0:T(8,128)(2,1)}, f32[64,1536]{1,0:T(8,128)}, bf16[64,1536]{1,0:T(8,128)(2,1)}, bf16[64,1536]{1,0:T(8,128)(2,1)}, bf16[64,1536]{1,0:T(8,128)(2,1)}) custom-call(s32[4]{0:T(128)} %pad_add_fusion.3.here_ref, bf16[256,384]{1,0:T(8,128)(2,1)} %get-tuple-element.258.dq_ref, f32[256,768]{1,0:T(8,128)} %get-tuple-element.259.own_ref, ...), custom_call_target="tpu_custom_call" | custom-call | flops 1 | bytes 1 | tf_op jit(solution)/shard_map/pallas_call | solution.py:118
  350.0 8.1 %collective-permute-done.66.b1 = bf16[64,1536]{1,0:T(8,128)(2,1)S(1)} collective-permute-done((bf16[64,1536]{1,0:T(8,128)(2,1)S(1)}, bf16[64,1536]{1,0:T(8,128)(2,1)S(1)}, u32[]{:S(2)}, u32[]{:S(2)}) %collective-permute-start.66) | collective-permute-done | bytes 196640 | tf_op jit(solution)/shard_map/ppermute | solution.py:23
  359.5 8.2 %shard_map.171 = (bf16[256,1536]{1,0:T(8,128)(2,1)}, bf16[256,1536]{1,0:T(8,128)(2,1)}, f32[64,1536]{1,0:T(8,128)}, bf16[64,1536]{1,0:T(8,128)(2,1)}, bf16[64,15...) custom-call(s32[4]{0:T(128)} %pad_add_fusion.3.here_ref, bf16[64,1536]{1,0:T(8,128)(2,1)} %copy-done.11, ...), custom_call_target="tpu_custom_call" | custom-call | flops 1 | bytes 1 | tf_op jit(solution)/shard_map/pallas_call | solution.py:118
  373.4 7.3 %shard_map.172 = bf16[4,2,192,1536]{3,2,1,0:T(8,128)(2,1)} custom-call(s32[4]{0:T(128)} %pad_add_fusion.3.here_ref, bf16[256,1536]{1,0:T(8,128)(2,1)} %get-tuple-element.288.refs_0_, bf16[256,1536]{1,0:T(8,128)(2,1)} %copy-done.46, bf16[256,1536]{1,0:T(8,128)(2,1)} %get-tuple-element.289.refs_2_, bf16[256,1536]{1,0:T(8,128)(2,1)} %copy-done.50, ...), custom_call_target="tpu_custom_call" | custom-call | flops 1 | bytes 1 | tf_op jit(solution)/shard_map/pallas_call | solution.py:371
  388.4 8.8 %collective-permute-done.76.b1 = bf16[64,1536]{1,0:T(8,128)(2,1)S(1)} collective-permute-done((bf16[64,1536]{1,0:T(8,128)(2,1)S(1)}, bf16[64,1536]{1,0:T(8,128)(2,1)S(1)}, u32[]{:S(2)}, u32[]{:S(2)}) %collective-permute-start.76) | collective-permute-done | bytes 196640 | tf_op jit(solution)/shard_map/ppermute | solution.py:23
  398.5 8.4 %shard_map.173 = (bf16[256,1536]{1,0:T(8,128)(2,1)}, bf16[256,384]{1,0:T(8,128)(2,1)}, f32[256,768]{1,0:T(8,128)}, bf16[512,768]{1,0:T(8,128)(2,1)}, bf16[256,768]{1,0:T(8,128)(2,1)}) custom-call(s32[4]{0:T(128)} %pad_add_fusion.3.here_ref, bf16[64,1536]{1,0:T(8,128)(2,1)} %copy-done.37, bf16[64,1536]{1,0:T(8,128)(2,1)} %copy-done.66, ...), custom_call_target="tpu_custom_call" | custom-call | flops 1 | bytes 1 | tf_op jit(solution)/shard_map/pallas_call | solution.py:118
  415.7 7.3 %collective-permute-done.80.far_ref = bf16[256,768]{1,0:T(8,128)(2,1)S(1)} collective-permute-done((bf16[256,768]{1,0:T(8,128)(2,1)}, bf16[256,768]{1,0:T(8,128)(2,1)S(1)}, u32[]{:S(2)}, u32[]{:S(2)}) %collective-permute-start.80) | collective-permute-done | bytes 393248 | tf_op jit(solution)/shard_map/ppermute | solution.py:23
  423.7 6.2 %shard_map.174 = (bf16[256,1152]{1,0:T(8,128)(2,1)}, f32[64,1536]{1,0:T(8,128)}, bf16[64,1536]{1,0:T(8,128)(2,1)}, bf16[64,1536]{1,0:T(8,128)(2,1)}, bf16[64,1536]{1,0:T(8,128)(2,1)}) custom-call(s32[4]{0:T(128)} %pad_add_fusion.3.here_ref, bf16[256,384]{1,0:T(8,128)(2,1)} %get-tuple-element.300.dq_ref, f32[256,768]{1,0:T(8,128)} %get-tuple-element.301.own_ref, ...), custom_call_target="tpu_custom_call" | custom-call | flops 1 | bytes 1 | tf_op jit(solution)/shard_map/pallas_call | solution.py:118
  497.8 8.2 %collective-permute-done.95 = bf16[96,1536]{1,0:T(8,128)(2,1)} collective-permute-done((bf16[96,1536]{1,0:T(8,128)(2,1)S(1)}, bf16[96,1536]{1,0:T(8,128)(2,1)}, u32[]{:S(2)}, u32[]{:S(2)}) %collective-permute-start.95) | collective-permute-done | bytes 294944 | tf_op jit(solution)/shard_map/ppermute | solution.py:676
  (541 shorter events, 325.2 us)
Async XLA Ops:
  17.2 65.9 %all-gather.9.cloned.1.call-start = ((), (), s32[]{:S(2)}) async-start(), calls=%async_computation.10 | async-start | bytes 2949120 | tf_op jit(solution)/shard_map/all_gather | solution.py:403
  48.1 89.3 %all-gather.11.cloned.1.call-start = ((), (), s32[]{:S(2)}) async-start(), calls=%async_computation.11 | async-start | bytes 5898240 | tf_op jit(solution)/shard_map/all_gather | solution.py:403
  48.4 17.6 %collective-permute-start.6 = (bf16[96,3072]{1,0:T(8,128)(2,1)S(1)}, bf16[96,3072]{1,0:T(8,128)(2,1)S(1)}, u32[]{:S(2)}, u32[]{:S(2)}) collective-permute-start(bf16[96,3072]{1,0:T(8,128)(2,1)S(1)} %get-tuple-element.401), channel_id=1, source_target_pairs={{0,32},{32,0},{1,33},{33,1},{2,34},{34,2},{3,35},{35,3},{4,36},{36... | collective-permute-start | bytes 1769480 | tf_op jit(solution)/shard_map/ppermute | solution.py:23
  51.7 26.8 %collective-permute-start.7 = (bf16[96,3072]{1,0:T(8,128)(2,1)S(1)}, bf16[96,3072]{1,0:T(8,128)(2,1)S(1)}, u32[]{:S(2)}, u32[]{:S(2)}) collective-permute-start(bf16[96,3072]{1,0:T(8,128)(2,1)S(1)} %get-tuple-element.401), channel_id=1, source_target_pairs={{0,64},{64,0},{1,65},{65,1},{2,66},{66,2},{3,67},{67,3},{4,68},{68... | collective-permute-start | bytes 1769480 | tf_op jit(solution)/shard_map/ppermute | solution.py:23
  52.0 26.8 %collective-permute-start.8 = (bf16[96,3072]{1,0:T(8,128)(2,1)S(1)}, bf16[96,3072]{1,0:T(8,128)(2,1)S(1)}, u32[]{:S(2)}, u32[]{:S(2)}) collective-permute-start(bf16[96,3072]{1,0:T(8,128)(2,1)S(1)} %get-tuple-element.401), channel_id=1, source_target_pairs={{0,96},{32,64},{64,32},{96,0},{1,97},{33,65},{65,33},{97,1},{2,98}... | collective-permute-start | bytes 1769480 | tf_op jit(solution)/shard_map/ppermute | solution.py:398
  52.9 27.5 %collective-permute-start.10 = (bf16[2,64,1536]{2,1,0:T(8,128)(2,1)S(1)}, bf16[2,64,1536]{2,1,0:T(8,128)(2,1)S(1)}, u32[]{:S(2)}, u32[]{:S(2)}) collective-permute-start(bf16[2,64,1536]{2,1,0:T(8,128)(2,1)S(1)} %pad_maximum_fusion.12), channel_id=1, source_target_pairs={{0,2},{1,3},{2,0},{3,1},{4,6},{5,7},{6,4},{7,5},{8,10},{9,11},{10,... | collective-permute-start | bytes 1179656 | tf_op jit(solution)/shard_map/ppermute | solution.py:23
  60.3 20.1 %collective-permute-start.11 = (bf16[2,64,1536]{2,1,0:T(8,128)(2,1)S(1)}, bf16[2,64,1536]{2,1,0:T(8,128)(2,1)S(1)}, u32[]{:S(2)}, u32[]{:S(2)}) collective-permute-start(bf16[2,64,1536]{2,1,0:T(8,128)(2,1)S(1)} %pad_maximum_fusion.12), channel_id=1, source_target_pairs={{0,3},{1,0},{2,1},{3,2},{4,7},{5,4},{6,5},{7,6},{8,11},{9,8},{10,9... | collective-permute-start | bytes 1179656 | tf_op jit(solution)/shard_map/ppermute | solution.py:23
  80.5 98.6 %all-gather.13.cloned.1.call-start = ((), (), s32[]{:S(2)}) async-start(), calls=%async_computation.12 | async-start | bytes 2949120 | tf_op jit(solution)/shard_map/all_gather | solution.py:403
  109.9 117.4 %all-gather.15.cloned.1.call-start = ((), (), s32[]{:S(2)}) async-start(), calls=%async_computation.13 | async-start | bytes 5898240 | tf_op jit(solution)/shard_map/all_gather | solution.py:403
  137.4 207.3 %reduce-scatter.5.cloned.1.call-start = ((), (), s32[]{:S(2)}) async-start(), calls=%async_computation.6 | async-start | bytes 5898240 | tf_op jit(solution)/shard_map/reduce_scatter | solution.py:662
  240.0 26.1 %collective-permute-start.50 = (bf16[256,1536]{1,0:T(8,128)(2,1)S(1)}, bf16[256,1536]{1,0:T(8,128)(2,1)S(1)}, u32[]{:S(2)}, u32[]{:S(2)}) collective-permute-start(bf16[256,1536]{1,0:T(8,128)(2,1)S(1)} %pad_maximum_fusion.5.b_ref.refs_6_), channel_id=1, source_target_pairs={{0,16},{16,0},{1,17},{17,1},{2,18},{18,2},{3,19},{19,3},{4,20},{20... | collective-permute-start | bytes 2359304 | tf_op jit(solution)/shard_map/ppermute | solution.py:23
  278.8 104.3 %reduce-scatter.7.cloned.1.call-start = ((), (), s32[]{:S(2)}) async-start(), calls=%async_computation.7 | async-start | bytes 2949120 | tf_op jit(solution)/shard_map/reduce_scatter | solution.py:662
  309.1 23.8 %collective-permute-start.64 = (bf16[256,1536]{1,0:T(8,128)(2,1)S(1)}, bf16[256,1536]{1,0:T(8,128)(2,1)}, u32[]{:S(2)}, u32[]{:S(2)}) collective-permute-start(bf16[256,1536]{1,0:T(8,128)(2,1)S(1)} %copy-done.40), channel_id=1, source_target_pairs={{0,16},{16,0},{1,17},{17,1},{2,18},{18,2},{3,19},{19,3},{4,20},{20... | collective-permute-start | bytes 2359304 | tf_op jit(solution)/shard_map/ppermute | solution.py:23
  344.6 87.3 %reduce-scatter.9.cloned.1.call-start = ((), (), s32[]{:S(2)}) async-start(), calls=%async_computation.8 | async-start | bytes 5898240 | tf_op jit(solution)/shard_map/reduce_scatter | solution.py:662
  349.1 21.5 %collective-permute-start.72 = (bf16[256,1536]{1,0:T(8,128)(2,1)S(1)}, bf16[256,1536]{1,0:T(8,128)(2,1)S(1)}, u32[]{:S(2)}, u32[]{:S(2)}) collective-permute-start(bf16[256,1536]{1,0:T(8,128)(2,1)S(1)} %copy-done.43), channel_id=1, source_target_pairs={{0,16},{16,0},{1,17},{17,1},{2,18},{18,2},{3,19},{19,3},{4,20},{20... | collective-permute-start | bytes 2359304 | tf_op jit(solution)/shard_map/ppermute | solution.py:23
  349.5 21.1 %collective-permute-start.74 = (bf16[256,1536]{1,0:T(8,128)(2,1)S(1)}, bf16[256,1536]{1,0:T(8,128)(2,1)S(1)}, u32[]{:S(2)}, u32[]{:S(2)}) collective-permute-start(bf16[256,1536]{1,0:T(8,128)(2,1)S(1)} %copy-done.44), channel_id=1, source_target_pairs={{0,16},{16,0},{1,17},{17,1},{2,18},{18,2},{3,19},{19,3},{4,20},{20... | collective-permute-start | bytes 2359304 | tf_op jit(solution)/shard_map/ppermute | solution.py:23
  383.0 90.2 %reduce-scatter.11.cloned.1.call-start = ((), (), s32[]{:S(2)}) async-start(), calls=%async_computation.9 | async-start | bytes 2949120 | tf_op jit(solution)/shard_map/reduce_scatter | solution.py:662
  412.1 21.8 %collective-permute-start.28 = (bf16[256,1536]{1,0:T(8,128)(2,1)S(1)}, bf16[256,1536]{1,0:T(8,128)(2,1)}, u32[]{:S(2)}, u32[]{:S(2)}) collective-permute-start(bf16[256,1536]{1,0:T(8,128)(2,1)S(1)} %copy-done.39), channel_id=1, source_target_pairs={{0,16},{16,0},{1,17},{17,1},{2,18},{18,2},{3,19},{19,3},{4,20},{20... | collective-permute-start | bytes 2359304 | tf_op jit(solution)/shard_map/ppermute | solution.py:23
  469.6 28.2 %collective-permute-start.93 = (bf16[96,1536]{1,0:T(8,128)(2,1)}, bf16[96,1536]{1,0:T(8,128)(2,1)S(1)}, u32[]{:S(2)}, u32[]{:S(2)}) collective-permute-start(bf16[96,1536]{1,0:T(8,128)(2,1)} %get-tuple-element.390), channel_id=1, source_target_pairs={{0,32},{32,0},{1,33},{33,1},{2,34},{34,2},{3,35},{35,3},{4,36},{36... | collective-permute-start | bytes 884744 | tf_op jit(solution)/shard_map/ppermute | solution.py:23
  472.5 25.3 %collective-permute-start.94 = (bf16[96,1536]{1,0:T(8,128)(2,1)}, bf16[96,1536]{1,0:T(8,128)(2,1)S(1)}, u32[]{:S(2)}, u32[]{:S(2)}) collective-permute-start(bf16[96,1536]{1,0:T(8,128)(2,1)} %get-tuple-element.389), channel_id=1, source_target_pairs={{0,64},{64,0},{1,65},{65,1},{2,66},{66,2},{3,67},{67,3},{4,68},{68... | collective-permute-start | bytes 884744 | tf_op jit(solution)/shard_map/ppermute | solution.py:23
  480.6 25.4 %all-to-all-start.1 = ((bf16[16,24,1152]{2,1,0:T(8,128)(2,1)}), bf16[16,24,1152]{2,1,0:T(8,128)(2,1)S(1)}, u32[]{:S(2)}, u32[]{:S(2)}) async-start(bf16[16,24,1152]{2,1,0:T(8,128)(2,1)} %bitcast.62), calls=%async_computation.5 | async-start | bytes 1769472 | tf_op jit(solution)/shard_map/all_to_all | solution.py:735
  488.2 17.8 %collective-permute-start.95 = (bf16[96,1536]{1,0:T(8,128)(2,1)S(1)}, bf16[96,1536]{1,0:T(8,128)(2,1)}, u32[]{:S(2)}, u32[]{:S(2)}) collective-permute-start(bf16[96,1536]{1,0:T(8,128)(2,1)S(1)} %get-tuple-element.388), channel_id=1, source_target_pairs={{0,96},{32,64},{64,32},{96,0},{1,97},{33,65},{65,33},{97,1},{2,98}... | collective-permute-start | bytes 884744 | tf_op jit(solution)/shard_map/ppermute | solution.py:676
  492.6 29.0 %collective-permute-start.98 = (bf16[2,64,1536]{2,1,0:T(8,128)(2,1)}, bf16[2,64,1536]{2,1,0:T(8,128)(2,1)}, u32[]{:S(2)}, u32[]{:S(2)}) collective-permute-start(bf16[2,64,1536]{2,1,0:T(8,128)(2,1)} %pad_maximum_fusion.13), channel_id=1, source_target_pairs={{0,64},{8,80},{16,68},{24,84},{64,72},{72,88},{80,76},{88,92},{1,6... | collective-permute-start | bytes 1179656 | tf_op jit(solution)/shard_map/ppermute | solution.py:80
  495.7 25.9 %collective-permute-start.99 = (bf16[2,64,1536]{2,1,0:T(8,128)(2,1)}, bf16[2,64,1536]{2,1,0:T(8,128)(2,1)}, u32[]{:S(2)}, u32[]{:S(2)}) collective-permute-start(bf16[2,64,1536]{2,1,0:T(8,128)(2,1)} %pad_maximum_fusion.13), channel_id=1, source_target_pairs={{4,64},{12,80},{20,68},{28,84},{68,72},{76,88},{84,76},{92,92},{5,... | collective-permute-start | bytes 1179656 | tf_op jit(solution)/shard_map/ppermute | solution.py:80
  (186 other events, 1426.2 us)
Sparse Core Ops, SparseCore 0:
  48.2 34.7 all-gather.8
  84.7 52.6 all-gather.10
  139.7 33.4 all-gather.12
  174.6 52.6 all-gather.14
  278.9 49.1 reduce-scatter.4
  344.7 29.3 reduce-scatter.6
  383.1 48.8 reduce-scatter.8
  439.9 31.5 reduce-scatter.10

commit v5 on v4

--- a/solution.py
+++ b/solution.py
@@ -24,7 +24,8 @@
 
 
 def gather_ring(block, axis):
-    return [block] + [shifted(block, axis, k) for k in range(1, lax.axis_size(axis))]
+    farthest_first = {k: shifted(block, axis, k) for k in (2, 1, 3)}
+    return [block] + [farthest_first[k] for k in (1, 2, 3)]
 
 
 def gathered(block, axis):
@@ -147,7 +148,7 @@
 
 
 def sent_home(parts):
-    return [shifted(parts[k], "z", -k) for k in range(1, 4)]
+    return [shifted(parts[k], "z", -k) for k in (2, 1, 3)]
 
 
 def stacked(refs, whole):
@@ -189,17 +190,20 @@
 
 
 def fetch_scratch(rows, blocks):
-    return [pltpu.VMEM((rows, blocks[0].shape[-1]), BF), pltpu.SemaphoreType.DMA((32,))]
+    return [pltpu.VMEM((rows, blocks[0].shape[-1]), BF), pltpu.SemaphoreType.DMA((48,))]
 
 
 def qkv_kernel(here_ref, n0, n1, n2, n3, cos_ref, sin_ref, *refs):
     *refs, n_ref, q_ref, kv_ref, whole, sems = refs
-    copies = fetches(here_ref, refs, whole, sems)
+    width = q_ref.shape[1]
+    copies = [
+        fetches(here_ref, refs, whole, sems.at[pl.ds(16 * j, 16)], slice(j * width, (j + 1) * width))
+        for j in (0, 1, 2)
+    ]
     stacked((n0, n1, n2, n3), n_ref)
-    fetched(copies)
-    width = q_ref.shape[1]
     cos, sin = cos_ref[...], sin_ref[...]
     for j in (0, 1, 2):
+        fetched(copies[j])
         ref, at = (q_ref, 0) if j == 0 else (kv_ref, (j - 1) * width)
         total = dot(n_ref[...], whole[:, j * width : (j + 1) * width])
         for h in range(0, width, HEAD):
@@ -323,21 +327,21 @@
 def feed_both_kernel(
     here_ref, n0, n1, n2, n3, mask_ref, b_ref, mine_ref, other_ref, n_ref, act_ref, grad_ref, *refs
 ):
-    *part_refs, whole, sems = refs
+    *part_refs, slope_ref, whole, sems = refs
     units = act_ref.shape[1]
     pair = (mine_ref, other_ref)
     ups = fetches(here_ref, pair, whole, sems.at[pl.ds(0, 16)], slice(0, units))
     downs = fetches(here_ref, pair, whole, sems.at[pl.ds(16, 16)], slice(units, None))
     stacked((n0, n1, n2, n3), n_ref)
     fetched(ups)
-    fetched(downs)
     step = units // 4
     for at in range(0, units, step):
         lanes = slice(at, at + step)
         value, slope = gelu_parts(dot(n_ref[...], whole[:, lanes]))
         act_ref[:, lanes] = (value * mask_ref[:, lanes]).astype(BF)
-        back = dot_t(b_ref[...], whole[at : at + step, units:])
-        grad_ref[:, lanes] = (back * (slope * mask_ref[:, lanes])).astype(BF)
+        slope_ref[:, lanes] = slope * mask_ref[:, lanes]
+    fetched(downs)
+    grad_ref[...] = (dot_t(b_ref[...], whole[:, units:]) * slope_ref[...]).astype(BF)
     store_parts(dot_t(grad_ref[...], whole[:, :units]), part_refs[4:])
     store_parts(dot(act_ref[...], whole[:, units:]), part_refs[:4])
 
@@ -652,6 +656,7 @@
         feed_both_kernel,
         feed_shapes(model, mask, BF, BF) + part_shapes(model),
         here, *normed, mask, branch_1, rows=model, blocks=at["feed"],
+        scratch=[pltpu.VMEM((256, mask.shape[1]), F32)],
     )
     lefts_1 += lefts_of(normed, activated)
     parts_1, feed_back_1 = parts[:4], [grad_up, *parts[4:]]
@@ -701,7 +706,8 @@
         if point == 5:
             chain = hold(chain, "feed0")
             feeds = jnp.stack([at["feed0"], at["feed1"]])
-            at["up"], down = tied(x_terms(feeds[:, :, : 4 * rows]), feeds[:, :, 4 * rows :])
+            at["up"] = x_terms(feeds[:, :, : 4 * rows])
+            at["up"][1], down = tied(at["up"][1], feeds[:, :, 4 * rows :])
             at["down"] = x_terms(down)
         if point == 4:
             g_in, at["to_1"] = tied(grads[0], at["to_1"])

time: 544 us -> 537 us (0.987)
  waiting for transfers between devices: 200 us -> 181 us
  starting transfers between devices: 137 us -> 147 us
    ppermute x91, waiting for transfers between devices: 164 us -> 141 us  [shifted(): lax.ppermute(block, axis, [(i, (i + distance) % n) for i in range(n)])]
    ppermute x91, starting transfers between devices: 97.4 us -> 108 us  [shifted(): lax.ppermute(block, axis, [(i, (i + distance) % n) for i in range(n)])]
  transfers between devices with their start and end apart: 114 -> 114, of which waited for: 60 -> 54; matrix products, arithmetic and copies ran while one was open for 9% -> 10% of each run, Pallas kernels for 19% -> 19%
where the time goes in v5:
time: 537 us; the launch traced here: 527 us
  waiting for transfers between devices  181 us (34%)
  starting transfers between devices  147 us (27%)
  Pallas kernels  105 us (20%)
  local copies, waits for them, and re-layouts  36.7 us (7%)
  other arithmetic  35.8 us (7%)
  between operations  16.6 us (3%)
    ppermute x91, waiting for transfers between devices, shifted(): lax.ppermute(block, axis, [(i, (i + distance) % n) for i in range(n)])  141 us
    ppermute x91, starting transfers between devices, shifted(): lax.ppermute(block, axis, [(i, (i + distance) % n) for i in range(n)])  108 us
    pallas_call x11, Pallas kernels, call(): pl.pallas_call(kernel, out_shape=out_shape, in_specs=[SMEM] + [VMEM] * le...  81.3 us
    pallas_call x4, Pallas kernels, weight_grads(): pl.pallas_call(weight_grad_kernel, grid_spec=pltpu.PrefetchScalarGridSpec...  24.1 us
    unnamed x193, local copies, waits for them, and re-layouts  18.7 us
  transfers between devices with their start and end apart: 114, of which 54 were waited for; matrix products, arithmetic and copies ran while one was open for 10% of the time, Pallas kernels for 19%

profile of v5, /device:TPU:0, one launch (start us, length us, event | category | flops | bytes accessed | tf_op | source)
XLA Modules:
  0.0 527.1 jit_solution(17143259612303814880)
XLA Ops:
  11.8 5.4 %all-to-all-start = ((bf16[4,24,2688]{2,1,0:T(8,128)(2,1)}), bf16[4,24,2688]{2,1,0:T(8,128)(2,1)S(1)}, u32[]{:S(2)}, u32[]{:S(2)}) async-start(bf16[4,24,2688]{2,1,0:T(8,128)(2,1)} %pad_maximum_fusion.9), calls=%async_computation | async-start | bytes 1032192 | tf_op jit(solution)/shard_map/all_to_all | solution.py:557
  18.0 8.6 %all-to-all-done = bf16[4,24,2688]{2,1,0:T(8,128)(2,1)S(1)} async-done(((bf16[4,24,2688]{2,1,0:T(8,128)(2,1)}), bf16[4,24,2688]{2,1,0:T(8,128)(2,1)S(1)}, u32[]{:S(2)}, u32[]{:S(2)}) %all-to-all-start) | async-done | bytes 516128 | tf_op jit(solution)/shard_map/all_to_all | solution.py:557
  52.9 7.4 %collective-permute-start.10 = (bf16[2,64,1536]{2,1,0:T(8,128)(2,1)S(1)}, bf16[2,64,1536]{2,1,0:T(8,128)(2,1)S(1)}, u32[]{:S(2)}, u32[]{:S(2)}) collective-permute-start(bf16[2,64,1536]{2,1,0:T(8,128)(2,1)S(1)} %pad_maximum_fusion.12), channel_id=1, source_target_pairs={{0,2},{1,3},{2,0},{3,1},{4,6},{5,7},{6,4},{7,5},{8,10},{9,11},{10,... | collective-permute-start | bytes 1179656 | tf_op jit(solution)/shard_map/ppermute | solution.py:23
  60.3 5.6 %collective-permute-done.6 = bf16[96,3072]{1,0:T(8,128)(2,1)S(1)} collective-permute-done((bf16[96,3072]{1,0:T(8,128)(2,1)S(1)}, bf16[96,3072]{1,0:T(8,128)(2,1)S(1)}, u32[]{:S(2)}, u32[]{:S(2)}) %collective-permute-start.6) | collective-permute-done | bytes 589856 | tf_op jit(solution)/shard_map/ppermute | solution.py:23
  68.8 9.7 %collective-permute-done.7 = bf16[96,3072]{1,0:T(8,128)(2,1)S(1)} collective-permute-done((bf16[96,3072]{1,0:T(8,128)(2,1)S(1)}, bf16[96,3072]{1,0:T(8,128)(2,1)S(1)}, u32[]{:S(2)}, u32[]{:S(2)}) %collective-permute-start.7) | collective-permute-done | bytes 589856 | tf_op jit(solution)/shard_map/ppermute | solution.py:23
  90.4 5.8 %shard_map.161 = (bf16[256,1536]{1,0:T(8,128)(2,1)}, bf16[256,384]{1,0:T(8,128)(2,1)}, bf16[256,768]{1,0:T(8,128)(2,1)}) custom-call(s32[4]{0:T(128)} %pad_add_fusion.3.here_ref, bf16[64,1536]{1,0:T(8,128)(2,1)} %get-tuple-element.180.n0, bf16[64,1536]{1,0:T(8,128)(2,1)} %get-tuple-element.181.n1, bf16[64,1536]{1,0:T(8,128)(2,1)} %get-tuple-element.182.n2, ...), custom_call_target="tpu_custom_call" | custom-call | flops 1 | bytes 1 | tf_op jit(solution)/shard_map/pallas_call | solution.py:119
  100.0 7.9 %collective-permute-done.15.kv2 = bf16[256,768]{1,0:T(8,128)(2,1)S(1)} collective-permute-done((bf16[256,768]{1,0:T(8,128)(2,1)}, bf16[256,768]{1,0:T(8,128)(2,1)S(1)}, u32[]{:S(2)}, u32[]{:S(2)}) %collective-permute-start.15) | collective-permute-done | bytes 393248 | tf_op jit(solution)/shard_map/ppermute | solution.py:23
  111.6 5.6 %shard_map.162 = (bf16[256,384]{1,0:T(8,128)(2,1)}, f32[256,384]{1,0:T(8,128)}, f32[64,1536]{1,0:T(8,128)}, bf16[64,1536]{1,0:T(8,128)(2,1)}, bf16[64,1536]{1,0:T(8,128)(2,1)}, /*index=5*/bf16[64,1536]{1,0:T(8,128)(2,1)}) custom-call(s32[4]{0:T(128)} %pad_add_fusion.3.here_ref, bf16[256,384]{1,0:T(8,128)(2,1)} %get-tuple-element.186.q_ref, ...), custom_call_target="tpu_custom_call" | custom-call | flops 1 | bytes 1 | tf_op jit(solution)/shard_map/pallas_call | solution.py:119
  117.1 5.9 %collective-permute-start.18 = (bf16[64,1536]{1,0:T(8,128)(2,1)}, bf16[64,1536]{1,0:T(8,128)(2,1)S(1)}, u32[]{:S(2)}, u32[]{:S(2)}) collective-permute-start(bf16[64,1536]{1,0:T(8,128)(2,1)} %get-tuple-element.197), channel_id=1, source_target_pairs={{0,2},{1,3},{2,0},{3,1},{4,6},{5,7},{6,4},{7,5},{8,10},{9,11},{10,... | collective-permute-start | bytes 589832 | tf_op jit(solution)/shard_map/ppermute | solution.py:23
  154.8 8.7 %shard_map.163 = (bf16[256,1536]{1,0:T(8,128)(2,1)}, bf16[256,1536]{1,0:T(8,128)(2,1)}, f32[256,1536]{1,0:T(8,128)}, f32[64,1536]{1,0:T(8,128)}, bf16[64,1536]{1...) custom-call(s32[4]{0:T(128)} %pad_add_fusion.3.here_ref, bf16[64,1536]{1,0:T(8,128)(2,1)} %copy-done.42, ...), custom_call_target="tpu_custom_call" | custom-call | flops 1 | bytes 1 | tf_op jit(solution)/shard_map/pallas_call | solution.py:119
  193.2 5.9 %shard_map.164 = (bf16[256,1536]{1,0:T(8,128)(2,1)}, bf16[256,384]{1,0:T(8,128)(2,1)}, bf16[256,768]{1,0:T(8,128)(2,1)}) custom-call(s32[4]{0:T(128)} %pad_add_fusion.3.here_ref, bf16[64,1536]{1,0:T(8,128)(2,1)} %copy-done.33, bf16[64,1536]{1,0:T(8,128)(2,1)} %copy-done.72, bf16[64,1536]{1,0:T(8,128)(2,1)} %copy-done.73, bf16[64,1536]{1,0:T(8,128)(2,1)} %copy-done.74, ...), custom_call_target="tpu_custom_call" | custom-call | flops 1 | bytes 1 | tf_op jit(solution)/shard_map/pallas_call | solution.py:119
  202.8 7.2 %collective-permute-done.34.kv2 = bf16[256,768]{1,0:T(8,128)(2,1)S(1)} collective-permute-done((bf16[256,768]{1,0:T(8,128)(2,1)}, bf16[256,768]{1,0:T(8,128)(2,1)S(1)}, u32[]{:S(2)}, u32[]{:S(2)}) %collective-permute-start.34) | collective-permute-done | bytes 393248 | tf_op jit(solution)/shard_map/ppermute | solution.py:23
  212.6 5.6 %shard_map.165 = (bf16[256,384]{1,0:T(8,128)(2,1)}, f32[256,384]{1,0:T(8,128)}, f32[64,1536]{1,0:T(8,128)}, bf16[64,1536]{1,0:T(8,128)(2,1)}, bf16[64,1536]{1,0:T(8,128)(2,1)}, /*index=5*/bf16[64,1536]{1,0:T(8,128)(2,1)}) custom-call(s32[4]{0:T(128)} %pad_add_fusion.3.here_ref, bf16[256,384]{1,0:T(8,128)(2,1)} %get-tuple-element.219.q_ref, ...), custom_call_target="tpu_custom_call" | custom-call | flops 1 | bytes 1 | tf_op jit(solution)/shard_map/pallas_call | solution.py:119
  247.2 11.4 %shard_map.166 = (bf16[256,1536]{1,0:T(8,128)(2,1)}, bf16[256,1536]{1,0:T(8,128)(2,1)}, bf16[256,1536]{1,0:T(8,128)(2,1)}, f32[64,1536]{1,0:T(8,128)}, bf16[64,1...) custom-call(s32[4]{0:T(128)} %pad_add_fusion.3.here_ref, ...), custom_call_target="tpu_custom_call" | custom-call | flops 1 | bytes 1 | tf_op jit(solution)/shard_map/pallas_call | solution.py:119
  265.4 7.3 %shard_map.167 = bf16[4,2,192,1536]{3,2,1,0:T(8,128)(2,1)} custom-call(s32[4]{0:T(128)} %pad_add_fusion.3.here_ref, bf16[256,1536]{1,0:T(8,128)(2,1)} %get-tuple-element.240.refs_0_, bf16[256,1536]{1,0:T(8,128)(2,1)} %copy-done.48, bf16[256,1536]{1,0:T(8,128)(2,1)} %get-tuple-element.241.refs_2_, bf16[256,1536]{1,0:T(8,128)(2,1)} %copy-done.49, ...), custom_call_target="tpu_custom_call" | custom-call | flops 1 | bytes 1 | tf_op jit(solution)/shard_map/pallas_call | solution.py:375
  288.6 8.7 %shard_map.168 = (bf16[256,1536]{1,0:T(8,128)(2,1)}, bf16[256,384]{1,0:T(8,128)(2,1)}, f32[256,768]{1,0:T(8,128)}, bf16[512,768]{1,0:T(8,128)(2,1)}, bf16[256,768]{1,0:T(8,128)(2,1)}) custom-call(s32[4]{0:T(128)} %pad_add_fusion.3.here_ref, bf16[64,1536]{1,0:T(8,128)(2,1)} %copy-done.38, bf16[64,1536]{1,0:T(8,128)(2,1)} %copy-done.67, ...), custom_call_target="tpu_custom_call" | custom-call | flops 1 | bytes 1 | tf_op jit(solution)/shard_map/pallas_call | solution.py:119
  316.9 6.4 %shard_map.169 = (bf16[256,1152]{1,0:T(8,128)(2,1)}, f32[64,1536]{1,0:T(8,128)}, bf16[64,1536]{1,0:T(8,128)(2,1)}, bf16[64,1536]{1,0:T(8,128)(2,1)}, bf16[64,1536]{1,0:T(8,128)(2,1)}) custom-call(s32[4]{0:T(128)} %pad_add_fusion.3.here_ref, bf16[256,384]{1,0:T(8,128)(2,1)} %get-tuple-element.255.dq_ref, f32[256,768]{1,0:T(8,128)} %get-tuple-element.256.own_ref, ...), custom_call_target="tpu_custom_call" | custom-call | flops 1 | bytes 1 | tf_op jit(solution)/shard_map/pallas_call | solution.py:119
  351.5 8.4 %shard_map.171 = (bf16[256,1536]{1,0:T(8,128)(2,1)}, bf16[256,1536]{1,0:T(8,128)(2,1)}, f32[64,1536]{1,0:T(8,128)}, bf16[64,1536]{1,0:T(8,128)(2,1)}, bf16[64,15...) custom-call(s32[4]{0:T(128)} %pad_add_fusion.3.here_ref, bf16[64,1536]{1,0:T(8,128)(2,1)} %copy-done.11, ...), custom_call_target="tpu_custom_call" | custom-call | flops 1 | bytes 1 | tf_op jit(solution)/shard_map/pallas_call | solution.py:119
  366.0 7.3 %shard_map.172 = bf16[4,2,192,1536]{3,2,1,0:T(8,128)(2,1)} custom-call(s32[4]{0:T(128)} %pad_add_fusion.3.here_ref, bf16[256,1536]{1,0:T(8,128)(2,1)} %get-tuple-element.285.refs_0_, bf16[256,1536]{1,0:T(8,128)(2,1)} %copy-done.46, bf16[256,1536]{1,0:T(8,128)(2,1)} %get-tuple-element.286.refs_2_, bf16[256,1536]{1,0:T(8,128)(2,1)} %copy-done.50, ...), custom_call_target="tpu_custom_call" | custom-call | flops 1 | bytes 1 | tf_op jit(solution)/shard_map/pallas_call | solution.py:375
  389.4 8.6 %shard_map.173 = (bf16[256,1536]{1,0:T(8,128)(2,1)}, bf16[256,384]{1,0:T(8,128)(2,1)}, f32[256,768]{1,0:T(8,128)}, bf16[512,768]{1,0:T(8,128)(2,1)}, bf16[256,768]{1,0:T(8,128)(2,1)}) custom-call(s32[4]{0:T(128)} %pad_add_fusion.3.here_ref, bf16[64,1536]{1,0:T(8,128)(2,1)} %copy-done.37, bf16[64,1536]{1,0:T(8,128)(2,1)} %copy-done.66, ...), custom_call_target="tpu_custom_call" | custom-call | flops 1 | bytes 1 | tf_op jit(solution)/shard_map/pallas_call | solution.py:119
  406.6 7.6 %collective-permute-done.80.far_ref = bf16[256,768]{1,0:T(8,128)(2,1)S(1)} collective-permute-done((bf16[256,768]{1,0:T(8,128)(2,1)}, bf16[256,768]{1,0:T(8,128)(2,1)S(1)}, u32[]{:S(2)}, u32[]{:S(2)}) %collective-permute-start.80) | collective-permute-done | bytes 393248 | tf_op jit(solution)/shard_map/ppermute | solution.py:23
  414.9 6.4 %shard_map.174 = (bf16[256,1152]{1,0:T(8,128)(2,1)}, f32[64,1536]{1,0:T(8,128)}, bf16[64,1536]{1,0:T(8,128)(2,1)}, bf16[64,1536]{1,0:T(8,128)(2,1)}, bf16[64,1536]{1,0:T(8,128)(2,1)}) custom-call(s32[4]{0:T(128)} %pad_add_fusion.3.here_ref, bf16[256,384]{1,0:T(8,128)(2,1)} %get-tuple-element.297.dq_ref, f32[256,768]{1,0:T(8,128)} %get-tuple-element.298.own_ref, ...), custom_call_target="tpu_custom_call" | custom-call | flops 1 | bytes 1 | tf_op jit(solution)/shard_map/pallas_call | solution.py:119
  472.9 5.9 %all-to-all-start.1 = ((bf16[16,24,1152]{2,1,0:T(8,128)(2,1)}), bf16[16,24,1152]{2,1,0:T(8,128)(2,1)S(1)}, u32[]{:S(2)}, u32[]{:S(2)}) async-start(bf16[16,24,1152]{2,1,0:T(8,128)(2,1)} %bitcast.62), calls=%async_computation.5 | async-start | bytes 1769472 | tf_op jit(solution)/shard_map/all_to_all | solution.py:741
  490.0 8.7 %collective-permute-done.95 = bf16[96,1536]{1,0:T(8,128)(2,1)} collective-permute-done((bf16[96,1536]{1,0:T(8,128)(2,1)S(1)}, bf16[96,1536]{1,0:T(8,128)(2,1)}, u32[]{:S(2)}, u32[]{:S(2)}) %collective-permute-start.95) | collective-permute-done | bytes 294944 | tf_op jit(solution)/shard_map/ppermute | solution.py:681
  (541 shorter events, 334.6 us)
Async XLA Ops:
  17.2 65.9 %all-gather.9.cloned.1.call-start = ((), (), s32[]{:S(2)}) async-start(), calls=%async_computation.10 | async-start | bytes 2949120 | tf_op jit(solution)/shard_map/all_gather | solution.py:407
  48.1 89.3 %all-gather.11.cloned.1.call-start = ((), (), s32[]{:S(2)}) async-start(), calls=%async_computation.11 | async-start | bytes 5898240 | tf_op jit(solution)/shard_map/all_gather | solution.py:407
  48.4 17.6 %collective-permute-start.6 = (bf16[96,3072]{1,0:T(8,128)(2,1)S(1)}, bf16[96,3072]{1,0:T(8,128)(2,1)S(1)}, u32[]{:S(2)}, u32[]{:S(2)}) collective-permute-start(bf16[96,3072]{1,0:T(8,128)(2,1)S(1)} %get-tuple-element.394), channel_id=1, source_target_pairs={{0,32},{32,0},{1,33},{33,1},{2,34},{34,2},{3,35},{35,3},{4,36},{36... | collective-permute-start | bytes 1769480 | tf_op jit(solution)/shard_map/ppermute | solution.py:23
  51.7 26.8 %collective-permute-start.7 = (bf16[96,3072]{1,0:T(8,128)(2,1)S(1)}, bf16[96,3072]{1,0:T(8,128)(2,1)S(1)}, u32[]{:S(2)}, u32[]{:S(2)}) collective-permute-start(bf16[96,3072]{1,0:T(8,128)(2,1)S(1)} %get-tuple-element.394), channel_id=1, source_target_pairs={{0,64},{64,0},{1,65},{65,1},{2,66},{66,2},{3,67},{67,3},{4,68},{68... | collective-permute-start | bytes 1769480 | tf_op jit(solution)/shard_map/ppermute | solution.py:23
  52.0 26.8 %collective-permute-start.8 = (bf16[96,3072]{1,0:T(8,128)(2,1)S(1)}, bf16[96,3072]{1,0:T(8,128)(2,1)S(1)}, u32[]{:S(2)}, u32[]{:S(2)}) collective-permute-start(bf16[96,3072]{1,0:T(8,128)(2,1)S(1)} %get-tuple-element.394), channel_id=1, source_target_pairs={{0,96},{32,64},{64,32},{96,0},{1,97},{33,65},{65,33},{97,1},{2,98}... | collective-permute-start | bytes 1769480 | tf_op jit(solution)/shard_map/ppermute | solution.py:402
  52.9 27.5 %collective-permute-start.10 = (bf16[2,64,1536]{2,1,0:T(8,128)(2,1)S(1)}, bf16[2,64,1536]{2,1,0:T(8,128)(2,1)S(1)}, u32[]{:S(2)}, u32[]{:S(2)}) collective-permute-start(bf16[2,64,1536]{2,1,0:T(8,128)(2,1)S(1)} %pad_maximum_fusion.12), channel_id=1, source_target_pairs={{0,2},{1,3},{2,0},{3,1},{4,6},{5,7},{6,4},{7,5},{8,10},{9,11},{10,... | collective-permute-start | bytes 1179656 | tf_op jit(solution)/shard_map/ppermute | solution.py:23
  60.3 20.1 %collective-permute-start.11 = (bf16[2,64,1536]{2,1,0:T(8,128)(2,1)S(1)}, bf16[2,64,1536]{2,1,0:T(8,128)(2,1)S(1)}, u32[]{:S(2)}, u32[]{:S(2)}) collective-permute-start(bf16[2,64,1536]{2,1,0:T(8,128)(2,1)S(1)} %pad_maximum_fusion.12), channel_id=1, source_target_pairs={{0,3},{1,0},{2,1},{3,2},{4,7},{5,4},{6,5},{7,6},{8,11},{9,8},{10,9... | collective-permute-start | bytes 1179656 | tf_op jit(solution)/shard_map/ppermute | solution.py:23
  80.5 96.7 %all-gather.13.cloned.1.call-start = ((), (), s32[]{:S(2)}) async-start(), calls=%async_computation.12 | async-start | bytes 2949120 | tf_op jit(solution)/shard_map/all_gather | solution.py:407
  109.7 117.6 %all-gather.15.cloned.1.call-start = ((), (), s32[]{:S(2)}) async-start(), calls=%async_computation.13 | async-start | bytes 5898240 | tf_op jit(solution)/shard_map/all_gather | solution.py:407
  137.4 199.3 %reduce-scatter.5.cloned.1.call-start = ((), (), s32[]{:S(2)}) async-start(), calls=%async_computation.6 | async-start | bytes 5898240 | tf_op jit(solution)/shard_map/reduce_scatter | solution.py:667
  237.8 23.5 %collective-permute-start.50 = (bf16[256,1536]{1,0:T(8,128)(2,1)S(1)}, bf16[256,1536]{1,0:T(8,128)(2,1)S(1)}, u32[]{:S(2)}, u32[]{:S(2)}) collective-permute-start(bf16[256,1536]{1,0:T(8,128)(2,1)S(1)} %pad_maximum_fusion.5.b_ref.refs_6_), channel_id=1, source_target_pairs={{0,16},{16,0},{1,17},{17,1},{2,18},{18,2},{3,19},{19,3},{4,20},{20... | collective-permute-start | bytes 2359304 | tf_op jit(solution)/shard_map/ppermute | solution.py:23
  272.7 100.8 %reduce-scatter.7.cloned.1.call-start = ((), (), s32[]{:S(2)}) async-start(), calls=%async_computation.7 | async-start | bytes 2949120 | tf_op jit(solution)/shard_map/reduce_scatter | solution.py:667
  303.6 23.4 %collective-permute-start.64 = (bf16[256,1536]{1,0:T(8,128)(2,1)S(1)}, bf16[256,1536]{1,0:T(8,128)(2,1)}, u32[]{:S(2)}, u32[]{:S(2)}) collective-permute-start(bf16[256,1536]{1,0:T(8,128)(2,1)S(1)} %copy-done.40), channel_id=1, source_target_pairs={{0,16},{16,0},{1,17},{17,1},{2,18},{18,2},{3,19},{19,3},{4,20},{20... | collective-permute-start | bytes 2359304 | tf_op jit(solution)/shard_map/ppermute | solution.py:23
  336.7 88.0 %reduce-scatter.9.cloned.1.call-start = ((), (), s32[]{:S(2)}) async-start(), calls=%async_computation.8 | async-start | bytes 5898240 | tf_op jit(solution)/shard_map/reduce_scatter | solution.py:667
  342.4 19.5 %collective-permute-start.72 = (bf16[256,1536]{1,0:T(8,128)(2,1)S(1)}, bf16[256,1536]{1,0:T(8,128)(2,1)S(1)}, u32[]{:S(2)}, u32[]{:S(2)}) collective-permute-start(bf16[256,1536]{1,0:T(8,128)(2,1)S(1)} %copy-done.43), channel_id=1, source_target_pairs={{0,16},{16,0},{1,17},{17,1},{2,18},{18,2},{3,19},{19,3},{4,20},{20... | collective-permute-start | bytes 2359304 | tf_op jit(solution)/shard_map/ppermute | solution.py:23
  342.5 21.5 %collective-permute-start.74 = (bf16[256,1536]{1,0:T(8,128)(2,1)S(1)}, bf16[256,1536]{1,0:T(8,128)(2,1)S(1)}, u32[]{:S(2)}, u32[]{:S(2)}) collective-permute-start(bf16[256,1536]{1,0:T(8,128)(2,1)S(1)} %copy-done.44), channel_id=1, source_target_pairs={{0,16},{16,0},{1,17},{17,1},{2,18},{18,2},{3,19},{19,3},{4,20},{20... | collective-permute-start | bytes 2359304 | tf_op jit(solution)/shard_map/ppermute | solution.py:23
  373.4 92.0 %reduce-scatter.11.cloned.1.call-start = ((), (), s32[]{:S(2)}) async-start(), calls=%async_computation.9 | async-start | bytes 2949120 | tf_op jit(solution)/shard_map/reduce_scatter | solution.py:667
  403.2 23.4 %collective-permute-start.28 = (bf16[256,1536]{1,0:T(8,128)(2,1)S(1)}, bf16[256,1536]{1,0:T(8,128)(2,1)}, u32[]{:S(2)}, u32[]{:S(2)}) collective-permute-start(bf16[256,1536]{1,0:T(8,128)(2,1)S(1)} %copy-done.39), channel_id=1, source_target_pairs={{0,16},{16,0},{1,17},{17,1},{2,18},{18,2},{3,19},{19,3},{4,20},{20... | collective-permute-start | bytes 2359304 | tf_op jit(solution)/shard_map/ppermute | solution.py:23
  461.8 28.2 %collective-permute-start.93 = (bf16[96,1536]{1,0:T(8,128)(2,1)}, bf16[96,1536]{1,0:T(8,128)(2,1)S(1)}, u32[]{:S(2)}, u32[]{:S(2)}) collective-permute-start(bf16[96,1536]{1,0:T(8,128)(2,1)} %get-tuple-element.384), channel_id=1, source_target_pairs={{0,32},{32,0},{1,33},{33,1},{2,34},{34,2},{3,35},{35,3},{4,36},{36... | collective-permute-start | bytes 884744 | tf_op jit(solution)/shard_map/ppermute | solution.py:23
  464.7 25.3 %collective-permute-start.94 = (bf16[96,1536]{1,0:T(8,128)(2,1)}, bf16[96,1536]{1,0:T(8,128)(2,1)S(1)}, u32[]{:S(2)}, u32[]{:S(2)}) collective-permute-start(bf16[96,1536]{1,0:T(8,128)(2,1)} %get-tuple-element.383), channel_id=1, source_target_pairs={{0,64},{64,0},{1,65},{65,1},{2,66},{66,2},{3,67},{67,3},{4,68},{68... | collective-permute-start | bytes 884744 | tf_op jit(solution)/shard_map/ppermute | solution.py:23
  472.9 25.9 %all-to-all-start.1 = ((bf16[16,24,1152]{2,1,0:T(8,128)(2,1)}), bf16[16,24,1152]{2,1,0:T(8,128)(2,1)S(1)}, u32[]{:S(2)}, u32[]{:S(2)}) async-start(bf16[16,24,1152]{2,1,0:T(8,128)(2,1)} %bitcast.62), calls=%async_computation.5 | async-start | bytes 1769472 | tf_op jit(solution)/shard_map/all_to_all | solution.py:741
  480.6 18.1 %collective-permute-start.95 = (bf16[96,1536]{1,0:T(8,128)(2,1)S(1)}, bf16[96,1536]{1,0:T(8,128)(2,1)}, u32[]{:S(2)}, u32[]{:S(2)}) collective-permute-start(bf16[96,1536]{1,0:T(8,128)(2,1)S(1)} %get-tuple-element.382), channel_id=1, source_target_pairs={{0,96},{32,64},{64,32},{96,0},{1,97},{33,65},{65,33},{97,1},{2,98}... | collective-permute-start | bytes 884744 | tf_op jit(solution)/shard_map/ppermute | solution.py:681
  484.7 29.5 %collective-permute-start.98 = (bf16[2,64,1536]{2,1,0:T(8,128)(2,1)}, bf16[2,64,1536]{2,1,0:T(8,128)(2,1)}, u32[]{:S(2)}, u32[]{:S(2)}) collective-permute-start(bf16[2,64,1536]{2,1,0:T(8,128)(2,1)} %pad_maximum_fusion.13), channel_id=1, source_target_pairs={{0,64},{8,80},{16,68},{24,84},{64,72},{72,88},{80,76},{88,92},{1,6... | collective-permute-start | bytes 1179656 | tf_op jit(solution)/shard_map/ppermute | solution.py:81
  487.9 26.4 %collective-permute-start.99 = (bf16[2,64,1536]{2,1,0:T(8,128)(2,1)}, bf16[2,64,1536]{2,1,0:T(8,128)(2,1)}, u32[]{:S(2)}, u32[]{:S(2)}) collective-permute-start(bf16[2,64,1536]{2,1,0:T(8,128)(2,1)} %pad_maximum_fusion.13), channel_id=1, source_target_pairs={{4,64},{12,80},{20,68},{28,84},{68,72},{76,88},{84,76},{92,92},{5,... | collective-permute-start | bytes 1179656 | tf_op jit(solution)/shard_map/ppermute | solution.py:81
  (186 other events, 1398.0 us)
Sparse Core Ops, SparseCore 0:
  48.2 34.7 all-gather.8
  84.7 52.6 all-gather.10
  139.7 33.4 all-gather.12
  174.6 52.6 all-gather.14
  272.8 51.2 reduce-scatter.4
  336.8 31.0 reduce-scatter.6
  373.5 51.1 reduce-scatter.8
  432.6 31.5 reduce-scatter.10
